TPU v7x, 32 devices: a whole 2x2x4 slice. The times are simulated.
32 devices in a mesh: groups: 2 (over x), blk: 8 (over z, y), sub: 2 (over core).
Axes of the slice: x: 2, y: 2, z: 4, core: 2. Of those that a mesh axis runs over, the one named last changes fastest.
Arguments:
- queries: bfloat16 [128, 32, 128], P(('groups', 'blk', 'sub')), parts along dimension 0, may hold values from -0.59765625 to 0.59765625
- candidates: int32 [128, 128], P(('groups', 'blk', 'sub')), parts along dimension 0, may hold values from 0 to 255, all different within a row; in each aligned block of 64 rows (0 to 63, 64 to 127, ...) at most 48 rows name the same one
- location: int32 [256], replicated, may hold values from 0 to 255, each once
- lengths: int32 [256], P(('blk', 'sub')), may hold values from 32 to 128
- centroid_ids: int32 [32768], P(('blk', 'sub')), may hold values from 0 to 262143, as said below
- residual_codes: int32 [32768, 128], P(('blk', 'sub')), may hold values from 0 to 3
- centroids: bfloat16 [262144, 128], P('blk'), may hold values from -0.5 to 0.5
- buckets: float32 [4, 128], replicated, may hold values from -0.4 to 0.4
Outputs:
- maxsim_scores: float32 [128, 128], P(('groups', 'blk', 'sub')), parts along dimension 0
There are 2 independent parts, one for each index of `groups`. A program takes and returns all parts, laid end to end along the dimension named above; an argument that names none is the same for every part. Nothing has to cross between parts.
Inputs may be any that keep to these rules, and one draw needn't show every extreme that they name: `candidates`: each query names 128 distinct passages; no passage is named by more than 48 queries, a bound that some block reaches. `location`: a permutation; slots s * 16 to (s + 1) * 16 - 1 are those of the s-th device along blk+sub. `centroid_ids`: among the 2048 token rows of one device, at most 512 have centroids in any one block of 32768 consecutive ids, and exactly 512 in some block, on every device.
All inputs are finite; a program needn't handle non-finite values.
Results may differ from a plain program's by a relative error of at most 0.0003.
Values may be sent and summed in bfloat16 or wider, within the bound.
No kernel may reach another device: no remote copies, remote signals or barrier semaphores. Data moves between devices by JAX's collectives and lax.ppermute only.
A program may use at most 64 MiB of HBM per device.

v0:
```python
import jax
import jax.numpy as jnp
from jax import lax
from jax.sharding import PartitionSpec as P


def residual_part(residual_codes, buckets):
    return jnp.where(
        residual_codes == 0,
        buckets[0],
        jnp.where(
            residual_codes == 1, buckets[1], jnp.where(residual_codes == 2, buckets[2], buckets[3])
        ),
    )


def body(queries, candidates, location, lengths, centroid_ids, residual_codes, centroids, buckets):
    token_count = centroid_ids.shape[0]
    passage_count = lengths.shape[0]
    tile_height = token_count // passage_count
    feature_width = residual_codes.shape[1]
    shard_rows = centroids.shape[0]
    shard_total = lax.axis_size("blk")
    owner_shard = centroid_ids // shard_rows
    offset = centroid_ids - owner_shard * shard_rows
    onehot = (owner_shard[:, None] == jnp.arange(shard_total, dtype=jnp.int32)[None, :]).astype(
        jnp.int32
    )
    before = jnp.cumsum(onehot, axis=0) - onehot
    token_rank = jnp.sum(before * onehot, axis=1)
    capacity = 2 * token_count // shard_total
    requests = jnp.zeros((shard_total, capacity), jnp.int32).at[owner_shard, token_rank].set(offset)
    found_rows = jnp.take(
        centroids, lax.all_to_all(requests, "blk", split_axis=0, concat_axis=0, tiled=True), axis=0
    )
    replies = lax.all_to_all(found_rows, "blk", split_axis=0, concat_axis=0, tiled=True)
    centroid_rows = replies[owner_shard, token_rank]
    embedded = (centroid_rows.astype(jnp.float32) + residual_part(residual_codes, buckets)).astype(
        jnp.bfloat16
    )
    embedded = embedded.reshape(passage_count, tile_height, feature_width)
    all_queries, all_lists = (
        lax.all_gather(queries, ("blk", "sub"), axis=0, tiled=True),
        lax.all_gather(candidates, ("blk", "sub"), axis=0, tiled=True),
    )
    query_count = all_queries.shape[0]
    listed = all_lists.shape[1]
    own_rank = lax.axis_index(("blk", "sub"))
    slots = jnp.take(location, all_lists, axis=0)
    local_slot = slots - own_rank * passage_count
    owned = (local_slot >= 0) & (local_slot < passage_count)
    target = jnp.where(owned, local_slot, passage_count)
    query_index = jnp.broadcast_to(
        jnp.arange(query_count, dtype=jnp.int32)[:, None], (query_count, listed)
    )
    list_index = jnp.broadcast_to(
        jnp.arange(listed, dtype=jnp.int32)[None, :], (query_count, listed)
    )
    chosen = (
        jnp.zeros((passage_count, query_count), jnp.int32)
        .at[target, query_index]
        .set(1, mode="drop")
    )
    list_of = (
        jnp.zeros((passage_count, query_count), jnp.int32)
        .at[target, query_index]
        .set(list_index, mode="drop")
    )
    query_rank = jnp.cumsum(chosen, axis=1) - chosen
    query_slots = 3 * query_count * listed // (2 * location.shape[0])
    passage_row = jnp.broadcast_to(
        jnp.arange(passage_count, dtype=jnp.int32)[:, None], (passage_count, query_count)
    )
    placed = jnp.where(chosen == 1, query_rank, query_slots)
    query_ids = jnp.broadcast_to(
        jnp.arange(query_count, dtype=jnp.int32)[None, :], (passage_count, query_count)
    )
    slot_query = (
        jnp.zeros((passage_count, query_slots), jnp.int32)
        .at[passage_row, placed]
        .set(query_ids, mode="drop")
    )
    slot_list = (
        jnp.full((passage_count, query_slots), listed, jnp.int32)
        .at[passage_row, placed]
        .set(list_of, mode="drop")
    )
    positions = jnp.arange(tile_height, dtype=jnp.int32)

    def one_passage(inputs):
        tile_rows, length, query_picks = inputs
        picked = jnp.take(all_queries, query_picks, axis=0)
        scores = jnp.einsum("rtd,jd->rtj", picked, tile_rows, preferred_element_type=jnp.float32)
        scores = jnp.where((positions < length)[None, None, :], scores, -1e30)
        return jnp.sum(jnp.max(scores, axis=2), axis=1)

    results = lax.map(one_passage, (embedded, lengths, slot_query))
    dense_scores = (
        jnp.zeros((query_count, listed), jnp.float32)
        .at[slot_query, slot_list]
        .set(results, mode="drop")
    )
    return lax.psum_scatter(dense_scores, ("blk", "sub"), scatter_dimension=0, tiled=True)


def solution(mesh):
    in_specs = (
        P(("groups", "blk", "sub"), None, None),
        P(("groups", "blk", "sub"), None),
        P(),
        P(("blk", "sub")),
        P(("blk", "sub")),
        P(("blk", "sub"), None),
        P("blk", None),
        P(),
    )
    out_specs = P(("groups", "blk", "sub"), None)
    return jax.shard_map(body, mesh=mesh, in_specs=in_specs, out_specs=out_specs, check_vma=False)
```

profile of v0, /device:TPU:0, one launch (start us, length us, event | category | flops | bytes accessed | tf_op | source)
XLA Modules:
  0.0 361.6 jit_solution(17276529961501579422)
XLA Ops:
  0.0 0.7 multiply_subtract_fusion
  0.7 2.3 reduce-window.6
  3.7 0.7 multiply_reduce_fusion.1
  4.4 0.8 and_reduce_fusion.1
  5.2 8.6 %scatter_custom_fusion.5 = s32[4096]{0:T(1024)} fusion(s32[2048]{0:T(1024)S(1)} %broadcast_select_fusion.2, s32[2048]{0:T(1024)S(1)} %get-tuple-element.71, s32[]{:T(128)} %constant.65.clone.1), kind=kCustom, calls=%fused_computation.79 | custom fusion | bytes 16388
  13.8 7.3 %all-to-all-start = ((s32[8,1,512]{2,1,0:T(1,128)}), s32[8,1,512]{2,1,0:T(1,128)S(1)}, u32[]{:S(2)}, u32[]{:S(2)}) async-start(s32[8,1,512]{2,1,0:T(1,128)} %bitcast.14), calls=%async_computation | async-start | bytes 32768 | tf_op jit(solution)/shard_map/all_to_all | solution.py:34
  21.1 22.1 %all-gather = s32[16,4,128]{2,1,0:T(4,128)S(1)} all-gather(s32[1,4,128]{2,1,0:T(4,128)} %bitcast.107), channel_id=1, replica_groups=mesh['groups'=2,'blk'=8,'sub'=2] {'blk','sub'}, dimensions={0}, use_global_device_ids=true | all-gather | bytes 34816 | tf_op jit(solution)/shard_map/all_gather | solution.py:44
  43.2 51.2 %gather_fusion.1 = s32[8192]{0:T(1024)S(1)} fusion(s32[256]{0:T(256)S(1)} %copy-done, s32[8192]{0:T(1024)S(1)} %bitcast_clamp_fusion), kind=kCustom, calls=%fused_computation.1 | custom fusion | bytes 98304 | tf_op jit(solution)/shard_map/jit(_take)/gather | solution.py:49
  94.6 15.6 %gather_fusion.2 = bf16[4096,128]{1,0:T(8,128)(2,1)S(1)} fusion(bf16[32768,128]{1,0:T(8,128)(2,1)} %param.16, s32[4096]{0:T(1024)S(1)} %broadcast_clamp_fusion), kind=kCustom, calls=%fused_computation.2 | custom fusion | bytes 2113536 | tf_op jit(solution)/shard_map/jit(_take)/gather | solution.py:33
  110.2 1.5 broadcast_select_fusion
  111.8 3.6 all-to-all-start.1
  115.6 30.4 %scatter_custom_fusion.1 = s32[1024]{0:T(1024)S(1)} fusion(s32[8192]{0:T(1024)S(1)} %get-tuple-element.79, s32[8192]{0:T(1024)S(1)} %broadcast.247, s32[]{:T(128)} %constant.65.clone.1), kind=kCustom, calls=%fused_computation.91 | custom fusion | bytes 4100
  146.7 4.3 %scatter_custom_fusion.2 = s32[768]{0:T(1024)S(1)} fusion(s32[1024]{0:T(1024)S(1)} %reshape.208, s32[1024]{0:T(1024)S(1)} %reshape.210, s32[]{:T(128)} %constant.65.clone.1), kind=kCustom, calls=%fused_computation.93 | custom fusion | bytes 3076
  151.1 30.4 %scatter_custom_fusion.3 = s32[1024]{0:T(1024)S(1)} fusion(s32[8192]{0:T(1024)S(1)} %get-tuple-element.79, s32[8192]{0:T(1024)S(1)} %get-tuple-element.80, s32[]{:T(128)} %constant.65.clone.1), kind=kCustom, calls=%fused_computation.89 | custom fusion | bytes 4100 | tf_op jit(solution)/shard_map/scatter | solution.py:67
  181.5 4.3 %scatter_custom_fusion.4 = s32[768]{0:T(1024)S(1)} fusion(s32[1024]{0:T(1024)S(1)} %reshape.208, s32[1024]{0:T(1024)S(1)} %scatter_custom_fusion.3, s32[]{:T(128)} %constant.119.clone.1), kind=kCustom, calls=%fused_computation.87 | custom fusion | bytes 3076
  186.0 0.7 dynamic-slice
  187.4 23.3 %all_gather.7 = bf16[64,32,128]{2,1,0:T(8,128)(2,1)S(1)} all-gather(bf16[4,32,128]{2,1,0:T(8,128)(2,1)S(1)} %copy-done.2), channel_id=1, replica_groups=mesh['groups'=2,'blk'=8,'sub'=2] {'blk','sub'}, dimensions={0}, use_global_device_ids=true | all-gather | bytes 557056 | tf_op jit(solution)/shard_map/all_gather | solution.py:43
  210.7 11.1 %gather_fusion.3 = bf16[2048,128]{1,0:T(8,128)(2,1)S(1)} fusion(bf16[8,512,128]{2,1,0:T(8,128)(2,1)S(1)} %all-to-all-done.1, s32[2048]{0:T(1024)S(1)} %bitcast.95), kind=kCustom, calls=%fused_computation.3 | custom fusion | bytes 1064960 | tf_op jit(solution)/shard_map/gather | solution.py:37
  222.1 43.5 %while.11 = (s32[]{:T(128)}, f32[16,48]{1,0:T(8,128)S(1)}, s32[16]{0:T(128)S(1)}, s32[16,48]{1,0:T(8,128)S(1)}, bf16[64,32,128]{2,1,0:T(8,128)(2,1)S(1)}, /*inde...) while((s32[]{:T(128)}, f32[16,48]{1,0:T(8,128)S(1)}, s32[16]{0:T(128)S(1)}, ...), condition=%wide.region_12.13_spmd.clone, body=%wide.region_9.12_spmd.clone.sunk | while | flops 50923008 | bytes 1231665 | solution.py:97
  222.2 0.6 gather_fusion
  222.8 0.7 dynamic_slice.31
  223.5 0.7 iota_compare_fusion.4
  224.9 0.6 gather_fusion
  225.6 0.7 dynamic_slice.31
  226.2 0.7 iota_compare_fusion.4
  227.6 0.6 gather_fusion
  228.3 0.7 dynamic_slice.31
  229.0 0.7 iota_compare_fusion.4
  230.3 0.6 gather_fusion
  231.0 0.7 dynamic_slice.31
  231.7 0.7 iota_compare_fusion.4
  233.1 0.6 gather_fusion
  233.7 0.7 dynamic_slice.31
  234.4 0.7 iota_compare_fusion.4
  235.8 0.6 gather_fusion
  236.4 0.7 dynamic_slice.31
  237.1 0.7 iota_compare_fusion.4
  238.5 0.6 gather_fusion
  239.2 0.7 dynamic_slice.31
  239.8 0.7 iota_compare_fusion.4
  241.2 0.6 gather_fusion
  241.9 0.7 dynamic_slice.31
  242.5 0.7 iota_compare_fusion.4
  243.9 0.6 gather_fusion
  244.6 0.7 dynamic_slice.31
  245.3 0.7 iota_compare_fusion.4
  246.7 0.6 gather_fusion
  247.3 0.7 dynamic_slice.31
  248.0 0.7 iota_compare_fusion.4
  249.4 0.6 gather_fusion
  250.0 0.7 dynamic_slice.31
  250.7 0.7 iota_compare_fusion.4
  252.8 0.7 dynamic_slice.31
  253.4 0.7 iota_compare_fusion.4
  255.5 0.7 dynamic_slice.31
  256.2 0.7 iota_compare_fusion.4
  258.2 0.7 dynamic_slice.31
  258.9 0.7 iota_compare_fusion.4
  260.9 0.7 dynamic_slice.31
  261.6 0.7 iota_compare_fusion.4
  263.6 0.7 dynamic_slice.31
  264.3 0.7 iota_compare_fusion.4
  265.8 37.4 %scatter_fusion = f32[64,128]{1,0:T(8,128)S(1)} fusion(f32[64,128]{1,0:T(8,128)S(1)} %broadcast_in_dim.128, s32[768]{0:T(1024)S(1)} %reshape.196, f32[768]{0:T(1024)S(1)} %reshape.198), kind=kCustom, calls=%fused_computation.4 | custom fusion | bytes 15360 | tf_op jit(solution)/shard_map/scatter | solution.py:101
  303.2 57.8 %all-reduce = f32[64,128]{1,0:T(8,128)S(1)} all-reduce(f32[64,128]{1,0:T(8,128)S(1)} %scatter_fusion), channel_id=2, replica_groups=mesh['groups'=2,'blk'=8,'sub'=2] {'blk','sub'}, use_global_device_ids=true, to_apply=%region_14.15.clone | all-reduce | flops 8192 | bytes 65536
  (160 shorter events, 16.7 us)
Async XLA Ops:
  0.0 43.2 %copy-start = (s32[256]{0:T(256)S(1)}, s32[256]{0:T(256)}, u32[]{:S(2)}) copy-start(s32[256]{0:T(256)} %param.12) | copy-start | bytes 3076
  13.8 80.7 %all-to-all-start = ((s32[8,1,512]{2,1,0:T(1,128)}), s32[8,1,512]{2,1,0:T(1,128)S(1)}, u32[]{:S(2)}, u32[]{:S(2)}) async-start(s32[8,1,512]{2,1,0:T(1,128)} %bitcast.14), calls=%async_computation | async-start | bytes 32768 | tf_op jit(solution)/shard_map/all_to_all | solution.py:34
  94.4 21.0 %copy-start.5 = (s32[2]{0:T(128)S(1)}, s32[2]{0:T(128)}, u32[]{:S(2)}) copy-start(s32[2]{0:T(128)} %constant.129) | copy-start | bytes 28
  94.5 21.0 %copy-start.4 = (s32[2]{0:T(128)S(1)}, s32[2]{0:T(128)}, u32[]{:S(2)}) copy-start(s32[2]{0:T(128)} %constant.132) | copy-start | bytes 28
  94.5 51.9 %copy-start.7 = (s32[2]{0:T(128)S(1)}, s32[2]{0:T(128)}, u32[]{:S(2)}) copy-start(s32[2]{0:T(128)} %constant.135) | copy-start | bytes 28
  94.5 52.0 %copy-start.6 = (s32[2]{0:T(128)S(1)}, s32[2]{0:T(128)}, u32[]{:S(2)}) copy-start(s32[2]{0:T(128)} %constant.138) | copy-start | bytes 28
  94.5 91.5 %copy-start.9 = (u32[32]{0:T(128)S(1)}, u32[32]{0:T(128)}, u32[]{:S(2)}) copy-start(u32[32]{0:T(128)} %constant.196) | copy-start | bytes 388
  94.5 92.9 %copy-start.3 = (f32[4,128]{1,0:T(4,128)S(1)}, f32[4,128]{1,0:T(4,128)}, u32[]{:S(2)}) copy-start(f32[4,128]{1,0:T(4,128)} %param.17) | copy-start | bytes 6148
  94.5 92.9 %copy-start.2 = (bf16[4,32,128]{2,1,0:T(8,128)(2,1)S(1)}, bf16[4,32,128]{2,1,0:T(8,128)(2,1)}, u32[]{:S(2)}) copy-start(bf16[4,32,128]{2,1,0:T(8,128)(2,1)} %param.10) | copy-start | bytes 98308
  94.6 127.2 %copy-start.1 = (s32[2048,128]{1,0:T(8,128)S(1)}, s32[2048,128]{1,0:T(8,128)}, u32[]{:S(2)}) copy-start(s32[2048,128]{1,0:T(8,128)} %param.15) | copy-start | bytes 3145732
  110.2 111.9 %copy-start.8 = (s32[16]{0:T(128)S(1)}, s32[16]{0:T(128)}, u32[]{:S(2)}) copy-start(s32[16]{0:T(128)} %param.13) | copy-start | bytes 196
  111.8 98.9 %all-to-all-start.1 = ((bf16[8,512,128]{2,1,0:T(8,128)(2,1)}), bf16[8,512,128]{2,1,0:T(8,128)(2,1)S(1)}, u32[]{:S(2)}, u32[]{:S(2)}) async-start(bf16[8,512,128]{2,1,0:T(8,128)(2,1)} %broadcast_select_fusion), calls=%async_computation.1 | async-start | bytes 2097152 | tf_op jit(solution)/shard_map/all_to_all | solution.py:36
where the time goes:
time: 362 us
  local copies, waits for them, and re-layouts  217 us (60%)
  blocking collectives  103 us (28%)
  other arithmetic  20.7 us (6%)
  starting transfers between devices  10.8 us (3%)
  matrix products  7.88 us (2%)
    unnamed x1, blocking collectives  57.8 us
    gather x1, local copies, waits for them, and re-layouts, body(): slots = jnp.take(location, all_lists, axis=0)  51.2 us
    unnamed x28, local copies, waits for them, and re-layouts  49.1 us
    scatter x1, local copies, waits for them, and re-layouts, body(): dense_scores = jnp.zeros((query_count, listed), jnp.float32).at[slot_quer...  37.4 us
    scatter x1, local copies, waits for them, and re-layouts, body(): list_of = jnp.zeros((passage_count, query_count), jnp.int32).at[target, q...  30.4 us
    all_gather x1, blocking collectives, body(): lax.all_gather(queries, ('blk', 'sub'), axis=0, tiled=True)  23.3 us
    all_gather x1, blocking collectives, body(): lax.all_gather(candidates, ('blk', 'sub'), axis=0, tiled=True)  22.1 us
    gather x1, local copies, waits for them, and re-layouts, body(): jnp.take(centroids, lax.all_to_all(requests, 'blk', split_axis=0, concat_...  15.6 us
  transfers between devices with their start and end apart: 2, of which 0 were waited for; matrix products, arithmetic and copies ran while one was open for 34% of the time, Pallas kernels for 0%

commit v1 on v0

v1 whole, which is shorter than its diff:
```python
import functools

import jax
import jax.numpy as jnp
from jax import lax
from jax.experimental import pallas as pl
from jax.experimental.pallas import tpu as pltpu
from jax.sharding import PartitionSpec as P

F32 = jnp.float32
BF16 = jnp.bfloat16
I32 = jnp.int32
MIB = 1 << 20


def dot_nt(a, b):
    return lax.dot_general(a, b, (((1,), (1,)), ((), ())), preferred_element_type=F32)


def dot_nn(a, b):
    return lax.dot_general(a, b, (((1,), (0,)), ((), ())), preferred_element_type=F32)


def plan_kernel(shards, shard_rows, cap, lengths_ref, ids_ref, requests_ref, pos_ref):
    passages, height = ids_ref.shape
    ids = ids_ref[...]
    owner = ids // shard_rows
    offset = ids - owner * shard_rows
    row = lax.broadcasted_iota(I32, (passages, height), 0)
    lane = lax.broadcasted_iota(I32, (passages, height), 1)
    limit = jnp.zeros((passages, height), I32)
    for p in range(passages):
        limit = jnp.where(row == p, lengths_ref[p], limit)
    owner = jnp.where(lane < limit, owner, shards)
    mask = jnp.concatenate([jnp.where(owner == b, 1.0, 0.0) for b in range(shards)], axis=0)
    mask16 = mask.astype(BF16)
    k = lax.broadcasted_iota(I32, (height, height), 0)
    l = lax.broadcasted_iota(I32, (height, height), 1)
    inside = dot_nn(mask16, jnp.where(k < l, 1.0, 0.0).astype(BF16))
    totals = dot_nn(mask16, jnp.ones((height, height), BF16))
    full = shards * passages
    r = lax.broadcasted_iota(I32, (full, full), 0)
    c = lax.broadcasted_iota(I32, (full, full), 1)
    same = r // passages == c // passages
    totals16 = totals.astype(BF16)
    ahead = dot_nn(jnp.where(same & (c < r), 1.0, 0.0).astype(BF16), totals16)
    place = (inside + ahead) * mask
    rank = jnp.zeros((passages, height), F32)
    counts = []
    for b in range(shards):
        rank = rank + place[b * passages : (b + 1) * passages]
        counts.append(jnp.sum(totals[b * passages : (b + 1) * passages], axis=0, keepdims=True))
    pos = owner * cap + rank.astype(I32)
    pos_ref[...] = jnp.where(lane < limit, pos, 0)
    pos_row = pos // height
    pos_lane = pos - pos_row * height
    high = (offset // 256).astype(F32)
    low = (offset % 256).astype(F32)
    rows = shards * cap // height
    out_row = lax.broadcasted_iota(I32, (rows, height), 0)
    out_lane = lax.broadcasted_iota(I32, (height, height), 0)
    total = jnp.zeros((rows, 2 * height), F32)
    for p in range(passages):
        here = jnp.where(out_row == pos_row[p : p + 1], 1.0, 0.0).astype(BF16)
        hit = out_lane == pos_lane[p : p + 1]
        values = jnp.concatenate(
            [jnp.where(hit, high[p : p + 1], 0.0), jnp.where(hit, low[p : p + 1], 0.0)], axis=0
        ).astype(BF16)
        total = total + dot_nt(here, values)
    found = (total[:, :height] * 256.0 + total[:, height:]).astype(I32)
    per = rows // shards
    for b in range(shards):
        requests_ref[b * per : (b + 1) * per] = (
            found[b * per : (b + 1) * per] + counts[b].astype(I32) * shard_rows
        )


def plan(lengths, ids, shards, shard_rows, cap):
    passages, height = ids.shape
    return pl.pallas_call(
        functools.partial(plan_kernel, shards, shard_rows, cap),
        out_shape=(
            jax.ShapeDtypeStruct((shards * cap // height, height), I32),
            jax.ShapeDtypeStruct((passages, height), I32),
        ),
        in_specs=[
            pl.BlockSpec(memory_space=pltpu.SMEM),
            pl.BlockSpec(memory_space=pltpu.VMEM),
        ],
        out_specs=(
            pl.BlockSpec(memory_space=pltpu.VMEM),
            pl.BlockSpec(memory_space=pltpu.VMEM),
        ),
        compiler_params=pltpu.CompilerParams(vmem_limit_bytes=16 * MIB),
    )(lengths, ids)


def widen_kernel(chunk, source_ref, wide_ref, buffers, sems):
    steps = source_ref.shape[0] // chunk

    def copy(step, slot):
        return pltpu.make_async_copy(
            source_ref.at[pl.ds(step * chunk, chunk)], buffers.at[slot], sems.at[slot]
        )

    copy(0, 0).start()
    for step in range(steps):
        if step + 1 < steps:
            copy(step + 1, (step + 1) % 2).start()
        copy(step, step % 2).wait()

        @pl.loop(0, chunk // 256)
        def _(i):
            at = pl.multiple_of(i * 256, 256)
            wide_ref[pl.ds(step * chunk + at, 256)] = buffers[step % 2, pl.ds(at, 256)].astype(F32)


def widen(centroids):
    rows, width = centroids.shape
    chunk = min(rows, 4096)
    return pl.pallas_call(
        functools.partial(widen_kernel, chunk),
        out_shape=jax.ShapeDtypeStruct((rows, width), F32),
        in_specs=[pl.BlockSpec(memory_space=pl.ANY)],
        out_specs=pl.BlockSpec(memory_space=pltpu.VMEM),
        scratch_shapes=[pltpu.VMEM((2, chunk, width), BF16), pltpu.SemaphoreType.DMA((2,))],
        compiler_params=pltpu.CompilerParams(vmem_limit_bytes=40 * MIB),
    )(centroids)


UNROLL = 16


def fetch_kernel(shards, shard_rows, cap, asked_ref, table_ref, out_ref, wide):
    @pl.loop(0, shards)
    def _(d):
        base = d * cap
        count = asked_ref[base] // shard_rows

        @pl.loop(0, (count + UNROLL - 1) // UNROLL)
        def _(i):
            at = pl.multiple_of(base + i * UNROLL, UNROLL)
            for u in range(UNROLL):
                offset = lax.rem(asked_ref[at + u], shard_rows)
                wide[pl.ds(at + u, 1)] = table_ref[pl.ds(offset, 1)]

    @pl.loop(0, shards * cap // 256)
    def _(i):
        at = pl.multiple_of(i * 256, 256)
        out_ref[pl.ds(at, 256)] = wide[pl.ds(at, 256)].astype(BF16)


def fetch(asked, table, shards, shard_rows, cap):
    width = table.shape[1]
    return pl.pallas_call(
        functools.partial(fetch_kernel, shards, shard_rows, cap),
        out_shape=jax.ShapeDtypeStruct((shards * cap, width), BF16),
        in_specs=[
            pl.BlockSpec(memory_space=pltpu.SMEM),
            pl.BlockSpec(memory_space=pltpu.VMEM),
        ],
        out_specs=pl.BlockSpec(memory_space=pltpu.VMEM),
        scratch_shapes=[pltpu.VMEM((shards * cap, width), F32)],
        compiler_params=pltpu.CompilerParams(vmem_limit_bytes=40 * MIB),
    )(asked, table)


def score_kernel(
    span, lengths_ref, pos_ref, replies_ref, codes_ref, buckets_ref, queries_ref, out_ref, wide, tile
):
    passages, height = codes_ref.shape[0], codes_ref.shape[1]
    width = codes_ref.shape[2]
    owners = queries_ref.shape[0] // span
    chunk = 2 * span

    @pl.loop(0, replies_ref.shape[0] // 256)
    def _(i):
        at = pl.multiple_of(i * 256, 256)
        wide[pl.ds(at, 256)] = replies_ref[pl.ds(at, 256)].astype(F32)

    levels = [jnp.broadcast_to(buckets_ref[b : b + 1], (height, width)) for b in range(4)]
    line = lax.broadcasted_iota(I32, (height, width), 0)

    @pl.loop(0, passages)
    def _(p):
        length = lengths_ref[p]

        @pl.loop(0, (length + UNROLL - 1) // UNROLL)
        def _(i):
            at = pl.multiple_of(i * UNROLL, UNROLL)
            for u in range(UNROLL):
                tile[pl.ds(at + u, 1)] = wide[pl.ds(pos_ref[p * height + at + u], 1)]

        codes = codes_ref[p]
        residual = jnp.where(
            codes == 0,
            levels[0],
            jnp.where(codes == 1, levels[1], jnp.where(codes == 2, levels[2], levels[3])),
        )
        rows = tile[...] + residual
        rows = jnp.where(line < length, rows, rows[0:1])
        embedded = rows.astype(BF16)
        for c in range(owners // 2):
            scores = dot_nt(embedded, queries_ref[c * chunk : (c + 1) * chunk])
            best = jnp.max(scores, axis=0, keepdims=True)
            out_ref[2 * c, pl.ds(p, 1)] = best[:, :span]
            out_ref[2 * c + 1, pl.ds(p, 1)] = best[:, span:]


def score(lengths, pos, replies, codes, buckets, queries, span):
    passages, height, width = codes.shape
    owners = queries.shape[0] // span
    return pl.pallas_call(
        functools.partial(score_kernel, span),
        out_shape=jax.ShapeDtypeStruct((owners, passages, span), F32),
        in_specs=[
            pl.BlockSpec(memory_space=pltpu.SMEM),
            pl.BlockSpec(memory_space=pltpu.SMEM),
            pl.BlockSpec(memory_space=pltpu.VMEM),
            pl.BlockSpec(memory_space=pltpu.VMEM),
            pl.BlockSpec(memory_space=pltpu.VMEM),
            pl.BlockSpec(memory_space=pltpu.VMEM),
        ],
        out_specs=pl.BlockSpec(memory_space=pltpu.VMEM),
        scratch_shapes=[
            pltpu.VMEM((replies.shape[0], width), F32),
            pltpu.VMEM((height, width), F32),
        ],
        compiler_params=pltpu.CompilerParams(vmem_limit_bytes=40 * MIB),
    )(lengths, pos, replies, codes, buckets, queries)


def pick_kernel(tokens, location_ref, candidates_ref, best_ref, out_ref):
    owned, listed = candidates_ref.shape
    slots_total, span = best_ref.shape
    groups, width = location_ref.shape
    which = lax.broadcasted_iota(I32, (width, listed), 0)
    slot = lax.broadcasted_iota(I32, (slots_total, listed), 0)
    sums = best_ref[...]
    shift = tokens // 2
    while shift:
        sums = sums + pltpu.roll(sums, span - shift, 1)
        shift //= 2
    for q in range(owned):
        named = candidates_ref[q : q + 1]
        found = jnp.zeros((2, listed), F32)
        for g in range(groups):
            here = location_ref[g : g + 1]
            pair = jnp.concatenate([here // 256, here % 256], axis=0).astype(F32).astype(BF16)
            hit = jnp.where(which + g * width == named, 1.0, 0.0).astype(BF16)
            found = found + dot_nn(pair, hit)
        slots = (found[0:1] * 256.0 + found[1:2]).astype(I32)
        column = jnp.broadcast_to(sums[:, q * tokens : q * tokens + 1], (slots_total, listed))
        out_ref[q : q + 1] = jnp.sum(jnp.where(slot == slots, column, 0.0), axis=0, keepdims=True)


def pick(location, candidates, best, tokens):
    return pl.pallas_call(
        functools.partial(pick_kernel, tokens),
        out_shape=jax.ShapeDtypeStruct(candidates.shape, F32),
        compiler_params=pltpu.CompilerParams(vmem_limit_bytes=16 * MIB),
    )(location, candidates, best)


def body(queries, candidates, location, lengths, centroid_ids, residual_codes, centroids, buckets):
    token_count = centroid_ids.shape[0]
    passage_count = lengths.shape[0]
    height = token_count // passage_count
    width = residual_codes.shape[1]
    shard_rows = centroids.shape[0]
    shards = lax.axis_size("blk")
    owners = shards * lax.axis_size("sub")
    cap = 2 * token_count // shards
    owned, tokens = queries.shape[0], queries.shape[1]
    span = owned * tokens

    requests, pos = plan(
        lengths, centroid_ids.reshape(passage_count, height), shards, shard_rows, cap
    )
    asked = lax.all_to_all(
        requests.reshape(shards, cap), "blk", split_axis=0, concat_axis=0, tiled=True
    )
    table = widen(centroids)
    sent = jnp.broadcast_to(queries.reshape(1, span, width), (owners, span, width))
    all_queries = lax.all_to_all(sent, ("blk", "sub"), split_axis=0, concat_axis=0, tiled=True)
    found = fetch(asked.reshape(shards * cap), table, shards, shard_rows, cap)
    replies = lax.all_to_all(
        found.reshape(shards, cap, width), "blk", split_axis=0, concat_axis=0, tiled=True
    )
    best = score(
        lengths,
        pos.reshape(token_count),
        replies.reshape(shards * cap, width),
        residual_codes.reshape(passage_count, height, width),
        buckets,
        all_queries.reshape(owners * span, width),
        span,
    )
    mine = lax.all_to_all(best, ("blk", "sub"), split_axis=0, concat_axis=0, tiled=True)
    return pick(
        location.reshape(location.shape[0] // 128, 128),
        candidates,
        mine.reshape(owners * passage_count, span),
        tokens,
    )


def solution(mesh):
    in_specs = (
        P(("groups", "blk", "sub"), None, None),
        P(("groups", "blk", "sub"), None),
        P(),
        P(("blk", "sub")),
        P(("blk", "sub")),
        P(("blk", "sub"), None),
        P("blk", None),
        P(),
    )
    out_specs = P(("groups", "blk", "sub"), None)
    return jax.shard_map(body, mesh=mesh, in_specs=in_specs, out_specs=out_specs, check_vma=False)
```

time: 362 us -> 94.8 us (0.26)
  local copies, waits for them, and re-layouts: 217 us -> 6.41 us
  blocking collectives: 103 us -> 55.9 us
  Pallas kernels: 0 us -> 28.5 us
  other arithmetic: 20.7 us -> 0 us
  matrix products: 7.88 us -> 0 us
  starting transfers between devices: 10.8 us -> 3.57 us
    gather x19 -> x0, local copies, waits for them, and re-layouts: 87.9 us -> none  [the longest x1 51.2 us: body(): slots = jnp.take(location, all_lists, axis=0)]
    scatter x5 -> x0, local copies, waits for them, and re-layouts: 68.1 us -> none  [the longest x1 37.4 us: body(): dense_scores = jnp.zeros((query_count, listed), jnp.float32).at[slot_quer...]
    unnamed x1 -> x0, blocking collectives: 57.8 us -> none
    all_to_all x0 -> x3, blocking collectives: none -> 55.9 us  [the longest x1 30.6 us: body(): lax.all_to_all(found.reshape(shards, cap, width), 'blk', split_axis=0, co...]
    all_gather x2 -> x0, blocking collectives: 45.4 us -> none  [the longest x1 23.3 us: body(): lax.all_gather(queries, ('blk', 'sub'), axis=0, tiled=True)]
    unnamed x28 -> x16, local copies, waits for them, and re-layouts: 49.1 us -> 4.75 us
    pallas_call x0 -> x5, Pallas kernels: none -> 28.5 us  [the longest x1 10.7 us: fetch(): pl.pallas_call(functools.partial(fetch_kernel, shards, shard_rows, cap),...]
    lt x16 -> x0, other arithmetic: 11.1 us -> none  [one_passage(): scores = jnp.where((positions < length)[None, None, :], scores, -1e+30)]
  transfers between devices with their start and end apart: 2 -> 1, of which waited for: 0 -> 0; matrix products, arithmetic and copies ran while one was open for 34% -> 0% of each run, Pallas kernels for 0% -> 20%
where the time goes in v1:
time: 94.8 us; the launch traced here: 94.4 us
  blocking collectives  55.9 us (59%)
  Pallas kernels  28.5 us (30%)
  local copies, waits for them, and re-layouts  6.41 us (7%)
  starting transfers between devices  3.57 us (4%)
    all_to_all x1, blocking collectives, body(): lax.all_to_all(found.reshape(shards, cap, width), 'blk', split_axis=0, co...  30.6 us
    all_to_all x1, blocking collectives, body(): lax.all_to_all(requests.reshape(shards, cap), 'blk', split_axis=0, concat...  13.7 us
    all_to_all x1, blocking collectives, body(): lax.all_to_all(best, ('blk', 'sub'), split_axis=0, concat_axis=0, tiled=T...  11.6 us
    pallas_call x1, Pallas kernels, fetch(): pl.pallas_call(functools.partial(fetch_kernel, shards, shard_rows, cap),...  10.7 us
    pallas_call x1, Pallas kernels, widen(): pl.pallas_call(functools.partial(widen_kernel, chunk), out_shape=jax.Shap...  7.93 us
    pallas_call x1, Pallas kernels, score(): pl.pallas_call(functools.partial(score_kernel, span), out_shape=jax.Shape...  7.31 us
    unnamed x16, local copies, waits for them, and re-layouts  4.75 us
    all_to_all x1, starting transfers between devices, body(): lax.all_to_all(sent, ('blk', 'sub'), split_axis=0, concat_axis=0, tiled=T...  3.57 us
  transfers between devices with their start and end apart: 1, of which 0 were waited for; matrix products, arithmetic and copies ran while one was open for 0% of the time, Pallas kernels for 20%

profile of v1, /device:TPU:0, one launch (start us, length us, event | category | flops | bytes accessed | tf_op | source)
XLA Modules:
  0.0 94.4 jit_solution(2121533884977837169)
XLA Ops:
  0.0 0.0 copy-start.2
  0.0 0.7 copy-done.2
  0.7 0.0 copy-start.5
  0.7 0.7 copy-done.5
  1.4 1.3 %shard_map.82 = (s32[32,128]{1,0:T(8,128)S(1)}, s32[16,128]{1,0:T(8,128)S(1)}) custom-call(s32[16]{0:T(128)S(1)} %copy-done.5, s32[16,128]{1,0:T(8,128)S(1)} %bitcast.19), custom_call_target="tpu_custom_call" | custom-call | tf_op jit(solution)/shard_map/pallas_call | solution.py:80
  2.7 13.7 %all_to_all.24 = s32[8,1,512]{2,1,0:T(1,128)S(1)} all-to-all(s32[8,1,512]{2,1,0:T(1,128)S(1)} %bitcast.17), channel_id=1, replica_groups=mesh['groups'=2,'blk'=8,'sub'=2] {'blk'}, dimensions={0} | all-to-all | bytes 32768 | tf_op jit(solution)/shard_map/all_to_all | solution.py:280
  16.4 1.7 %broadcast_in_dim.8 = bf16[16,128,128]{2,1,0:T(8,128)(2,1)} broadcast(bf16[128,128]{1,0:T(8,128)(2,1)} %bitcast.21), dimensions={1,2} | broadcast | bytes 557056 | tf_op jit(solution)/shard_map/broadcast_in_dim | solution.py:284
  18.0 3.6 %all-to-all-start.2 = ((bf16[16,128,128]{2,1,0:T(8,128)(2,1)}), bf16[16,128,128]{2,1,0:T(8,128)(2,1)S(1)}, u32[]{:S(2)}, u32[]{:S(2)}) async-start(bf16[16,128,128]{2,1,0:T(8,128)(2,1)} %broadcast_in_dim.8), calls=%async_computation.2 | async-start | bytes 1048576 | tf_op jit(solution)/shard_map/all_to_all | solution.py:285
  21.6 0.0 copy-start
  21.6 3.4 %copy-done = bf16[32768,128]{1,0:T(8,128)(2,1)S(1)} copy-done((bf16[32768,128]{1,0:T(8,128)(2,1)S(1)}, bf16[32768,128]{1,0:T(8,128)(2,1)}, u32[]{:S(2)}) %copy-start) | copy-done | bytes 8388632
  25.0 0.0 copy-start.1
  25.0 0.0 copy-start.4
  25.0 0.0 copy-start.6
  25.0 7.9 %shard_map.83.table_ref = f32[32768,128]{1,0:T(8,128)} custom-call(bf16[32768,128]{1,0:T(8,128)(2,1)S(1)} %copy-done), custom_call_target="tpu_custom_call" | custom-call | tf_op jit(solution)/shard_map/pallas_call | solution.py:121
  32.9 0.0 copy-start.3
  32.9 0.0 copy-start.7
  33.0 10.7 %shard_map.84 = bf16[4096,128]{1,0:T(8,128)(2,1)S(1)} custom-call(s32[4096]{0:T(1024)S(1)} %bitcast.16, f32[32768,128]{1,0:T(8,128)} %shard_map.83.table_ref), custom_call_target="tpu_custom_call" | custom-call | tf_op jit(solution)/shard_map/pallas_call | solution.py:155
  43.7 0.0 all-to-all-done.2
  43.7 30.6 %all_to_all.25 = bf16[8,512,128]{2,1,0:T(8,128)(2,1)S(1)} all-to-all(bf16[8,512,128]{2,1,0:T(8,128)(2,1)S(1)} %bitcast.11), channel_id=1, replica_groups=mesh['groups'=2,'blk'=8,'sub'=2] {'blk'}, dimensions={0} | all-to-all | bytes 2097152 | tf_op jit(solution)/shard_map/all_to_all | solution.py:287
  74.3 0.0 copy-done.1
  74.3 0.0 copy-done.4
  74.3 0.0 copy-done.6
  74.3 7.3 %shard_map.85 = f32[16,16,128]{2,1,0:T(8,128)S(1)} custom-call(s32[16]{0:T(128)S(1)} %copy-done.6, s32[2048]{0:T(1024)S(1)} %bitcast.18, bf16[4096,128]{1,0:T(8,128)(2,1)S(1)} %bitcast.12, s32[16,128,128]{2,1,0:T(8,128)S(1)} %bitcast.14, f32[4,128]{1,0:T(4,128)S(1)} %copy-done.4, bf16[2048,128]{1,0:T(8,128)(2,1)S(1)} %bitcast.13), custom_call_target="tpu_custom_call" | custom-call | tf_op jit(solution)/shard_map/pallas_call | solution.py:213
  81.7 11.6 %all_to_all.26 = f32[16,16,128]{2,1,0:T(8,128)S(1)} all-to-all(f32[16,16,128]{2,1,0:T(8,128)S(1)} %shard_map.85), channel_id=1, replica_groups=mesh['groups'=2,'blk'=8,'sub'=2] {'blk','sub'}, dimensions={0} | all-to-all | bytes 262144 | tf_op jit(solution)/shard_map/all_to_all | solution.py:299
  93.3 0.0 copy-done.3
  93.3 0.0 copy-done.7
  93.3 1.1 %shard_map.86 = f32[4,128]{1,0:T(4,128)} custom-call(s32[2,128]{1,0:T(2,128)S(1)} %bitcast.20, s32[4,128]{1,0:T(4,128)S(1)} %copy-done.3, f32[256,128]{1,0:T(8,128)S(1)} %bitcast.15), custom_call_target="tpu_custom_call" | custom-call | tf_op jit(solution)/shard_map/pallas_call | solution.py:258
Async XLA Ops:
  0.0 0.7 copy-start.2
  0.7 0.7 copy-start.5
  18.0 25.7 %all-to-all-start.2 = ((bf16[16,128,128]{2,1,0:T(8,128)(2,1)}), bf16[16,128,128]{2,1,0:T(8,128)(2,1)S(1)}, u32[]{:S(2)}, u32[]{:S(2)}) async-start(bf16[16,128,128]{2,1,0:T(8,128)(2,1)} %broadcast_in_dim.8), calls=%async_computation.2 | async-start | bytes 1048576 | tf_op jit(solution)/shard_map/all_to_all | solution.py:285
  21.6 3.4 %copy-start = (bf16[32768,128]{1,0:T(8,128)(2,1)S(1)}, bf16[32768,128]{1,0:T(8,128)(2,1)}, u32[]{:S(2)}) copy-start(bf16[32768,128]{1,0:T(8,128)(2,1)} %source_ref.1) | copy-start | bytes 25165828
  25.0 49.3 %copy-start.1 = (s32[2048,128]{1,0:T(8,128)S(1)}, s32[2048,128]{1,0:T(8,128)}, u32[]{:S(2)}) copy-start(s32[2048,128]{1,0:T(8,128)} %param.13) | copy-start | bytes 3145732
  25.0 49.3 %copy-start.4 = (f32[4,128]{1,0:T(4,128)S(1)}, f32[4,128]{1,0:T(4,128)}, u32[]{:S(2)}) copy-start(f32[4,128]{1,0:T(4,128)} %buckets_ref.1) | copy-start | bytes 6148
  25.0 49.3 %copy-start.6 = (s32[16]{0:T(128)S(1)}, s32[16]{0:T(128)}, u32[]{:S(2)}) copy-start(s32[16]{0:T(128)} %lengths_ref.3) | copy-start | bytes 196
  32.9 60.4 %copy-start.3 = (s32[4,128]{1,0:T(4,128)S(1)}, s32[4,128]{1,0:T(4,128)}, u32[]{:S(2)}) copy-start(s32[4,128]{1,0:T(4,128)} %candidates_ref.1) | copy-start | bytes 6148
  32.9 60.4 %copy-start.7 = (s32[256]{0:T(256)S(1)}, s32[256]{0:T(256)}, u32[]{:S(2)}) copy-start(s32[256]{0:T(256)} %param.10) | copy-start | bytes 3076

commit v2 on v1

v2 whole, which is shorter than its diff:
```python
import functools

import jax
import jax.numpy as jnp
from jax import lax
from jax.experimental import pallas as pl
from jax.experimental.pallas import tpu as pltpu
from jax.sharding import PartitionSpec as P

F32 = jnp.float32
BF16 = jnp.bfloat16
I32 = jnp.int32
MIB = 1 << 20
UNROLL = 16
TILE = 16
COUNT_AT = 1 << 18
SMEM = pl.BlockSpec(memory_space=pltpu.SMEM)
VMEM = pl.BlockSpec(memory_space=pltpu.VMEM)
HBM = pl.BlockSpec(memory_space=pl.ANY)


def dot_nt(a, b):
    return lax.dot_general(a, b, (((1,), (1,)), ((), ())), preferred_element_type=F32)


def dot_nn(a, b):
    return lax.dot_general(a, b, (((1,), (0,)), ((), ())), preferred_element_type=F32)


def plan_kernel(
    shards, shard_rows, cap, parts, lengths_hbm, ids_hbm, queries_hbm, sent_ref, pos_ref,
    lengths_ref, ids_ref, queries_ref, sems,
):
    copies = [
        pltpu.make_async_copy(lengths_hbm, lengths_ref, sems.at[0]),
        pltpu.make_async_copy(ids_hbm, ids_ref, sems.at[1]),
        pltpu.make_async_copy(queries_hbm, queries_ref, sems.at[2]),
    ]
    for copy in copies:
        copy.start()
    for copy in copies:
        copy.wait()
    passages, height = ids_ref.shape
    span = queries_ref.shape[0]
    part = lax.axis_index("groups")
    ids = ids_ref[...]
    owner = ids // shard_rows
    offset = ids - owner * shard_rows
    row = lax.broadcasted_iota(I32, (passages, height), 0)
    lane = lax.broadcasted_iota(I32, (passages, height), 1)
    limit = jnp.zeros((passages, height), I32)
    for p in range(passages):
        limit = jnp.where(row == p, lengths_ref[p], limit)
    owner = jnp.where(lane < limit, owner, shards)
    mask = jnp.concatenate([jnp.where(owner == b, 1.0, 0.0) for b in range(shards)], axis=0)
    mask16 = mask.astype(BF16)
    k = lax.broadcasted_iota(I32, (height, height), 0)
    l = lax.broadcasted_iota(I32, (height, height), 1)
    inside = dot_nn(mask16, jnp.where(k < l, 1.0, 0.0).astype(BF16))
    totals = dot_nn(mask16, jnp.ones((height, height), BF16))
    full = shards * passages
    r = lax.broadcasted_iota(I32, (full, full), 0)
    c = lax.broadcasted_iota(I32, (full, full), 1)
    same = r // passages == c // passages
    ahead = dot_nn(jnp.where(same & (c < r), 1.0, 0.0).astype(BF16), totals.astype(BF16))
    place = (inside + ahead) * mask
    rank = jnp.zeros((passages, height), F32)
    for b in range(shards):
        rank = rank + place[b * passages : (b + 1) * passages]
    rank = rank.astype(I32)
    mine = (lane < limit) & (rank % parts == part)
    rank = rank // parts
    pos_ref[...] = jnp.where(mine, owner * cap + rank, -1)
    per = list_rows(cap, height)
    list_row = jnp.where(mine, owner * per + rank // height, -1)
    list_lane = rank % height
    high = (offset // 256).astype(F32)
    low = (offset % 256).astype(F32)
    rows = shards * per
    out_row = lax.broadcasted_iota(I32, (rows, height), 0)
    at_lane = lax.broadcasted_iota(I32, (height, height), 0)
    sums = jnp.zeros((rows, 2 * height), F32)
    for p in range(passages):
        here = jnp.where(out_row == list_row[p : p + 1], 1.0, 0.0).astype(BF16)
        hit = at_lane == list_lane[p : p + 1]
        values = jnp.concatenate(
            [jnp.where(hit, high[p : p + 1], 0.0), jnp.where(hit, low[p : p + 1], 0.0)], axis=0
        ).astype(BF16)
        sums = sums + dot_nt(here, values)
    queries = queries_ref[...]
    extra = message_rows(cap, height)
    for b in range(shards):
        total = jnp.sum(totals[b * passages : (b + 1) * passages], axis=0, keepdims=True)
        share = (total.astype(I32) + (parts - 1 - part)) // parts
        sent_ref[b, :span] = queries
        sent_ref[b, span:] = jnp.concatenate(
            [
                sums[b * per : (b + 1) * per, :height],
                sums[b * per : (b + 1) * per, height:],
                share.astype(F32),
                jnp.zeros((extra - 2 * per - 1, height), F32),
            ],
            axis=0,
        ).astype(BF16)


def list_rows(cap, lanes):
    return (cap + lanes - 1) // lanes


def message_rows(cap, lanes):
    return (2 * list_rows(cap, lanes) + TILE) // TILE * TILE


def plan(lengths, ids, queries, shards, shard_rows, cap, parts):
    passages, height = ids.shape
    span = queries.shape[0]
    return pl.pallas_call(
        functools.partial(plan_kernel, shards, shard_rows, cap, parts),
        out_shape=(
            jax.ShapeDtypeStruct((shards, span + message_rows(cap, height), height), BF16),
            jax.ShapeDtypeStruct((passages, height), I32),
        ),
        in_specs=[HBM, HBM, HBM],
        out_specs=(VMEM, VMEM),
        scratch_shapes=[
            pltpu.SMEM(lengths.shape, I32),
            pltpu.VMEM(ids.shape, I32),
            pltpu.VMEM(queries.shape, BF16),
            pltpu.SemaphoreType.DMA((3,)),
        ],
        compiler_params=pltpu.CompilerParams(vmem_limit_bytes=8 * MIB),
    )(lengths, ids, queries)


def order_kernel(pos_ref, list_ref):
    passages, height = pos_ref.shape
    pos = pos_ref[...]
    mine = jnp.where(pos >= 0, 1.0, 0.0).astype(BF16)
    k = lax.broadcasted_iota(I32, (height, height), 0)
    l = lax.broadcasted_iota(I32, (height, height), 1)
    rank = dot_nn(mine, jnp.where(k < l, 1.0, 0.0).astype(BF16))
    total = dot_nn(mine, jnp.ones((height, height), BF16))
    rank = jnp.where(pos >= 0, rank.astype(I32), -1)
    high = (pos // 256).astype(F32)
    low = (pos % 256).astype(F32)
    token = lax.broadcasted_iota(I32, (1, height), 1).astype(F32)
    for p in range(passages):
        hit = jnp.where(k == rank[p : p + 1], 1.0, 0.0).astype(BF16)
        values = jnp.concatenate([high[p : p + 1], low[p : p + 1], token], axis=0).astype(BF16)
        found = dot_nt(values, hit)
        place = found[0:1] * 256.0 + found[1:2]
        entry = (place * height + found[2:3]).astype(I32)
        list_ref[p : p + 1] = entry + total[p : p + 1].astype(I32) * COUNT_AT


def order(pos):
    return pl.pallas_call(
        order_kernel,
        out_shape=jax.ShapeDtypeStruct(pos.shape, I32),
        in_specs=[VMEM],
        out_specs=VMEM,
        compiler_params=pltpu.CompilerParams(vmem_limit_bytes=8 * MIB),
    )(pos)


def fetch_kernel(span, cap, received_ref, table_ref, out_ref, ask, asked, sem):
    shards = received_ref.shape[0]
    height = received_ref.shape[2]
    width = table_ref.shape[1]
    per = list_rows(cap, height)
    for d in range(shards):
        message = received_ref[d, span:].astype(F32)
        ask[d, :per] = (message[:per] * 256.0 + message[per : 2 * per]).astype(I32)
        ask[d, per : per + 1] = message[2 * per : 2 * per + 1].astype(I32)
    copy = pltpu.make_async_copy(ask, asked, sem)
    copy.start()
    copy.wait()
    line = lax.broadcasted_iota(I32, (8, width), 0)

    @pl.loop(0, shards)
    def _(d):
        count = asked[d, per, 0]

        @pl.loop(0, (count + TILE - 1) // TILE)
        def _(i):
            halves = [jnp.zeros((8, width), F32), jnp.zeros((8, width), F32)]
            at = i * TILE
            at_row, at_lane = at // height, lax.rem(at, height)
            for u in range(TILE):
                offset = asked[d, at_row, at_lane + u]
                low = offset & (TILE - 1)
                near = pl.multiple_of(offset - low, TILE)
                rows = table_ref[pl.ds(near, TILE)].astype(F32)
                row = jnp.where(low >= 8, rows[8:], rows[:8])
                row = pltpu.roll(row, (u - low) & 7, 0)
                halves[u // 8] = jnp.where(line == u % 8, row, halves[u // 8])
            to = pl.multiple_of(d * cap + at, TILE)
            out_ref[pl.ds(to, TILE)] = jnp.concatenate(halves, axis=0).astype(BF16)


def fetch(received, table, span, cap):
    width = table.shape[1]
    shards, _, height = received.shape
    ask_rows = (list_rows(cap, height) + 8) // 8 * 8
    return pl.pallas_call(
        functools.partial(fetch_kernel, span, cap),
        out_shape=jax.ShapeDtypeStruct((shards * cap, width), BF16),
        in_specs=[VMEM, VMEM],
        out_specs=VMEM,
        scratch_shapes=[
            pltpu.VMEM((shards, ask_rows, height), I32),
            pltpu.SMEM((shards, ask_rows, height), I32),
            pltpu.SemaphoreType.DMA,
        ],
        compiler_params=pltpu.CompilerParams(vmem_limit_bytes=24 * MIB),
    )(received, table)


def block_rows(height, shards, parts):
    most = min(height, (height + shards * (parts - 1)) // parts)
    return (most + 7) // 8 * 8


def residual_kernel(list_ref, codes_ref, buckets_ref, out_ref, picked):
    passages, block, width = out_ref.shape
    height = codes_ref.shape[1]

    @pl.loop(0, passages)
    def _(p):
        count = list_ref[p * height] // COUNT_AT

        @pl.loop(0, (count + UNROLL - 1) // UNROLL)
        def _(i):
            at = pl.multiple_of(i * UNROLL, UNROLL)
            for u in range(UNROLL):
                token = list_ref[p * height + at + u] & (height - 1)
                picked[pl.ds(at + u, 1)] = codes_ref[p, pl.ds(token, 1)]

        codes = picked[:block]
        out_ref[p] = jnp.where(
            codes == 0,
            buckets_ref[0:1],
            jnp.where(
                codes == 1,
                buckets_ref[1:2],
                jnp.where(codes == 2, buckets_ref[2:3], buckets_ref[3:4]),
            ),
        )


def residual(lists, codes, buckets, block):
    passages, height, width = codes.shape
    return pl.pallas_call(
        residual_kernel,
        out_shape=jax.ShapeDtypeStruct((passages, block, width), F32),
        in_specs=[SMEM, VMEM, VMEM],
        out_specs=VMEM,
        scratch_shapes=[pltpu.VMEM((block + UNROLL, width), I32)],
        compiler_params=pltpu.CompilerParams(vmem_limit_bytes=16 * MIB),
    )(lists, codes, buckets)


def score_kernel(span, list_ref, replies_ref, residual_ref, *refs):
    passages, block, width = residual_ref.shape
    *query_refs, out_ref, wide, tile, embedded = refs
    groups, subs = lax.axis_size("groups"), lax.axis_size("sub")
    own_group, own_sub = lax.axis_index("groups"), lax.axis_index("sub")
    shards = query_refs[0].shape[0]
    height = list_ref.shape[0] // passages
    pair = 2 if shards % 2 == 0 else 1

    @pl.loop(0, replies_ref.shape[0] // 256)
    def _(i):
        at = pl.multiple_of(i * 256, 256)
        wide[pl.ds(at, 256)] = replies_ref[pl.ds(at, 256)].astype(F32)

    @pl.loop(0, passages)
    def _(p):
        count = list_ref[p * height] // COUNT_AT

        @pl.loop(0, (count + UNROLL - 1) // UNROLL)
        def _(i):
            at = pl.multiple_of(i * UNROLL, UNROLL)
            for u in range(UNROLL):
                place = (list_ref[p * height + at + u] & (COUNT_AT - 1)) // height
                tile[pl.ds(p * block + at + u, 1)] = wide[pl.ds(place, 1)]

    line = lax.broadcasted_iota(I32, (block, width), 0)
    here = lax.broadcasted_iota(I32, (passages, pair * span), 0)
    counts = jnp.zeros((passages, pair * span), I32)
    for p in range(0, passages, 2):
        both = []
        for q in (p, p + 1):
            count = list_ref[q * height] // COUNT_AT
            counts = jnp.where(here == q, count, counts)
            rows = tile[q * block : (q + 1) * block] + residual_ref[q]
            both.append(jnp.where(line < count, rows, rows[0:1]))
        embedded[p * block : (p + 2) * block] = jnp.concatenate(both, axis=0).astype(BF16)

    for step, query_ref in enumerate(query_refs):
        group = lax.rem(own_group + groups - step // subs, groups)
        sub = lax.rem(own_sub + subs - step % subs, subs)

        @pl.loop(0, shards // pair)
        def _(c):
            queries = jnp.concatenate(
                [query_ref[c * pair + e, :span] for e in range(pair)], axis=0
            )
            scores = dot_nt(embedded[...], queries)
            best = jnp.max(scores.reshape(passages, block, pair * span), axis=1)
            best = jnp.where(counts > 0, best, -3e38)
            for e in range(pair):
                device = (group * shards + c * pair + e) * subs + sub
                out_ref[device] = best[:, e * span : (e + 1) * span]


def score(lists, replies, residuals, queries, span):
    passages, block, width = residuals.shape
    devices = len(queries) * queries[0].shape[0]
    return pl.pallas_call(
        functools.partial(score_kernel, span),
        out_shape=jax.ShapeDtypeStruct((devices, passages, span), F32),
        in_specs=[SMEM, VMEM, VMEM] + [VMEM] * len(queries),
        out_specs=VMEM,
        scratch_shapes=[
            pltpu.VMEM((replies.shape[0], width), F32),
            pltpu.VMEM((passages * block + UNROLL, width), F32),
            pltpu.VMEM((passages * block, width), BF16),
        ],
        compiler_params=pltpu.CompilerParams(vmem_limit_bytes=24 * MIB),
    )(lists, replies, residuals, *queries)


def pick_kernel(tokens, location_ref, candidates_ref, best_ref, out_ref):
    owned, listed = candidates_ref.shape
    parts, slots_total, span = best_ref.shape
    blocks, width = location_ref.shape
    which = lax.broadcasted_iota(I32, (width, listed), 0)
    slot = lax.broadcasted_iota(I32, (slots_total, listed), 0)
    sums = best_ref[0]
    for g in range(1, parts):
        sums = jnp.maximum(sums, best_ref[g])
    shift = tokens // 2
    while shift:
        sums = sums + pltpu.roll(sums, span - shift, 1)
        shift //= 2
    for q in range(owned):
        named = candidates_ref[q : q + 1]
        found = jnp.zeros((2, listed), F32)
        for g in range(blocks):
            here = location_ref[g : g + 1]
            pair = jnp.concatenate([here // 256, here % 256], axis=0).astype(F32).astype(BF16)
            hit = jnp.where(which + g * width == named, 1.0, 0.0).astype(BF16)
            found = found + dot_nn(pair, hit)
        slots = (found[0:1] * 256.0 + found[1:2]).astype(I32)
        column = jnp.broadcast_to(sums[:, q * tokens : q * tokens + 1], (slots_total, listed))
        out_ref[q : q + 1] = jnp.sum(jnp.where(slot == slots, column, 0.0), axis=0, keepdims=True)


def pick(location, candidates, best, tokens):
    return pl.pallas_call(
        functools.partial(pick_kernel, tokens),
        out_shape=jax.ShapeDtypeStruct(candidates.shape, F32),
        compiler_params=pltpu.CompilerParams(vmem_limit_bytes=16 * MIB),
    )(location, candidates, best)


def turned(array, axis, shift):
    size = lax.axis_size(axis)
    return lax.ppermute(array, axis, [(i, (i + shift) % size) for i in range(size)])


def body(queries, candidates, location, lengths, centroid_ids, residual_codes, centroids, buckets):
    token_count = centroid_ids.shape[0]
    passages = lengths.shape[0]
    height = token_count // passages
    width = residual_codes.shape[1]
    shard_rows = centroids.shape[0]
    shards, subs, parts = lax.axis_size("blk"), lax.axis_size("sub"), lax.axis_size("groups")
    cap = 2 * token_count // shards // parts
    owned, tokens = queries.shape[0], queries.shape[1]
    span = owned * tokens

    sent, pos = plan(
        lengths,
        centroid_ids.reshape(passages, height),
        queries.reshape(span, width),
        shards,
        shard_rows,
        cap,
        parts,
    )
    near = lax.all_to_all(sent, "blk", split_axis=0, concat_axis=0, tiled=True)
    found = fetch(near, centroids, span, cap)
    replies = lax.all_to_all(
        found.reshape(shards, cap, width), "blk", split_axis=0, concat_axis=0, tiled=True
    )
    lists = order(pos).reshape(token_count)
    residuals = residual(
        lists,
        residual_codes.reshape(passages, height, width),
        buckets,
        block_rows(height, shards, parts),
    )
    across = [near] + [turned(near, "groups", g) for g in range(1, parts)]
    spread = []
    for array in across:
        spread += [array] + [turned(array, "sub", s) for s in range(1, subs)]
    best = score(lists, replies.reshape(shards * cap, width), residuals, spread, span)
    mine = lax.all_to_all(best, ("groups", "blk", "sub"), split_axis=0, concat_axis=0, tiled=True)
    return pick(
        location.reshape(location.shape[0] // 128, 128),
        candidates,
        mine.reshape(parts, shards * subs * passages, span),
        tokens,
    )


def solution(mesh):
    in_specs = (
        P(("groups", "blk", "sub"), None, None),
        P(("groups", "blk", "sub"), None),
        P(),
        P(("blk", "sub")),
        P(("blk", "sub")),
        P(("blk", "sub"), None),
        P("blk", None),
        P(),
    )
    out_specs = P(("groups", "blk", "sub"), None)
    return jax.shard_map(body, mesh=mesh, in_specs=in_specs, out_specs=out_specs, check_vma=False)
```

time: 94.8 us -> 73.1 us (0.77)
  blocking collectives: 55.9 us -> 31.1 us
  waiting for transfers between devices: 0.01 us -> 8.41 us
  Pallas kernels: 28.5 us -> 22.7 us
  starting transfers between devices: 3.57 us -> 5.08 us
    all_to_all x3 -> x2, blocking collectives: 55.9 us -> 31.1 us  [the longest x1 17.4 us: body(): near = lax.all_to_all(sent, 'blk', split_axis=0, concat_axis=0, tiled=True)]
    pallas_call x3 -> x4, Pallas kernels: 20 us -> 12 us  [the longest x1 7.68 us: fetch(): pl.pallas_call(functools.partial(fetch_kernel, span, cap), out_shape=jax....]
    ppermute x0 -> x3, waiting for transfers between devices: none -> 5.46 us  [turned(): lax.ppermute(array, axis, [(i, (i + shift) % size) for i in range(size)])]
    all_to_all x1, waiting for transfers between devices: 0.01 us -> 2.95 us  [body(): lax.all_to_all(found.reshape(shards, cap, width), 'blk', split_axis=0, co...]
    pallas_call x1, Pallas kernels: 7.31 us -> 9.56 us  [score(): pl.pallas_call(functools.partial(score_kernel, span), out_shape=jax.Shape...]
    broadcast_in_dim x1 -> x0, local copies, waits for them, and re-layouts: 1.66 us -> none  [body(): jnp.broadcast_to(queries.reshape(1, span, width), (owners, span, width))]
    ppermute x0 -> x3, starting transfers between devices: none -> 1.55 us  [turned(): lax.ppermute(array, axis, [(i, (i + shift) % size) for i in range(size)])]
  transfers between devices with their start and end apart: 1 -> 4, of which waited for: 0 -> 2; matrix products, arithmetic and copies ran while one was open for 0% -> 0% of each run, Pallas kernels for 20% -> 4%
where the time goes in v2:
time: 73.1 us; the launch traced here: 72.9 us
  blocking collectives  31.1 us (43%)
  Pallas kernels  22.7 us (31%)
  waiting for transfers between devices  8.41 us (12%)
  local copies, waits for them, and re-layouts  5.54 us (8%)
  starting transfers between devices  5.08 us (7%)
    all_to_all x1, blocking collectives, body(): near = lax.all_to_all(sent, 'blk', split_axis=0, concat_axis=0, tiled=True)  17.4 us
    all_to_all x1, blocking collectives, body(): lax.all_to_all(best, ('groups', 'blk', 'sub'), split_axis=0, concat_axis=...  13.7 us
    pallas_call x1, Pallas kernels, score(): pl.pallas_call(functools.partial(score_kernel, span), out_shape=jax.Shape...  9.56 us
    pallas_call x1, Pallas kernels, fetch(): pl.pallas_call(functools.partial(fetch_kernel, span, cap), out_shape=jax....  7.68 us
    unnamed x16, local copies, waits for them, and re-layouts  5.54 us
    ppermute x3, waiting for transfers between devices, turned(): lax.ppermute(array, axis, [(i, (i + shift) % size) for i in range(size)])  5.46 us
    all_to_all x1, starting transfers between devices, body(): lax.all_to_all(found.reshape(shards, cap, width), 'blk', split_axis=0, co...  3.53 us
    all_to_all x1, waiting for transfers between devices, body(): lax.all_to_all(found.reshape(shards, cap, width), 'blk', split_axis=0, co...  2.95 us
  transfers between devices with their start and end apart: 4, of which 2 were waited for; matrix products, arithmetic and copies ran while one was open for 0% of the time, Pallas kernels for 4%

profile of v2, /device:TPU:0, one launch (start us, length us, event | category | flops | bytes accessed | tf_op | source)
XLA Modules:
  0.0 72.9 jit_solution(11134187816122286122)
XLA Ops:
  0.0 0.0 copy-start.4
  0.0 0.0 copy-start.6
  0.0 0.0 copy-start.2
  0.0 0.8 %copy-done.2 = bf16[4,32,128]{2,1,0:T(8,128)(2,1)S(1)} copy-done((bf16[4,32,128]{2,1,0:T(8,128)(2,1)S(1)}, bf16[4,32,128]{2,1,0:T(8,128)(2,1)}, u32[]{:S(2)}) %copy-start.2) | copy-done | bytes 32792
  0.8 0.0 copy-start.3
  0.8 0.7 copy-done.3
  1.5 0.0 copy-start.7
  1.5 0.7 copy-done.7
  2.1 0.0 copy-start.5
  2.1 1.3 %shard_map.82 = (bf16[8,144,128]{2,1,0:T(8,128)(2,1)S(1)}, s32[16,128]{1,0:T(8,128)S(1)}) custom-call(s32[16]{0:T(128)S(1)} %copy-done.7, s32[16,128]{1,0:T(8,128)S(1)} %bitcast.14, bf16[128,128]{1,0:T(8,128)(2,1)S(1)} %bitcast.13), custom_call_target="tpu_custom_call" | custom-call | tf_op jit(solution)/shard_map/pallas_call | solution.py:118
  3.5 17.4 %all_to_all.15.received_ref.refs_0_ = bf16[8,144,128]{2,1,0:T(8,128)(2,1)S(1)} all-to-all(bf16[8,144,128]{2,1,0:T(8,128)(2,1)S(1)} %get-tuple-element.8), channel_id=1, replica_groups=mesh['groups'=2,'blk'=8,'sub'=2] {'blk'}, dimensions={0} | all-to-all | bytes 589824 | tf_op jit(solution)/shard_map/all_to_all | solution.py:394
  20.9 0.0 copy-start
  20.9 3.4 %copy-done = bf16[32768,128]{1,0:T(8,128)(2,1)S(1)} copy-done((bf16[32768,128]{1,0:T(8,128)(2,1)S(1)}, bf16[32768,128]{1,0:T(8,128)(2,1)}, u32[]{:S(2)}) %copy-start) | copy-done | bytes 8388632
  24.3 0.0 copy-start.1
  24.3 7.7 %shard_map.84 = bf16[2048,128]{1,0:T(8,128)(2,1)} custom-call(bf16[8,144,128]{2,1,0:T(8,128)(2,1)S(1)} %all_to_all.15.received_ref.refs_0_, bf16[32768,128]{1,0:T(8,128)(2,1)S(1)} %copy-done), custom_call_target="tpu_custom_call" | custom-call | tf_op jit(solution)/shard_map/pallas_call | solution.py:206
  32.0 3.5 %all-to-all-start.1 = ((bf16[8,256,128]{2,1,0:T(8,128)(2,1)}), bf16[8,256,128]{2,1,0:T(8,128)(2,1)S(1)}, u32[]{:S(2)}, u32[]{:S(2)}) async-start(bf16[8,256,128]{2,1,0:T(8,128)(2,1)} %bitcast.4), calls=%async_computation.1 | async-start | bytes 1048576 | tf_op jit(solution)/shard_map/all_to_all | solution.py:396
  35.5 1.5 %collective-permute-start.1 = (bf16[8,144,128]{2,1,0:T(8,128)(2,1)S(1)}, bf16[8,144,128]{2,1,0:T(8,128)(2,1)S(1)}, u32[]{:S(2)}, u32[]{:S(2)}) collective-permute-start(bf16[8,144,128]{2,1,0:T(8,128)(2,1)S(1)} %all_to_all.15.received_ref.refs_0_), channel_id=1, source_target_pairs={{0,16},{16,0},{1,17},{17,1},{2,18},{18,2},{3,19},{19,3},{4,20},{20... | collective-permute-start | bytes 884744 | tf_op jit(solution)/shard_map/ppermute | solution.py:371
  37.1 0.0 collective-permute-start
  37.1 5.5 %collective-permute-done.1.refs_2_ = bf16[8,144,128]{2,1,0:T(8,128)(2,1)S(1)} collective-permute-done((bf16[8,144,128]{2,1,0:T(8,128)(2,1)S(1)}, bf16[8,144,128]{2,1,0:T(8,128)(2,1)S(1)}, u32[]{:S(2)}, u32[]{:S(2)}) %collective-permute-start.1) | collective-permute-done | bytes 294944 | tf_op jit(solution)/shard_map/ppermute | solution.py:371
  42.5 0.0 collective-permute-start.2
  42.5 0.5 shard_map.83
  43.0 0.0 copy-done.4
  43.0 0.0 copy-done.1
  43.1 2.5 %shard_map.85.residual_ref = f32[16,72,128]{2,1,0:T(8,128)S(1)} custom-call(s32[2048]{0:T(1024)S(1)} %bitcast.11, s32[16,128,128]{2,1,0:T(8,128)S(1)} %bitcast.9, f32[4,128]{1,0:T(4,128)S(1)} %copy-done.4), custom_call_target="tpu_custom_call" | custom-call | tf_op jit(solution)/shard_map/pallas_call | solution.py:254
  45.6 0.0 collective-permute-done.refs_1_
  45.6 0.0 collective-permute-done.2.refs_3_
  45.6 2.9 %all-to-all-done.1 = bf16[8,256,128]{2,1,0:T(8,128)(2,1)S(1)} async-done(((bf16[8,256,128]{2,1,0:T(8,128)(2,1)}), bf16[8,256,128]{2,1,0:T(8,128)(2,1)S(1)}, u32[]{:S(2)}, u32[]{:S(2)}) %all-to-all-start.1) | async-done | bytes 524320 | tf_op jit(solution)/shard_map/all_to_all | solution.py:396
  48.5 9.6 %shard_map.86 = f32[32,16,128]{2,1,0:T(8,128)S(1)} custom-call(s32[2048]{0:T(1024)S(1)} %bitcast.12, bf16[2048,128]{1,0:T(8,128)(2,1)S(1)} %bitcast.8, f32[16,72,128]{2,1,0:T(8,128)S(1)} %shard_map.85.residual_ref, bf16[8,144,128]{2,1,0:T(8,128)(2,1)S(1)} %all_to_all.15.received_ref.refs_0_, bf16[8,144,128]{2,1,0:T(8,128)(2,1)S(1)} %collective-permute-done.refs_1_, ...), custom_call_target="tpu_custom_call" | custom-call | tf_op jit(solution)/shard_map/pallas_call | solution.py:321
  58.1 13.7 %all_to_all.16 = f32[32,16,128]{2,1,0:T(8,128)S(1)} all-to-all(f32[32,16,128]{2,1,0:T(8,128)S(1)} %shard_map.86), channel_id=1, replica_groups=mesh['groups'=2,'blk'=8,'sub'=2] {'groups','blk','sub'}, dimensions={0} | all-to-all | bytes 524288 | tf_op jit(solution)/shard_map/all_to_all | solution.py:411
  71.8 0.0 copy-done.6
  71.8 0.0 copy-done.5
  71.8 1.1 %shard_map.87 = f32[4,128]{1,0:T(4,128)} custom-call(s32[2,128]{1,0:T(2,128)S(1)} %bitcast.15, s32[4,128]{1,0:T(4,128)S(1)} %copy-done.5, f32[2,256,128]{2,1,0:T(8,128)S(1)} %bitcast.10), custom_call_target="tpu_custom_call" | custom-call | tf_op jit(solution)/shard_map/pallas_call | solution.py:362
Async XLA Ops:
  0.0 43.0 %copy-start.4 = (f32[4,128]{1,0:T(4,128)S(1)}, f32[4,128]{1,0:T(4,128)}, u32[]{:S(2)}) copy-start(f32[4,128]{1,0:T(4,128)} %buckets_ref.1) | copy-start | bytes 6148
  0.0 71.8 %copy-start.6 = (s32[256]{0:T(256)S(1)}, s32[256]{0:T(256)}, u32[]{:S(2)}) copy-start(s32[256]{0:T(256)} %param.10) | copy-start | bytes 3076
  0.0 0.8 %copy-start.2 = (bf16[4,32,128]{2,1,0:T(8,128)(2,1)S(1)}, bf16[4,32,128]{2,1,0:T(8,128)(2,1)}, u32[]{:S(2)}) copy-start(bf16[4,32,128]{2,1,0:T(8,128)(2,1)} %param.8) | copy-start | bytes 98308
  0.8 0.7 copy-start.3
  1.5 0.7 copy-start.7
  2.1 69.7 %copy-start.5 = (s32[4,128]{1,0:T(4,128)S(1)}, s32[4,128]{1,0:T(4,128)}, u32[]{:S(2)}) copy-start(s32[4,128]{1,0:T(4,128)} %candidates_ref.1) | copy-start | bytes 6148
  20.9 3.4 %copy-start = (bf16[32768,128]{1,0:T(8,128)(2,1)S(1)}, bf16[32768,128]{1,0:T(8,128)(2,1)}, u32[]{:S(2)}) copy-start(bf16[32768,128]{1,0:T(8,128)(2,1)} %table_ref.1) | copy-start | bytes 25165828
  24.3 18.8 %copy-start.1 = (s32[2048,128]{1,0:T(8,128)S(1)}, s32[2048,128]{1,0:T(8,128)}, u32[]{:S(2)}) copy-start(s32[2048,128]{1,0:T(8,128)} %param.13) | copy-start | bytes 3145732
  32.0 16.6 %all-to-all-start.1 = ((bf16[8,256,128]{2,1,0:T(8,128)(2,1)}), bf16[8,256,128]{2,1,0:T(8,128)(2,1)S(1)}, u32[]{:S(2)}, u32[]{:S(2)}) async-start(bf16[8,256,128]{2,1,0:T(8,128)(2,1)} %bitcast.4), calls=%async_computation.1 | async-start | bytes 1048576 | tf_op jit(solution)/shard_map/all_to_all | solution.py:396
  35.5 7.0 %collective-permute-start.1 = (bf16[8,144,128]{2,1,0:T(8,128)(2,1)S(1)}, bf16[8,144,128]{2,1,0:T(8,128)(2,1)S(1)}, u32[]{:S(2)}, u32[]{:S(2)}) collective-permute-start(bf16[8,144,128]{2,1,0:T(8,128)(2,1)S(1)} %all_to_all.15.received_ref.refs_0_), channel_id=1, source_target_pairs={{0,16},{16,0},{1,17},{17,1},{2,18},{18,2},{3,19},{19,3},{4,20},{20... | collective-permute-start | bytes 884744 | tf_op jit(solution)/shard_map/ppermute | solution.py:371
  37.1 8.5 %collective-permute-start = (bf16[8,144,128]{2,1,0:T(8,128)(2,1)S(1)}, bf16[8,144,128]{2,1,0:T(8,128)(2,1)S(1)}, u32[]{:S(2)}, u32[]{:S(2)}) collective-permute-start(bf16[8,144,128]{2,1,0:T(8,128)(2,1)S(1)} %all_to_all.15.received_ref.refs_0_), channel_id=1, source_target_pairs={{0,1},{1,0},{2,3},{3,2},{4,5},{5,4},{6,7},{7,6},{8,9},{9,8},{10,11... | collective-permute-start | bytes 884744 | tf_op jit(solution)/shard_map/ppermute | solution.py:371
  42.5 3.1 %collective-permute-start.2 = (bf16[8,144,128]{2,1,0:T(8,128)(2,1)S(1)}, bf16[8,144,128]{2,1,0:T(8,128)(2,1)S(1)}, u32[]{:S(2)}, u32[]{:S(2)}) collective-permute-start(bf16[8,144,128]{2,1,0:T(8,128)(2,1)S(1)} %collective-permute-done.1.refs_2_), channel_id=1, source_target_pairs={{0,1},{1,0},{2,3},{3,2},{4,5},{5,4},{6,7},{7,6},{8,9},{9,8},{10,11... | collective-permute-start | bytes 884744 | tf_op jit(solution)/shard_map/ppermute | solution.py:371

commit v3 on v2

--- a/solution.py
+++ b/solution.py
@@ -13,7 +13,8 @@
 MIB = 1 << 20
 UNROLL = 16
 TILE = 16
-COUNT_AT = 1 << 18
+TOKEN_AT = 12
+COUNT_AT = 20
 SMEM = pl.BlockSpec(memory_space=pltpu.SMEM)
 VMEM = pl.BlockSpec(memory_space=pltpu.VMEM)
 HBM = pl.BlockSpec(memory_space=pl.ANY)
@@ -129,18 +130,24 @@
             pltpu.VMEM(queries.shape, BF16),
             pltpu.SemaphoreType.DMA((3,)),
         ],
-        compiler_params=pltpu.CompilerParams(vmem_limit_bytes=8 * MIB),
+        compiler_params=pltpu.CompilerParams(vmem_limit_bytes=56 * MIB),
     )(lengths, ids, queries)
 
 
-def order_kernel(pos_ref, list_ref):
+def block_rows(height, shards, parts):
+    most = min(height, (height + shards * (parts - 1)) // parts)
+    return (most + 7) // 8 * 8
+
+
+def prepare_kernel(pos_ref, codes_ref, buckets_ref, list_ref, residual_ref, flat, picked, sems):
     passages, height = pos_ref.shape
+    block, width = residual_ref.shape[1:]
     pos = pos_ref[...]
     mine = jnp.where(pos >= 0, 1.0, 0.0).astype(BF16)
     k = lax.broadcasted_iota(I32, (height, height), 0)
     l = lax.broadcasted_iota(I32, (height, height), 1)
     rank = dot_nn(mine, jnp.where(k < l, 1.0, 0.0).astype(BF16))
-    total = dot_nn(mine, jnp.ones((height, height), BF16))
+    total = dot_nn(mine, jnp.ones((height, height), BF16)).astype(I32)
     rank = jnp.where(pos >= 0, rank.astype(I32), -1)
     high = (pos // 256).astype(F32)
     low = (pos % 256).astype(F32)
@@ -148,97 +155,35 @@
     for p in range(passages):
         hit = jnp.where(k == rank[p : p + 1], 1.0, 0.0).astype(BF16)
         values = jnp.concatenate([high[p : p + 1], low[p : p + 1], token], axis=0).astype(BF16)
-        found = dot_nt(values, hit)
-        place = found[0:1] * 256.0 + found[1:2]
-        entry = (place * height + found[2:3]).astype(I32)
-        list_ref[p : p + 1] = entry + total[p : p + 1].astype(I32) * COUNT_AT
-
-
-def order(pos):
-    return pl.pallas_call(
-        order_kernel,
-        out_shape=jax.ShapeDtypeStruct(pos.shape, I32),
-        in_specs=[VMEM],
-        out_specs=VMEM,
-        compiler_params=pltpu.CompilerParams(vmem_limit_bytes=8 * MIB),
-    )(pos)
-
-
-def fetch_kernel(span, cap, received_ref, table_ref, out_ref, ask, asked, sem):
-    shards = received_ref.shape[0]
-    height = received_ref.shape[2]
-    width = table_ref.shape[1]
-    per = list_rows(cap, height)
-    for d in range(shards):
-        message = received_ref[d, span:].astype(F32)
-        ask[d, :per] = (message[:per] * 256.0 + message[per : 2 * per]).astype(I32)
-        ask[d, per : per + 1] = message[2 * per : 2 * per + 1].astype(I32)
-    copy = pltpu.make_async_copy(ask, asked, sem)
-    copy.start()
-    copy.wait()
-    line = lax.broadcasted_iota(I32, (8, width), 0)
-
-    @pl.loop(0, shards)
-    def _(d):
-        count = asked[d, per, 0]
-
-        @pl.loop(0, (count + TILE - 1) // TILE)
-        def _(i):
-            halves = [jnp.zeros((8, width), F32), jnp.zeros((8, width), F32)]
-            at = i * TILE
-            at_row, at_lane = at // height, lax.rem(at, height)
-            for u in range(TILE):
-                offset = asked[d, at_row, at_lane + u]
-                low = offset & (TILE - 1)
-                near = pl.multiple_of(offset - low, TILE)
-                rows = table_ref[pl.ds(near, TILE)].astype(F32)
-                row = jnp.where(low >= 8, rows[8:], rows[:8])
-                row = pltpu.roll(row, (u - low) & 7, 0)
-                halves[u // 8] = jnp.where(line == u % 8, row, halves[u // 8])
-            to = pl.multiple_of(d * cap + at, TILE)
-            out_ref[pl.ds(to, TILE)] = jnp.concatenate(halves, axis=0).astype(BF16)
-
-
-def fetch(received, table, span, cap):
-    width = table.shape[1]
-    shards, _, height = received.shape
-    ask_rows = (list_rows(cap, height) + 8) // 8 * 8
-    return pl.pallas_call(
-        functools.partial(fetch_kernel, span, cap),
-        out_shape=jax.ShapeDtypeStruct((shards * cap, width), BF16),
-        in_specs=[VMEM, VMEM],
-        out_specs=VMEM,
-        scratch_shapes=[
-            pltpu.VMEM((shards, ask_rows, height), I32),
-            pltpu.SMEM((shards, ask_rows, height), I32),
-            pltpu.SemaphoreType.DMA,
-        ],
-        compiler_params=pltpu.CompilerParams(vmem_limit_bytes=24 * MIB),
-    )(received, table)
-
-
-def block_rows(height, shards, parts):
-    most = min(height, (height + shards * (parts - 1)) // parts)
-    return (most + 7) // 8 * 8
-
-
-def residual_kernel(list_ref, codes_ref, buckets_ref, out_ref, picked):
-    passages, block, width = out_ref.shape
-    height = codes_ref.shape[1]
+        found = dot_nt(values, hit).astype(I32)
+        list_ref[p : p + 1] = (
+            found[0:1] * 256
+            + found[1:2]
+            + found[2:3] * (1 << TOKEN_AT)
+            + total[p : p + 1] * (1 << COUNT_AT)
+        )
+    copies = [
+        pltpu.make_async_copy(list_ref.at[p], flat.at[pl.ds(p * height, height)], sems.at[p])
+        for p in range(passages)
+    ]
+    for copy in copies:
+        copy.start()
+    for copy in copies:
+        copy.wait()
 
     @pl.loop(0, passages)
     def _(p):
-        count = list_ref[p * height] // COUNT_AT
+        count = flat[p * height] >> COUNT_AT
 
         @pl.loop(0, (count + UNROLL - 1) // UNROLL)
         def _(i):
             at = pl.multiple_of(i * UNROLL, UNROLL)
             for u in range(UNROLL):
-                token = list_ref[p * height + at + u] & (height - 1)
+                token = (flat[p * height + at + u] >> TOKEN_AT) & ((1 << COUNT_AT - TOKEN_AT) - 1)
                 picked[pl.ds(at + u, 1)] = codes_ref[p, pl.ds(token, 1)]
 
         codes = picked[:block]
-        out_ref[p] = jnp.where(
+        residual_ref[p] = jnp.where(
             codes == 0,
             buckets_ref[0:1],
             jnp.where(
@@ -249,16 +194,95 @@
         )
 
 
-def residual(lists, codes, buckets, block):
+def prepare(pos, codes, buckets, block):
     passages, height, width = codes.shape
     return pl.pallas_call(
-        residual_kernel,
-        out_shape=jax.ShapeDtypeStruct((passages, block, width), F32),
-        in_specs=[SMEM, VMEM, VMEM],
+        prepare_kernel,
+        out_shape=(
+            jax.ShapeDtypeStruct((passages, height), I32),
+            jax.ShapeDtypeStruct((passages, block, width), F32),
+        ),
+        in_specs=[VMEM, VMEM, VMEM],
+        out_specs=(VMEM, VMEM),
+        scratch_shapes=[
+            pltpu.SMEM((passages * height,), I32),
+            pltpu.VMEM((block + UNROLL, width), I32),
+            pltpu.SemaphoreType.DMA((passages,)),
+        ],
+        compiler_params=pltpu.CompilerParams(vmem_limit_bytes=56 * MIB),
+    )(pos, codes, buckets)
+
+
+def fetch_kernel(
+    span, shard_rows, cap, received_ref, table_hbm, after_ref, out_ref, table_ref, ask, asked, stage, sems, sem
+):
+    shards = received_ref.shape[0]
+    height = received_ref.shape[2]
+    width = table_ref.shape[1]
+    per = list_rows(cap, height)
+    load = pltpu.make_async_copy(table_hbm, table_ref, sem)
+    load.start()
+    copies = []
+    for d in range(shards):
+        message = received_ref[d, span:].astype(F32)
+        count = message[2 * per : 2 * per + 1].astype(I32)
+        offset = (message[:per] * 256.0 + message[per : 2 * per]).astype(I32)
+        ask[d * per : (d + 1) * per] = offset + count * shard_rows
+    for r in range(shards * per):
+        copies.append(
+            pltpu.make_async_copy(ask.at[r], asked.at[pl.ds(r * height, height)], sems.at[r])
+        )
+    for copy in copies:
+        copy.start()
+    for copy in copies:
+        copy.wait()
+    line = lax.broadcasted_iota(I32, (8, width), 0)
+    low_bits = TILE - 1
+    near_bits = shard_rows - TILE
+    load.wait()
+
+    @pl.loop(0, shards)
+    def _(d):
+        base = d * (per * height)
+        count = asked[base] // shard_rows
+
+        @pl.loop(0, (count + TILE - 1) // TILE)
+        def _(i):
+            at = pl.multiple_of(base + i * TILE, TILE)
+            for u in range(TILE):
+                near = pl.multiple_of(asked[at + u] & near_bits, TILE)
+                stage[u * TILE : (u + 1) * TILE] = table_ref[pl.ds(near, TILE)].astype(F32)
+            halves = []
+            for h in range(0, TILE, 8):
+                half = jnp.zeros((8, width), F32)
+                for u in range(h, h + 8):
+                    row = stage[pl.ds(u * TILE + (asked[at + u] & low_bits), 1)]
+                    half = jnp.where(line == u - h, row, half)
+                halves.append(half)
+            to = pl.multiple_of(d * cap + i * TILE, TILE)
+            out_ref[pl.ds(to, TILE)] = jnp.concatenate(halves, axis=0).astype(BF16)
+
+
+def fetch(received, table, after, span, cap):
+    shard_rows, width = table.shape
+    shards, _, height = received.shape
+    rows = shards * list_rows(cap, height)
+    assert shard_rows & (shard_rows - 1) == 0
+    return pl.pallas_call(
+        functools.partial(fetch_kernel, span, shard_rows, cap),
+        out_shape=jax.ShapeDtypeStruct((shards * cap, width), BF16),
+        in_specs=[VMEM, HBM, HBM],
         out_specs=VMEM,
-        scratch_shapes=[pltpu.VMEM((block + UNROLL, width), I32)],
-        compiler_params=pltpu.CompilerParams(vmem_limit_bytes=16 * MIB),
-    )(lists, codes, buckets)
+        scratch_shapes=[
+            pltpu.VMEM(table.shape, table.dtype),
+            pltpu.VMEM((rows, height), I32),
+            pltpu.SMEM((rows * height,), I32),
+            pltpu.VMEM((TILE * TILE, width), F32),
+            pltpu.SemaphoreType.DMA((rows,)),
+            pltpu.SemaphoreType.DMA,
+        ],
+        compiler_params=pltpu.CompilerParams(vmem_limit_bytes=56 * MIB),
+    )(received, table, after)
 
 
 def score_kernel(span, list_ref, replies_ref, residual_ref, *refs):
@@ -269,6 +293,7 @@
     shards = query_refs[0].shape[0]
     height = list_ref.shape[0] // passages
     pair = 2 if shards % 2 == 0 else 1
+    ahead = 4 if shards % (4 * pair) == 0 else 1
 
     @pl.loop(0, replies_ref.shape[0] // 256)
     def _(i):
@@ -277,13 +302,13 @@
 
     @pl.loop(0, passages)
     def _(p):
-        count = list_ref[p * height] // COUNT_AT
+        count = list_ref[p * height] >> COUNT_AT
 
         @pl.loop(0, (count + UNROLL - 1) // UNROLL)
         def _(i):
             at = pl.multiple_of(i * UNROLL, UNROLL)
             for u in range(UNROLL):
-                place = (list_ref[p * height + at + u] & (COUNT_AT - 1)) // height
+                place = list_ref[p * height + at + u] & ((1 << TOKEN_AT) - 1)
                 tile[pl.ds(p * block + at + u, 1)] = wide[pl.ds(place, 1)]
 
     line = lax.broadcasted_iota(I32, (block, width), 0)
@@ -292,7 +317,7 @@
     for p in range(0, passages, 2):
         both = []
         for q in (p, p + 1):
-            count = list_ref[q * height] // COUNT_AT
+            count = list_ref[q * height] >> COUNT_AT
             counts = jnp.where(here == q, count, counts)
             rows = tile[q * block : (q + 1) * block] + residual_ref[q]
             both.append(jnp.where(line < count, rows, rows[0:1]))
@@ -302,17 +327,19 @@
         group = lax.rem(own_group + groups - step // subs, groups)
         sub = lax.rem(own_sub + subs - step % subs, subs)
 
-        @pl.loop(0, shards // pair)
-        def _(c):
-            queries = jnp.concatenate(
-                [query_ref[c * pair + e, :span] for e in range(pair)], axis=0
-            )
-            scores = dot_nt(embedded[...], queries)
-            best = jnp.max(scores.reshape(passages, block, pair * span), axis=1)
-            best = jnp.where(counts > 0, best, -3e38)
-            for e in range(pair):
-                device = (group * shards + c * pair + e) * subs + sub
-                out_ref[device] = best[:, e * span : (e + 1) * span]
+        @pl.loop(0, shards // (pair * ahead))
+        def _(i):
+            for h in range(ahead):
+                c = i * ahead + h
+                queries = jnp.concatenate(
+                    [query_ref[c * pair + e, :span] for e in range(pair)], axis=0
+                )
+                scores = dot_nt(embedded[...], queries)
+                best = jnp.max(scores.reshape(passages, block, pair * span), axis=1)
+                best = jnp.where(counts > 0, best, -3e38)
+                for e in range(pair):
+                    device = (group * shards + c * pair + e) * subs + sub
+                    out_ref[device] = best[:, e * span : (e + 1) * span]
 
 
 def score(lists, replies, residuals, queries, span):
@@ -392,22 +419,21 @@
         parts,
     )
     near = lax.all_to_all(sent, "blk", split_axis=0, concat_axis=0, tiled=True)
-    found = fetch(near, centroids, span, cap)
-    replies = lax.all_to_all(
-        found.reshape(shards, cap, width), "blk", split_axis=0, concat_axis=0, tiled=True
-    )
-    lists = order(pos).reshape(token_count)
-    residuals = residual(
-        lists,
+    lists, residuals = prepare(
+        pos,
         residual_codes.reshape(passages, height, width),
         buckets,
         block_rows(height, shards, parts),
+    )
+    found = fetch(near, centroids, residuals, span, cap)
+    replies = lax.all_to_all(
+        found.reshape(shards, cap, width), "blk", split_axis=0, concat_axis=0, tiled=True
     )
     across = [near] + [turned(near, "groups", g) for g in range(1, parts)]
     spread = []
     for array in across:
         spread += [array] + [turned(array, "sub", s) for s in range(1, subs)]
-    best = score(lists, replies.reshape(shards * cap, width), residuals, spread, span)
+    best = score(lists.reshape(token_count), replies.reshape(shards * cap, width), residuals, spread, span)
     mine = lax.all_to_all(best, ("groups", "blk", "sub"), split_axis=0, concat_axis=0, tiled=True)
     return pick(
         location.reshape(location.shape[0] // 128, 128),

time: 73.1 us -> 66.2 us (0.906)
  blocking collectives: 31.1 us -> 13.8 us
  waiting for transfers between devices: 8.41 us -> 17 us
  starting transfers between devices: 5.08 us -> 12.4 us
  local copies, waits for them, and re-layouts: 5.54 us -> 1.7 us
  Pallas kernels: 22.7 us -> 20.4 us
    all_to_all x1 -> x0, blocking collectives: 17.4 us -> none  [body(): near = lax.all_to_all(sent, 'blk', split_axis=0, concat_axis=0, tiled=True)]
    all_to_all x0 -> x1, starting transfers between devices: none -> 7.29 us  [body(): near = lax.all_to_all(sent, 'blk', split_axis=0, concat_axis=0, tiled=True)]
    pallas_call x1, Pallas kernels: 9.56 us -> 4.65 us  [score(): pl.pallas_call(functools.partial(score_kernel, span), out_shape=jax.Shape...]
    all_to_all x0 -> x1, waiting for transfers between devices: none -> 4.51 us  [body(): near = lax.all_to_all(sent, 'blk', split_axis=0, concat_axis=0, tiled=True)]
    unnamed x16 -> x12, local copies, waits for them, and re-layouts: 5.54 us -> 1.7 us
    ppermute x3, waiting for transfers between devices: 5.46 us -> 8.24 us  [turned(): lax.ppermute(array, axis, [(i, (i + shift) % size) for i in range(size)])]
    pallas_call x3 -> x2, Pallas kernels: 10.7 us -> 12.4 us  [the longest x1 7.29 us: fetch(): pl.pallas_call(functools.partial(fetch_kernel, span, shard_rows, cap), ou...]
    all_to_all x1, waiting for transfers between devices: 2.95 us -> 4.27 us  [body(): lax.all_to_all(found.reshape(shards, cap, width), 'blk', split_axis=0, co...]
  transfers between devices with their start and end apart: 4 -> 5, of which waited for: 2 -> 4; matrix products, arithmetic and copies ran while one was open for 0% -> 0% of each run, Pallas kernels for 4% -> 8%
where the time goes in v3:
time: 66.2 us; the launch traced here: 65.5 us
  Pallas kernels  20.4 us (31%)
  waiting for transfers between devices  17 us (26%)
  blocking collectives  13.8 us (21%)
  starting transfers between devices  12.4 us (19%)
  local copies, waits for them, and re-layouts  1.7 us (3%)
    all_to_all x1, blocking collectives, body(): lax.all_to_all(best, ('groups', 'blk', 'sub'), split_axis=0, concat_axis=...  13.8 us
    ppermute x3, waiting for transfers between devices, turned(): lax.ppermute(array, axis, [(i, (i + shift) % size) for i in range(size)])  8.24 us
    pallas_call x1, Pallas kernels, fetch(): pl.pallas_call(functools.partial(fetch_kernel, span, shard_rows, cap), ou...  7.29 us
    all_to_all x1, starting transfers between devices, body(): near = lax.all_to_all(sent, 'blk', split_axis=0, concat_axis=0, tiled=True)  7.29 us
    pallas_call x1, Pallas kernels, prepare(): pl.pallas_call(prepare_kernel, out_shape=(jax.ShapeDtypeStruct((passages,...  5.08 us
    pallas_call x1, Pallas kernels, score(): pl.pallas_call(functools.partial(score_kernel, span), out_shape=jax.Shape...  4.65 us
    all_to_all x1, waiting for transfers between devices, body(): near = lax.all_to_all(sent, 'blk', split_axis=0, concat_axis=0, tiled=True)  4.51 us
    all_to_all x1, waiting for transfers between devices, body(): lax.all_to_all(found.reshape(shards, cap, width), 'blk', split_axis=0, co...  4.27 us
  transfers between devices with their start and end apart: 5, of which 4 were waited for; matrix products, arithmetic and copies ran while one was open for 0% of the time, Pallas kernels for 8%

profile of v3, /device:TPU:0, one launch (start us, length us, event | category | flops | bytes accessed | tf_op | source)
XLA Modules:
  0.0 65.5 jit_solution(13964882326980400471)
XLA Ops:
  0.0 0.0 copy-start.5
  0.0 0.0 copy-start.4
  0.0 2.3 %shard_map.82 = (bf16[8,144,128]{2,1,0:T(8,128)(2,1)}, s32[16,128]{1,0:T(8,128)}) custom-call(s32[16]{0:T(128)} %lengths_hbm.1, s32[16,128]{1,0:T(8,128)} %bitcast.15, bf16[128,128]{1,0:T(8,128)(2,1)} %bitcast.14), custom_call_target="tpu_custom_call" | custom-call | tf_op jit(solution)/shard_map/pallas_call | solution.py:119
  2.3 7.3 %all-to-all-start = ((bf16[8,144,128]{2,1,0:T(8,128)(2,1)}), bf16[8,144,128]{2,1,0:T(8,128)(2,1)S(1)}, u32[]{:S(2)}, u32[]{:S(2)}) async-start(bf16[8,144,128]{2,1,0:T(8,128)(2,1)} %get-tuple-element.11), calls=%async_computation | async-start | bytes 589824 | tf_op jit(solution)/shard_map/all_to_all | solution.py:421
  9.6 5.1 %shard_map.83 = (s32[16,128]{1,0:T(8,128)}, f32[16,72,128]{2,1,0:T(8,128)}) custom-call(s32[16,128]{1,0:T(8,128)} %get-tuple-element.9.pos_ref, s32[16,128,128]{2,1,0:T(8,128)} %bitcast.13, f32[4,128]{1,0:T(4,128)} %buckets_ref.1), custom_call_target="tpu_custom_call" | custom-call | tf_op jit(solution)/shard_map/pallas_call | solution.py:199
  14.7 0.0 copy-start.2
  14.7 0.0 copy-start.3
  14.7 4.5 %all-to-all-done.received_ref.refs_0_ = bf16[8,144,128]{2,1,0:T(8,128)(2,1)S(1)} async-done(((bf16[8,144,128]{2,1,0:T(8,128)(2,1)}), bf16[8,144,128]{2,1,0:T(8,128)(2,1)S(1)}, u32[]{:S(2)}, u32[]{:S(2)}) %all-to-all-start) | async-done | bytes 294944 | tf_op jit(solution)/shard_map/all_to_all | solution.py:421
  19.2 0.0 copy-start
  19.2 0.7 %copy-done = bf16[8,144,128]{2,1,0:T(8,128)(2,1)} copy-done((bf16[8,144,128]{2,1,0:T(8,128)(2,1)}, bf16[8,144,128]{2,1,0:T(8,128)(2,1)S(1)}, u32[]{:S(2)}) %copy-start) | copy-done | bytes 294936
  19.9 7.3 %shard_map.84 = bf16[2048,128]{1,0:T(8,128)(2,1)} custom-call(bf16[8,144,128]{2,1,0:T(8,128)(2,1)} %copy-done, bf16[32768,128]{1,0:T(8,128)(2,1)} %table_hbm.1, f32[16,72,128]{2,1,0:T(8,128)} %get-tuple-element.12.after_ref.residual_ref), custom_call_target="tpu_custom_call" | custom-call | tf_op jit(solution)/shard_map/pallas_call | solution.py:271
  27.2 3.6 %all-to-all-start.1 = ((bf16[8,256,128]{2,1,0:T(8,128)(2,1)}), bf16[8,256,128]{2,1,0:T(8,128)(2,1)S(1)}, u32[]{:S(2)}, u32[]{:S(2)}) async-start(bf16[8,256,128]{2,1,0:T(8,128)(2,1)} %bitcast.12), calls=%async_computation.1 | async-start | bytes 1048576 | tf_op jit(solution)/shard_map/all_to_all | solution.py:429
  30.9 1.5 %collective-permute-start.1 = (bf16[8,144,128]{2,1,0:T(8,128)(2,1)}, bf16[8,144,128]{2,1,0:T(8,128)(2,1)S(1)}, u32[]{:S(2)}, u32[]{:S(2)}) collective-permute-start(bf16[8,144,128]{2,1,0:T(8,128)(2,1)} %copy-done), channel_id=1, source_target_pairs={{0,16},{16,0},{1,17},{17,1},{2,18},{18,2},{3,19},{19,3},{4,20},{20... | collective-permute-start | bytes 884744 | tf_op jit(solution)/shard_map/ppermute | solution.py:398
  32.4 0.0 collective-permute-start
  32.4 6.7 %collective-permute-done.1.refs_2_ = bf16[8,144,128]{2,1,0:T(8,128)(2,1)S(1)} collective-permute-done((bf16[8,144,128]{2,1,0:T(8,128)(2,1)}, bf16[8,144,128]{2,1,0:T(8,128)(2,1)S(1)}, u32[]{:S(2)}, u32[]{:S(2)}) %collective-permute-start.1) | collective-permute-done | bytes 294944 | tf_op jit(solution)/shard_map/ppermute | solution.py:398
  39.0 0.0 collective-permute-start.2
  39.0 0.0 collective-permute-done.refs_1_
  39.0 1.6 %collective-permute-done.2.refs_3_ = bf16[8,144,128]{2,1,0:T(8,128)(2,1)S(1)} collective-permute-done((bf16[8,144,128]{2,1,0:T(8,128)(2,1)S(1)}, bf16[8,144,128]{2,1,0:T(8,128)(2,1)S(1)}, u32[]{:S(2)}, u32[]{:S(2)}) %collective-permute-start.2) | collective-permute-done | bytes 294944 | tf_op jit(solution)/shard_map/ppermute | solution.py:398
  40.6 4.3 %all-to-all-done.1 = bf16[8,256,128]{2,1,0:T(8,128)(2,1)S(1)} async-done(((bf16[8,256,128]{2,1,0:T(8,128)(2,1)}), bf16[8,256,128]{2,1,0:T(8,128)(2,1)S(1)}, u32[]{:S(2)}, u32[]{:S(2)}) %all-to-all-start.1) | async-done | bytes 524320 | tf_op jit(solution)/shard_map/all_to_all | solution.py:429
  44.9 0.0 copy-done.2
  44.9 0.0 copy-done.3
  44.9 0.0 copy-start.1
  44.9 1.0 %copy-done.1 = bf16[8,144,128]{2,1,0:T(8,128)(2,1)S(1)} copy-done((bf16[8,144,128]{2,1,0:T(8,128)(2,1)S(1)}, bf16[8,144,128]{2,1,0:T(8,128)(2,1)}, u32[]{:S(2)}) %copy-start.1) | copy-done | bytes 294936
  45.9 4.7 %shard_map.85 = f32[32,16,128]{2,1,0:T(8,128)S(1)} custom-call(s32[2048]{0:T(1024)S(1)} %bitcast.10, bf16[2048,128]{1,0:T(8,128)(2,1)S(1)} %bitcast.8, f32[16,72,128]{2,1,0:T(8,128)S(1)} %copy-done.2, bf16[8,144,128]{2,1,0:T(8,128)(2,1)S(1)} %copy-done.1, bf16[8,144,128]{2,1,0:T(8,128)(2,1)S(1)} %collective-permute-done.refs_1_, ...), custom_call_target="tpu_custom_call" | custom-call | tf_op jit(solution)/shard_map/pallas_call | solution.py:348
  50.5 13.8 %all_to_all.15 = f32[32,16,128]{2,1,0:T(8,128)S(1)} all-to-all(f32[32,16,128]{2,1,0:T(8,128)S(1)} %shard_map.85), channel_id=1, replica_groups=mesh['groups'=2,'blk'=8,'sub'=2] {'groups','blk','sub'}, dimensions={0} | all-to-all | bytes 524288 | tf_op jit(solution)/shard_map/all_to_all | solution.py:437
  64.4 0.0 copy-done.5
  64.4 0.0 copy-done.4
  64.4 1.1 %shard_map.86 = f32[4,128]{1,0:T(4,128)} custom-call(s32[2,128]{1,0:T(2,128)S(1)} %bitcast.11, s32[4,128]{1,0:T(4,128)S(1)} %copy-done.4, f32[2,256,128]{2,1,0:T(8,128)S(1)} %bitcast.9), custom_call_target="tpu_custom_call" | custom-call | tf_op jit(solution)/shard_map/pallas_call | solution.py:389
Async XLA Ops:
  0.0 64.4 %copy-start.5 = (s32[256]{0:T(256)S(1)}, s32[256]{0:T(256)}, u32[]{:S(2)}) copy-start(s32[256]{0:T(256)} %param.10) | copy-start | bytes 3076
  0.0 64.4 %copy-start.4 = (s32[4,128]{1,0:T(4,128)S(1)}, s32[4,128]{1,0:T(4,128)}, u32[]{:S(2)}) copy-start(s32[4,128]{1,0:T(4,128)} %candidates_ref.1) | copy-start | bytes 6148
  2.3 16.9 %all-to-all-start = ((bf16[8,144,128]{2,1,0:T(8,128)(2,1)}), bf16[8,144,128]{2,1,0:T(8,128)(2,1)S(1)}, u32[]{:S(2)}, u32[]{:S(2)}) async-start(bf16[8,144,128]{2,1,0:T(8,128)(2,1)} %get-tuple-element.11), calls=%async_computation | async-start | bytes 589824 | tf_op jit(solution)/shard_map/all_to_all | solution.py:421
  14.7 30.2 %copy-start.2 = (f32[16,72,128]{2,1,0:T(8,128)S(1)}, f32[16,72,128]{2,1,0:T(8,128)}, u32[]{:S(2)}) copy-start(f32[16,72,128]{2,1,0:T(8,128)} %get-tuple-element.12.after_ref.residual_ref) | copy-start | bytes 1769476
  14.7 30.2 %copy-start.3 = (s32[16,128]{1,0:T(8,128)S(1)}, s32[16,128]{1,0:T(8,128)}, u32[]{:S(2)}) copy-start(s32[16,128]{1,0:T(8,128)} %get-tuple-element.10) | copy-start | bytes 24580
  19.2 0.7 %copy-start = (bf16[8,144,128]{2,1,0:T(8,128)(2,1)}, bf16[8,144,128]{2,1,0:T(8,128)(2,1)S(1)}, u32[]{:S(2)}) copy-start(bf16[8,144,128]{2,1,0:T(8,128)(2,1)S(1)} %all-to-all-done.received_ref.refs_0_) | copy-start | bytes 884740
  27.2 17.7 %all-to-all-start.1 = ((bf16[8,256,128]{2,1,0:T(8,128)(2,1)}), bf16[8,256,128]{2,1,0:T(8,128)(2,1)S(1)}, u32[]{:S(2)}, u32[]{:S(2)}) async-start(bf16[8,256,128]{2,1,0:T(8,128)(2,1)} %bitcast.12), calls=%async_computation.1 | async-start | bytes 1048576 | tf_op jit(solution)/shard_map/all_to_all | solution.py:429
  30.9 8.2 %collective-permute-start.1 = (bf16[8,144,128]{2,1,0:T(8,128)(2,1)}, bf16[8,144,128]{2,1,0:T(8,128)(2,1)S(1)}, u32[]{:S(2)}, u32[]{:S(2)}) collective-permute-start(bf16[8,144,128]{2,1,0:T(8,128)(2,1)} %copy-done), channel_id=1, source_target_pairs={{0,16},{16,0},{1,17},{17,1},{2,18},{18,2},{3,19},{19,3},{4,20},{20... | collective-permute-start | bytes 884744 | tf_op jit(solution)/shard_map/ppermute | solution.py:398
  32.4 6.7 %collective-permute-start = (bf16[8,144,128]{2,1,0:T(8,128)(2,1)}, bf16[8,144,128]{2,1,0:T(8,128)(2,1)S(1)}, u32[]{:S(2)}, u32[]{:S(2)}) collective-permute-start(bf16[8,144,128]{2,1,0:T(8,128)(2,1)} %copy-done), channel_id=1, source_target_pairs={{0,1},{1,0},{2,3},{3,2},{4,5},{5,4},{6,7},{7,6},{8,9},{9,8},{10,11... | collective-permute-start | bytes 884744 | tf_op jit(solution)/shard_map/ppermute | solution.py:398
  39.0 1.6 %collective-permute-start.2 = (bf16[8,144,128]{2,1,0:T(8,128)(2,1)S(1)}, bf16[8,144,128]{2,1,0:T(8,128)(2,1)S(1)}, u32[]{:S(2)}, u32[]{:S(2)}) collective-permute-start(bf16[8,144,128]{2,1,0:T(8,128)(2,1)S(1)} %collective-permute-done.1.refs_2_), channel_id=1, source_target_pairs={{0,1},{1,0},{2,3},{3,2},{4,5},{5,4},{6,7},{7,6},{8,9},{9,8},{10,11... | collective-permute-start | bytes 884744 | tf_op jit(solution)/shard_map/ppermute | solution.py:398
  44.9 1.0 %copy-start.1 = (bf16[8,144,128]{2,1,0:T(8,128)(2,1)S(1)}, bf16[8,144,128]{2,1,0:T(8,128)(2,1)}, u32[]{:S(2)}) copy-start(bf16[8,144,128]{2,1,0:T(8,128)(2,1)} %copy-done) | copy-start | bytes 884740

commit v4 on v3

--- a/solution.py
+++ b/solution.py
@@ -53,21 +53,26 @@
     for p in range(passages):
         limit = jnp.where(row == p, lengths_ref[p], limit)
     owner = jnp.where(lane < limit, owner, shards)
-    mask = jnp.concatenate([jnp.where(owner == b, 1.0, 0.0) for b in range(shards)], axis=0)
+    kind = 2 * owner + offset // (shard_rows // 2)
+    kinds = 2 * shards
+    mask = jnp.concatenate([jnp.where(kind == b, 1.0, 0.0) for b in range(kinds)], axis=0)
     mask16 = mask.astype(BF16)
     k = lax.broadcasted_iota(I32, (height, height), 0)
     l = lax.broadcasted_iota(I32, (height, height), 1)
     inside = dot_nn(mask16, jnp.where(k < l, 1.0, 0.0).astype(BF16))
     totals = dot_nn(mask16, jnp.ones((height, height), BF16))
-    full = shards * passages
+    full = kinds * passages
     r = lax.broadcasted_iota(I32, (full, full), 0)
     c = lax.broadcasted_iota(I32, (full, full), 1)
-    same = r // passages == c // passages
+    same = r // (2 * passages) == c // (2 * passages)
     ahead = dot_nn(jnp.where(same & (c < r), 1.0, 0.0).astype(BF16), totals.astype(BF16))
     place = (inside + ahead) * mask
     rank = jnp.zeros((passages, height), F32)
-    for b in range(shards):
+    sizes = []
+    for b in range(kinds):
         rank = rank + place[b * passages : (b + 1) * passages]
+        size = jnp.sum(totals[b * passages : (b + 1) * passages], axis=0, keepdims=True)
+        sizes.append(size.astype(I32))
     rank = rank.astype(I32)
     mine = (lane < limit) & (rank % parts == part)
     rank = rank // parts
@@ -91,15 +96,16 @@
     queries = queries_ref[...]
     extra = message_rows(cap, height)
     for b in range(shards):
-        total = jnp.sum(totals[b * passages : (b + 1) * passages], axis=0, keepdims=True)
-        share = (total.astype(I32) + (parts - 1 - part)) // parts
+        share = (sizes[2 * b] + sizes[2 * b + 1] + (parts - 1 - part)) // parts
+        first = (sizes[2 * b] + (parts - 1 - part)) // parts
         sent_ref[b, :span] = queries
         sent_ref[b, span:] = jnp.concatenate(
             [
                 sums[b * per : (b + 1) * per, :height],
                 sums[b * per : (b + 1) * per, height:],
                 share.astype(F32),
-                jnp.zeros((extra - 2 * per - 1, height), F32),
+                first.astype(F32),
+                jnp.zeros((extra - 2 * per - 2, height), F32),
             ],
             axis=0,
         ).astype(BF16)
@@ -110,7 +116,7 @@
 
 
 def message_rows(cap, lanes):
-    return (2 * list_rows(cap, lanes) + TILE) // TILE * TILE
+    return (2 * list_rows(cap, lanes) + 1 + TILE) // TILE * TILE
 
 
 def plan(lengths, ids, queries, shards, shard_rows, cap, parts):
@@ -135,11 +141,14 @@
 
 
 def block_rows(height, shards, parts):
-    most = min(height, (height + shards * (parts - 1)) // parts)
+    most = min(height, (height + 2 * shards * (parts - 1)) // parts)
     return (most + 7) // 8 * 8
 
 
-def prepare_kernel(pos_ref, codes_ref, buckets_ref, list_ref, residual_ref, flat, picked, sems):
+def prepare_kernel(
+    pos_ref, codes_ref, buckets_ref, location_ref, candidates_ref,
+    list_ref, residual_ref, slots_ref, flat, picked, sems,
+):
     passages, height = pos_ref.shape
     block, width = residual_ref.shape[1:]
     pos = pos_ref[...]
@@ -193,101 +202,147 @@
             ),
         )
 
-
-def prepare(pos, codes, buckets, block):
+    owned, listed = candidates_ref.shape
+    blocks, width = location_ref.shape
+    which = lax.broadcasted_iota(I32, (width, listed), 0)
+    for q in range(owned):
+        named = candidates_ref[q : q + 1]
+        found = jnp.zeros((2, listed), F32)
+        for g in range(blocks):
+            here = location_ref[g : g + 1]
+            pair = jnp.concatenate([here // 256, here % 256], axis=0).astype(F32).astype(BF16)
+            hit = jnp.where(which + g * width == named, 1.0, 0.0).astype(BF16)
+            found = found + dot_nn(pair, hit)
+        slots_ref[q : q + 1] = (found[0:1] * 256.0 + found[1:2]).astype(I32)
+
+
+def prepare(pos, codes, buckets, location, candidates, block):
     passages, height, width = codes.shape
     return pl.pallas_call(
         prepare_kernel,
         out_shape=(
             jax.ShapeDtypeStruct((passages, height), I32),
             jax.ShapeDtypeStruct((passages, block, width), F32),
+            jax.ShapeDtypeStruct(candidates.shape, I32),
         ),
-        in_specs=[VMEM, VMEM, VMEM],
-        out_specs=(VMEM, VMEM),
+        in_specs=[VMEM] * 5,
+        out_specs=(VMEM, VMEM, VMEM),
         scratch_shapes=[
             pltpu.SMEM((passages * height,), I32),
             pltpu.VMEM((block + UNROLL, width), I32),
             pltpu.SemaphoreType.DMA((passages,)),
         ],
         compiler_params=pltpu.CompilerParams(vmem_limit_bytes=56 * MIB),
-    )(pos, codes, buckets)
+    )(pos, codes, buckets, location, candidates)
 
 
 def fetch_kernel(
-    span, shard_rows, cap, received_ref, table_hbm, after_ref, out_ref, table_ref, ask, asked, stage, sems, sem
+    span, cap, received_hbm, table_hbm, after_ref, out_ref,
+    front, back, message, ask, asked, even, odd, load_sems, sems, sem,
 ):
-    shards = received_ref.shape[0]
-    height = received_ref.shape[2]
-    width = table_ref.shape[1]
+    shards, _, height = received_hbm.shape
+    half_tiles, _, width = front.shape
     per = list_rows(cap, height)
-    load = pltpu.make_async_copy(table_hbm, table_ref, sem)
-    load.start()
-    copies = []
+    rows = shards * per
+    receive = pltpu.make_async_copy(
+        received_hbm.at[:, pl.ds(span, message.shape[1])], message, sem
+    )
+    receive.start()
+    loads = [
+        pltpu.make_async_copy(table_hbm.at[pl.ds(h * half_tiles, half_tiles)], table, load_sems.at[h])
+        for h, table in enumerate((front, back))
+    ]
+    loads[0].start()
+    receive.wait()
+    lane = lax.broadcasted_iota(I32, (1, height), 1)
+    sizes = jnp.zeros((1, height), F32)
     for d in range(shards):
-        message = received_ref[d, span:].astype(F32)
-        count = message[2 * per : 2 * per + 1].astype(I32)
-        offset = (message[:per] * 256.0 + message[per : 2 * per]).astype(I32)
-        ask[d * per : (d + 1) * per] = offset + count * shard_rows
-    for r in range(shards * per):
-        copies.append(
-            pltpu.make_async_copy(ask.at[r], asked.at[pl.ds(r * height, height)], sems.at[r])
-        )
+        lists = message[d].astype(F32)
+        sizes = jnp.where(lane == d, lists[2 * per : 2 * per + 1], sizes)
+        sizes = jnp.where(lane == d + shards, lists[2 * per + 1 : 2 * per + 2], sizes)
+        offset = (lists[:per] * 256.0 + lists[per : 2 * per]).astype(I32)
+        ask[d * per : (d + 1) * per] = (offset // TILE) & (half_tiles - 1)
+        ask[rows + d * per : rows + (d + 1) * per] = offset & (TILE - 1)
+    ask[2 * rows : 2 * rows + 1] = sizes.astype(I32)
+    copies = [
+        pltpu.make_async_copy(ask.at[r], asked.at[pl.ds(r * height, height)], sems.at[r])
+        for r in range(2 * rows + 1)
+    ]
     for copy in copies:
         copy.start()
     for copy in copies:
         copy.wait()
+    loads[1].start()
     line = lax.broadcasted_iota(I32, (8, width), 0)
-    low_bits = TILE - 1
-    near_bits = shard_rows - TILE
-    load.wait()
-
-    @pl.loop(0, shards)
-    def _(d):
-        base = d * (per * height)
-        count = asked[base] // shard_rows
-
-        @pl.loop(0, (count + TILE - 1) // TILE)
-        def _(i):
-            at = pl.multiple_of(base + i * TILE, TILE)
-            for u in range(TILE):
-                near = pl.multiple_of(asked[at + u] & near_bits, TILE)
-                stage[u * TILE : (u + 1) * TILE] = table_ref[pl.ds(near, TILE)].astype(F32)
-            halves = []
-            for h in range(0, TILE, 8):
-                half = jnp.zeros((8, width), F32)
-                for u in range(h, h + 8):
-                    row = stage[pl.ds(u * TILE + (asked[at + u] & low_bits), 1)]
-                    half = jnp.where(line == u - h, row, half)
-                halves.append(half)
-            to = pl.multiple_of(d * cap + i * TILE, TILE)
-            out_ref[pl.ds(to, TILE)] = jnp.concatenate(halves, axis=0).astype(BF16)
+
+    for h, table in enumerate((front, back)):
+        loads[h].wait()
+
+        @pl.loop(0, shards)
+        def _(d):
+            base = d * (per * height)
+            count = asked[2 * rows * height + d]
+            first = asked[2 * rows * height + shards + d]
+            begin = 0 if h == 0 else first // TILE
+            end = ((first if h == 0 else count) + TILE - 1) // TILE
+
+            @pl.loop(begin, end)
+            def _(i):
+                at = pl.multiple_of(base + i * TILE, TILE)
+                low_at = pl.multiple_of(at + rows * height, TILE)
+                to = pl.multiple_of(d * cap + i * TILE, TILE)
+                stages = (even, odd)
+                for g, stage in enumerate(stages):
+                    for u in range(8):
+                        stage[u * TILE : (u + 1) * TILE] = table[asked[at + 8 * g + u]].astype(F32)
+                if h == 0:
+                    halves = [jnp.zeros((8, width), F32)] * 2
+                else:
+                    old = out_ref[pl.ds(to, TILE)].astype(F32)
+                    halves = [old[:8], old[8:]]
+                for g, stage in enumerate(stages):
+                    for u in range(8):
+                        row = stage[pl.ds(u * TILE + asked[low_at + 8 * g + u], 1)]
+                        here = line == u
+                        if h == 1:
+                            here = here & (line + (i * TILE + 8 * g) >= first)
+                        halves[g] = jnp.where(here, row, halves[g])
+                out_ref[pl.ds(to, TILE)] = jnp.concatenate(halves, axis=0).astype(BF16)
 
 
 def fetch(received, table, after, span, cap):
     shard_rows, width = table.shape
-    shards, _, height = received.shape
+    shards, length, height = received.shape
     rows = shards * list_rows(cap, height)
     assert shard_rows & (shard_rows - 1) == 0
+    half = (shard_rows // TILE // 2, TILE, width)
+    ask_rows = (2 * rows + 8) // 8 * 8
     return pl.pallas_call(
-        functools.partial(fetch_kernel, span, shard_rows, cap),
+        functools.partial(fetch_kernel, span, cap),
         out_shape=jax.ShapeDtypeStruct((shards * cap, width), BF16),
-        in_specs=[VMEM, HBM, HBM],
+        in_specs=[HBM, HBM, HBM],
         out_specs=VMEM,
         scratch_shapes=[
-            pltpu.VMEM(table.shape, table.dtype),
-            pltpu.VMEM((rows, height), I32),
-            pltpu.SMEM((rows * height,), I32),
-            pltpu.VMEM((TILE * TILE, width), F32),
-            pltpu.SemaphoreType.DMA((rows,)),
+            pltpu.VMEM(half, table.dtype),
+            pltpu.VMEM(half, table.dtype),
+            pltpu.VMEM((shards, length - span, height), BF16),
+            pltpu.VMEM((ask_rows, height), I32),
+            pltpu.SMEM((ask_rows * height,), I32),
+            pltpu.VMEM((8 * TILE, width), F32),
+            pltpu.VMEM((8 * TILE, width), F32),
+            pltpu.SemaphoreType.DMA((2,)),
+            pltpu.SemaphoreType.DMA((2 * rows + 1,)),
             pltpu.SemaphoreType.DMA,
         ],
         compiler_params=pltpu.CompilerParams(vmem_limit_bytes=56 * MIB),
-    )(received, table, after)
-
-
-def score_kernel(span, list_ref, replies_ref, residual_ref, *refs):
-    passages, block, width = residual_ref.shape
-    *query_refs, out_ref, wide, tile, embedded = refs
+    )(received, table.reshape(shard_rows // TILE, TILE, width), after)
+
+
+def score_kernel(span, list_ref, replies_ref, residual_hbm, *refs):
+    passages, block, width = residual_hbm.shape
+    *query_refs, out_ref, wide, tile, embedded, residual_ref, sem = refs
+    load = pltpu.make_async_copy(residual_hbm, residual_ref, sem)
+    load.start()
     groups, subs = lax.axis_size("groups"), lax.axis_size("sub")
     own_group, own_sub = lax.axis_index("groups"), lax.axis_index("sub")
     shards = query_refs[0].shape[0]
@@ -311,6 +366,7 @@
                 place = list_ref[p * height + at + u] & ((1 << TOKEN_AT) - 1)
                 tile[pl.ds(p * block + at + u, 1)] = wide[pl.ds(place, 1)]
 
+    load.wait()
     line = lax.broadcasted_iota(I32, (block, width), 0)
     here = lax.broadcasted_iota(I32, (passages, pair * span), 0)
     counts = jnp.zeros((passages, pair * span), I32)
@@ -348,22 +404,22 @@
     return pl.pallas_call(
         functools.partial(score_kernel, span),
         out_shape=jax.ShapeDtypeStruct((devices, passages, span), F32),
-        in_specs=[SMEM, VMEM, VMEM] + [VMEM] * len(queries),
+        in_specs=[SMEM, VMEM, HBM] + [VMEM] * len(queries),
         out_specs=VMEM,
         scratch_shapes=[
             pltpu.VMEM((replies.shape[0], width), F32),
             pltpu.VMEM((passages * block + UNROLL, width), F32),
             pltpu.VMEM((passages * block, width), BF16),
+            pltpu.VMEM((passages, block, width), F32),
+            pltpu.SemaphoreType.DMA,
         ],
         compiler_params=pltpu.CompilerParams(vmem_limit_bytes=24 * MIB),
     )(lists, replies, residuals, *queries)
 
 
-def pick_kernel(tokens, location_ref, candidates_ref, best_ref, out_ref):
-    owned, listed = candidates_ref.shape
+def pick_kernel(tokens, slots_ref, best_ref, out_ref):
+    owned, listed = slots_ref.shape
     parts, slots_total, span = best_ref.shape
-    blocks, width = location_ref.shape
-    which = lax.broadcasted_iota(I32, (width, listed), 0)
     slot = lax.broadcasted_iota(I32, (slots_total, listed), 0)
     sums = best_ref[0]
     for g in range(1, parts):
@@ -373,24 +429,17 @@
         sums = sums + pltpu.roll(sums, span - shift, 1)
         shift //= 2
     for q in range(owned):
-        named = candidates_ref[q : q + 1]
-        found = jnp.zeros((2, listed), F32)
-        for g in range(blocks):
-            here = location_ref[g : g + 1]
-            pair = jnp.concatenate([here // 256, here % 256], axis=0).astype(F32).astype(BF16)
-            hit = jnp.where(which + g * width == named, 1.0, 0.0).astype(BF16)
-            found = found + dot_nn(pair, hit)
-        slots = (found[0:1] * 256.0 + found[1:2]).astype(I32)
         column = jnp.broadcast_to(sums[:, q * tokens : q * tokens + 1], (slots_total, listed))
-        out_ref[q : q + 1] = jnp.sum(jnp.where(slot == slots, column, 0.0), axis=0, keepdims=True)
-
-
-def pick(location, candidates, best, tokens):
+        chosen = jnp.where(slot == slots_ref[q : q + 1], column, 0.0)
+        out_ref[q : q + 1] = jnp.sum(chosen, axis=0, keepdims=True)
+
+
+def pick(slots, best, tokens):
     return pl.pallas_call(
         functools.partial(pick_kernel, tokens),
-        out_shape=jax.ShapeDtypeStruct(candidates.shape, F32),
+        out_shape=jax.ShapeDtypeStruct(slots.shape, F32),
         compiler_params=pltpu.CompilerParams(vmem_limit_bytes=16 * MIB),
-    )(location, candidates, best)
+    )(slots, best)
 
 
 def turned(array, axis, shift):
@@ -419,28 +468,27 @@
         parts,
     )
     near = lax.all_to_all(sent, "blk", split_axis=0, concat_axis=0, tiled=True)
-    lists, residuals = prepare(
+    lists, residuals, slots = prepare(
         pos,
         residual_codes.reshape(passages, height, width),
         buckets,
+        location.reshape(location.shape[0] // 128, 128),
+        candidates,
         block_rows(height, shards, parts),
     )
-    found = fetch(near, centroids, residuals, span, cap)
+    found = fetch(near, centroids, slots, span, cap)
     replies = lax.all_to_all(
         found.reshape(shards, cap, width), "blk", split_axis=0, concat_axis=0, tiled=True
     )
     across = [near] + [turned(near, "groups", g) for g in range(1, parts)]
     spread = []
     for array in across:
-        spread += [array] + [turned(array, "sub", s) for s in range(1, subs)]
+        others = [turned(array, "sub", s) for s in range(1, subs)]
+        own = turned(others[-1], "sub", 1) if array is near and others else array
+        spread += [own] + others
     best = score(lists.reshape(token_count), replies.reshape(shards * cap, width), residuals, spread, span)
     mine = lax.all_to_all(best, ("groups", "blk", "sub"), split_axis=0, concat_axis=0, tiled=True)
-    return pick(
-        location.reshape(location.shape[0] // 128, 128),
-        candidates,
-        mine.reshape(parts, shards * subs * passages, span),
-        tokens,
-    )
+    return pick(slots, mine.reshape(parts, shards * subs * passages, span), tokens)
 
 
 def solution(mesh):

time: 66.2 us -> 64.1 us (0.968)
  Pallas kernels: 20.4 us -> 19.4 us
  local copies, waits for them, and re-layouts: 1.7 us -> 0.75 us
    all_to_all x1, waiting for transfers between devices: 4.27 us -> 2.72 us  [body(): lax.all_to_all(found.reshape(shards, cap, width), 'blk', split_axis=0, co...]
    ppermute x3 -> x4, waiting for transfers between devices: 8.24 us -> 9.47 us  [turned(): lax.ppermute(array, axis, [(i, (i + shift) % size) for i in range(size)])]
    pallas_call x1, Pallas kernels: 7.29 us -> 6.2 us  [fetch(): pl.pallas_call(functools.partial(fetch_kernel, span, cap), out_shape=jax....]
    unnamed x12 -> x8, local copies, waits for them, and re-layouts: 1.7 us -> 0.75 us
    ppermute x3 -> x4, starting transfers between devices: 1.5 us -> 1.74 us  [turned(): lax.ppermute(array, axis, [(i, (i + shift) % size) for i in range(size)])]
  transfers between devices with their start and end apart: 5 -> 6, of which waited for: 4 -> 5; matrix products, arithmetic and copies ran while one was open for 0% -> 0% of each run, Pallas kernels for 8% -> 8%
where the time goes in v4:
time: 64.1 us; the launch traced here: 63.5 us
  Pallas kernels  19.4 us (30%)
  waiting for transfers between devices  16.8 us (26%)
  blocking collectives  13.7 us (21%)
  starting transfers between devices  12.8 us (20%)
  local copies, waits for them, and re-layouts  0.75 us (1%)
    all_to_all x1, blocking collectives, body(): lax.all_to_all(best, ('groups', 'blk', 'sub'), split_axis=0, concat_axis=...  13.7 us
    ppermute x4, waiting for transfers between devices, turned(): lax.ppermute(array, axis, [(i, (i + shift) % size) for i in range(size)])  9.47 us
    all_to_all x1, starting transfers between devices, body(): near = lax.all_to_all(sent, 'blk', split_axis=0, concat_axis=0, tiled=True)  7.3 us
    pallas_call x1, Pallas kernels, fetch(): pl.pallas_call(functools.partial(fetch_kernel, span, cap), out_shape=jax....  6.2 us
    pallas_call x1, Pallas kernels, prepare(): pl.pallas_call(prepare_kernel, out_shape=(jax.ShapeDtypeStruct((passages,...  5.01 us
    pallas_call x1, Pallas kernels, score(): pl.pallas_call(functools.partial(score_kernel, span), out_shape=jax.Shape...  4.73 us
    all_to_all x1, waiting for transfers between devices, body(): near = lax.all_to_all(sent, 'blk', split_axis=0, concat_axis=0, tiled=True)  4.57 us
    all_to_all x1, starting transfers between devices, body(): lax.all_to_all(found.reshape(shards, cap, width), 'blk', split_axis=0, co...  3.76 us
  transfers between devices with their start and end apart: 6, of which 5 were waited for; matrix products, arithmetic and copies ran while one was open for 0% of the time, Pallas kernels for 8%

profile of v4, /device:TPU:0, one launch (start us, length us, event | category | flops | bytes accessed | tf_op | source)
XLA Modules:
  0.0 63.5 jit_solution(8798737678224678314)
XLA Ops:
  0.0 2.3 %shard_map.82 = (bf16[8,144,128]{2,1,0:T(8,128)(2,1)}, s32[16,128]{1,0:T(8,128)}) custom-call(s32[16]{0:T(128)} %lengths_hbm.1, s32[16,128]{1,0:T(8,128)} %bitcast.16, bf16[128,128]{1,0:T(8,128)(2,1)} %bitcast.15), custom_call_target="tpu_custom_call" | custom-call | tf_op jit(solution)/shard_map/pallas_call | solution.py:125
  2.3 7.3 %all-to-all-start = ((bf16[8,144,128]{2,1,0:T(8,128)(2,1)}), bf16[8,144,128]{2,1,0:T(8,128)(2,1)S(1)}, u32[]{:S(2)}, u32[]{:S(2)}) async-start(bf16[8,144,128]{2,1,0:T(8,128)(2,1)} %get-tuple-element.13), calls=%async_computation | async-start | bytes 589824 | tf_op jit(solution)/shard_map/all_to_all | solution.py:470
  9.6 5.0 %shard_map.83 = (s32[16,128]{1,0:T(8,128)}, f32[16,72,128]{2,1,0:T(8,128)}, s32[4,128]{1,0:T(4,128)}) custom-call(s32[16,128]{1,0:T(8,128)} %get-tuple-element.10.pos_ref, s32[16,128,128]{2,1,0:T(8,128)} %bitcast.14, f32[4,128]{1,0:T(4,128)} %buckets_ref.1, s32[2,128]{1,0:T(2,128)} %bitcast.17, s32[4,128]{1,0:T(4,128)} %candidates_ref.1), custom_call_target="tpu_custom_call" | custom-call | tf_op jit(solution)/shard_map/pallas_call | solution.py:221
  14.6 0.0 copy-start
  14.6 0.0 copy-start.1
  14.6 0.0 copy-start.2
  14.7 4.6 %all-to-all-done.received_hbm = bf16[8,144,128]{2,1,0:T(8,128)(2,1)S(1)} async-done(((bf16[8,144,128]{2,1,0:T(8,128)(2,1)}), bf16[8,144,128]{2,1,0:T(8,128)(2,1)S(1)}, u32[]{:S(2)}, u32[]{:S(2)}) %all-to-all-start) | async-done | bytes 294944 | tf_op jit(solution)/shard_map/all_to_all | solution.py:470
  19.2 0.0 copy-start.3
  19.2 0.7 %copy-done.3 = bf16[8,144,128]{2,1,0:T(8,128)(2,1)} copy-done((bf16[8,144,128]{2,1,0:T(8,128)(2,1)}, bf16[8,144,128]{2,1,0:T(8,128)(2,1)S(1)}, u32[]{:S(2)}) %copy-start.3) | copy-done | bytes 294936
  20.0 6.2 %shard_map.84 = bf16[2048,128]{1,0:T(8,128)(2,1)} custom-call(bf16[8,144,128]{2,1,0:T(8,128)(2,1)} %copy-done.3, bf16[2048,16,128]{2,1,0:T(8,128)(2,1)} %bitcast.12, s32[4,128]{1,0:T(4,128)} %get-tuple-element.11.after_ref.slots_ref), custom_call_target="tpu_custom_call" | custom-call | tf_op jit(solution)/shard_map/pallas_call | solution.py:320
  26.2 3.8 %all-to-all-start.1 = ((bf16[8,256,128]{2,1,0:T(8,128)(2,1)}), bf16[8,256,128]{2,1,0:T(8,128)(2,1)S(1)}, u32[]{:S(2)}, u32[]{:S(2)}) async-start(bf16[8,256,128]{2,1,0:T(8,128)(2,1)} %bitcast.13), calls=%async_computation.1 | async-start | bytes 1048576 | tf_op jit(solution)/shard_map/all_to_all | solution.py:480
  29.9 0.0 collective-permute-start
  29.9 1.6 %collective-permute-start.2 = (bf16[8,144,128]{2,1,0:T(8,128)(2,1)}, bf16[8,144,128]{2,1,0:T(8,128)(2,1)S(1)}, u32[]{:S(2)}, u32[]{:S(2)}) collective-permute-start(bf16[8,144,128]{2,1,0:T(8,128)(2,1)} %copy-done.3), channel_id=1, source_target_pairs={{0,16},{16,0},{1,17},{17,1},{2,18},{18,2},{3,19},{19,3},{4,20},{20... | collective-permute-start | bytes 884744 | tf_op jit(solution)/shard_map/ppermute | solution.py:447
  31.5 0.2 collective-permute-done.refs_1_
  31.7 0.1 collective-permute-start.1
  31.9 7.7 %collective-permute-done.2.refs_2_ = bf16[8,144,128]{2,1,0:T(8,128)(2,1)S(1)} collective-permute-done((bf16[8,144,128]{2,1,0:T(8,128)(2,1)}, bf16[8,144,128]{2,1,0:T(8,128)(2,1)S(1)}, u32[]{:S(2)}, u32[]{:S(2)}) %collective-permute-start.2) | collective-permute-done | bytes 294944 | tf_op jit(solution)/shard_map/ppermute | solution.py:447
  39.6 0.0 collective-permute-start.3
  39.6 0.0 collective-permute-done.1.refs_0_
  39.6 1.6 %collective-permute-done.3.refs_3_ = bf16[8,144,128]{2,1,0:T(8,128)(2,1)S(1)} collective-permute-done((bf16[8,144,128]{2,1,0:T(8,128)(2,1)S(1)}, bf16[8,144,128]{2,1,0:T(8,128)(2,1)S(1)}, u32[]{:S(2)}, u32[]{:S(2)}) %collective-permute-start.3) | collective-permute-done | bytes 294944 | tf_op jit(solution)/shard_map/ppermute | solution.py:447
  41.1 2.7 %all-to-all-done.1 = bf16[8,256,128]{2,1,0:T(8,128)(2,1)S(1)} async-done(((bf16[8,256,128]{2,1,0:T(8,128)(2,1)}), bf16[8,256,128]{2,1,0:T(8,128)(2,1)S(1)}, u32[]{:S(2)}, u32[]{:S(2)}) %all-to-all-start.1) | async-done | bytes 524320 | tf_op jit(solution)/shard_map/all_to_all | solution.py:480
  43.9 0.0 copy-done
  43.9 0.0 copy-done.1
  43.9 4.7 %shard_map.85 = f32[32,16,128]{2,1,0:T(8,128)S(1)} custom-call(s32[2048]{0:T(1024)S(1)} %bitcast.11, bf16[2048,128]{1,0:T(8,128)(2,1)S(1)} %bitcast.9, f32[16,72,128]{2,1,0:T(8,128)S(1)} %copy-done, bf16[8,144,128]{2,1,0:T(8,128)(2,1)S(1)} %collective-permute-done.1.refs_0_, bf16[8,144,128]{2,1,0:T(8,128)(2,1)S(1)} %collective-permute-done.refs_1_, ...), custom_call_target="tpu_custom_call" | custom-call | tf_op jit(solution)/shard_map/pallas_call | solution.py:404
  48.6 13.7 %all_to_all.15 = f32[32,16,128]{2,1,0:T(8,128)S(1)} all-to-all(f32[32,16,128]{2,1,0:T(8,128)S(1)} %shard_map.85), channel_id=1, replica_groups=mesh['groups'=2,'blk'=8,'sub'=2] {'groups','blk','sub'}, dimensions={0} | all-to-all | bytes 524288 | tf_op jit(solution)/shard_map/all_to_all | solution.py:490
  62.4 0.0 copy-done.2
  62.4 1.1 %shard_map.86 = f32[4,128]{1,0:T(4,128)} custom-call(s32[4,128]{1,0:T(4,128)S(1)} %copy-done.2, f32[2,256,128]{2,1,0:T(8,128)S(1)} %bitcast.10), custom_call_target="tpu_custom_call" | custom-call | tf_op jit(solution)/shard_map/pallas_call | solution.py:438
Async XLA Ops:
  2.3 16.9 %all-to-all-start = ((bf16[8,144,128]{2,1,0:T(8,128)(2,1)}), bf16[8,144,128]{2,1,0:T(8,128)(2,1)S(1)}, u32[]{:S(2)}, u32[]{:S(2)}) async-start(bf16[8,144,128]{2,1,0:T(8,128)(2,1)} %get-tuple-element.13), calls=%async_computation | async-start | bytes 589824 | tf_op jit(solution)/shard_map/all_to_all | solution.py:470
  14.6 29.2 %copy-start = (f32[16,72,128]{2,1,0:T(8,128)S(1)}, f32[16,72,128]{2,1,0:T(8,128)}, u32[]{:S(2)}) copy-start(f32[16,72,128]{2,1,0:T(8,128)} %get-tuple-element.14.residual_hbm) | copy-start | bytes 1769476
  14.6 29.2 %copy-start.1 = (s32[16,128]{1,0:T(8,128)S(1)}, s32[16,128]{1,0:T(8,128)}, u32[]{:S(2)}) copy-start(s32[16,128]{1,0:T(8,128)} %get-tuple-element.12) | copy-start | bytes 24580
  14.6 47.7 %copy-start.2 = (s32[4,128]{1,0:T(4,128)S(1)}, s32[4,128]{1,0:T(4,128)}, u32[]{:S(2)}) copy-start(s32[4,128]{1,0:T(4,128)} %get-tuple-element.11.after_ref.slots_ref) | copy-start | bytes 6148
  19.2 0.7 %copy-start.3 = (bf16[8,144,128]{2,1,0:T(8,128)(2,1)}, bf16[8,144,128]{2,1,0:T(8,128)(2,1)S(1)}, u32[]{:S(2)}) copy-start(bf16[8,144,128]{2,1,0:T(8,128)(2,1)S(1)} %all-to-all-done.received_hbm) | copy-start | bytes 884740
  26.2 17.7 %all-to-all-start.1 = ((bf16[8,256,128]{2,1,0:T(8,128)(2,1)}), bf16[8,256,128]{2,1,0:T(8,128)(2,1)S(1)}, u32[]{:S(2)}, u32[]{:S(2)}) async-start(bf16[8,256,128]{2,1,0:T(8,128)(2,1)} %bitcast.13), calls=%async_computation.1 | async-start | bytes 1048576 | tf_op jit(solution)/shard_map/all_to_all | solution.py:480
  29.9 1.8 %collective-permute-start = (bf16[8,144,128]{2,1,0:T(8,128)(2,1)}, bf16[8,144,128]{2,1,0:T(8,128)(2,1)S(1)}, u32[]{:S(2)}, u32[]{:S(2)}) collective-permute-start(bf16[8,144,128]{2,1,0:T(8,128)(2,1)} %copy-done.3), channel_id=1, source_target_pairs={{0,1},{1,0},{2,3},{3,2},{4,5},{5,4},{6,7},{7,6},{8,9},{9,8},{10,11... | collective-permute-start | bytes 884744 | tf_op jit(solution)/shard_map/ppermute | solution.py:447
  29.9 9.6 %collective-permute-start.2 = (bf16[8,144,128]{2,1,0:T(8,128)(2,1)}, bf16[8,144,128]{2,1,0:T(8,128)(2,1)S(1)}, u32[]{:S(2)}, u32[]{:S(2)}) collective-permute-start(bf16[8,144,128]{2,1,0:T(8,128)(2,1)} %copy-done.3), channel_id=1, source_target_pairs={{0,16},{16,0},{1,17},{17,1},{2,18},{18,2},{3,19},{19,3},{4,20},{20... | collective-permute-start | bytes 884744 | tf_op jit(solution)/shard_map/ppermute | solution.py:447
  31.7 7.8 %collective-permute-start.1 = (bf16[8,144,128]{2,1,0:T(8,128)(2,1)S(1)}, bf16[8,144,128]{2,1,0:T(8,128)(2,1)S(1)}, u32[]{:S(2)}, u32[]{:S(2)}) collective-permute-start(bf16[8,144,128]{2,1,0:T(8,128)(2,1)S(1)} %collective-permute-done.refs_1_), channel_id=1, source_target_pairs={{0,1},{1,0},{2,3},{3,2},{4,5},{5,4},{6,7},{7,6},{8,9},{9,8},{10,11... | collective-permute-start | bytes 884744 | tf_op jit(solution)/shard_map/ppermute | solution.py:447
  39.6 1.6 %collective-permute-start.3 = (bf16[8,144,128]{2,1,0:T(8,128)(2,1)S(1)}, bf16[8,144,128]{2,1,0:T(8,128)(2,1)S(1)}, u32[]{:S(2)}, u32[]{:S(2)}) collective-permute-start(bf16[8,144,128]{2,1,0:T(8,128)(2,1)S(1)} %collective-permute-done.2.refs_2_), channel_id=1, source_target_pairs={{0,1},{1,0},{2,3},{3,2},{4,5},{5,4},{6,7},{7,6},{8,9},{9,8},{10,11... | collective-permute-start | bytes 884744 | tf_op jit(solution)/shard_map/ppermute | solution.py:447

commit v5 on v4

--- a/solution.py
+++ b/solution.py
@@ -13,8 +13,6 @@
 MIB = 1 << 20
 UNROLL = 16
 TILE = 16
-TOKEN_AT = 12
-COUNT_AT = 20
 SMEM = pl.BlockSpec(memory_space=pltpu.SMEM)
 VMEM = pl.BlockSpec(memory_space=pltpu.VMEM)
 HBM = pl.BlockSpec(memory_space=pl.ANY)
@@ -39,7 +37,7 @@
     ]
     for copy in copies:
         copy.start()
-    for copy in copies:
+    for copy in copies[:2]:
         copy.wait()
     passages, height = ids_ref.shape
     span = queries_ref.shape[0]
@@ -93,6 +91,7 @@
             [jnp.where(hit, high[p : p + 1], 0.0), jnp.where(hit, low[p : p + 1], 0.0)], axis=0
         ).astype(BF16)
         sums = sums + dot_nt(here, values)
+    copies[2].wait()
     queries = queries_ref[...]
     extra = message_rows(cap, height)
     for b in range(shards):
@@ -147,7 +146,7 @@
 
 def prepare_kernel(
     pos_ref, codes_ref, buckets_ref, location_ref, candidates_ref,
-    list_ref, residual_ref, slots_ref, flat, picked, sems,
+    list_ref, residual_ref, slots_ref, tokens, flat, picked, sems,
 ):
     passages, height = pos_ref.shape
     block, width = residual_ref.shape[1:]
@@ -161,19 +160,20 @@
     high = (pos // 256).astype(F32)
     low = (pos % 256).astype(F32)
     token = lax.broadcasted_iota(I32, (1, height), 1).astype(F32)
+    lane = lax.broadcasted_iota(I32, (1, height), 1)
+    counts = jnp.zeros((1, height), I32)
     for p in range(passages):
         hit = jnp.where(k == rank[p : p + 1], 1.0, 0.0).astype(BF16)
         values = jnp.concatenate([high[p : p + 1], low[p : p + 1], token], axis=0).astype(BF16)
         found = dot_nt(values, hit).astype(I32)
-        list_ref[p : p + 1] = (
-            found[0:1] * 256
-            + found[1:2]
-            + found[2:3] * (1 << TOKEN_AT)
-            + total[p : p + 1] * (1 << COUNT_AT)
-        )
+        list_ref[p : p + 1] = found[0:1] * 256 + found[1:2]
+        tokens[p : p + 1] = found[2:3]
+        counts = jnp.where(lane == p, total[p : p + 1], counts)
+    list_ref[passages : passages + 1] = counts
+    tokens[passages : passages + 1] = counts
     copies = [
-        pltpu.make_async_copy(list_ref.at[p], flat.at[pl.ds(p * height, height)], sems.at[p])
-        for p in range(passages)
+        pltpu.make_async_copy(tokens.at[p], flat.at[pl.ds(p * height, height)], sems.at[p])
+        for p in range(passages + 1)
     ]
     for copy in copies:
         copy.start()
@@ -182,14 +182,13 @@
 
     @pl.loop(0, passages)
     def _(p):
-        count = flat[p * height] >> COUNT_AT
+        count = flat[passages * height + p]
 
         @pl.loop(0, (count + UNROLL - 1) // UNROLL)
         def _(i):
             at = pl.multiple_of(i * UNROLL, UNROLL)
             for u in range(UNROLL):
-                token = (flat[p * height + at + u] >> TOKEN_AT) & ((1 << COUNT_AT - TOKEN_AT) - 1)
-                picked[pl.ds(at + u, 1)] = codes_ref[p, pl.ds(token, 1)]
+                picked[pl.ds(at + u, 1)] = codes_ref[p, pl.ds(flat[p * height + at + u], 1)]
 
         codes = picked[:block]
         residual_ref[p] = jnp.where(
@@ -221,16 +220,17 @@
     return pl.pallas_call(
         prepare_kernel,
         out_shape=(
-            jax.ShapeDtypeStruct((passages, height), I32),
+            jax.ShapeDtypeStruct((passages + 8, height), I32),
             jax.ShapeDtypeStruct((passages, block, width), F32),
             jax.ShapeDtypeStruct(candidates.shape, I32),
         ),
         in_specs=[VMEM] * 5,
         out_specs=(VMEM, VMEM, VMEM),
         scratch_shapes=[
-            pltpu.SMEM((passages * height,), I32),
+            pltpu.VMEM((passages + 8, height), I32),
+            pltpu.SMEM(((passages + 1) * height,), I32),
             pltpu.VMEM((block + UNROLL, width), I32),
-            pltpu.SemaphoreType.DMA((passages,)),
+            pltpu.SemaphoreType.DMA((passages + 1,)),
         ],
         compiler_params=pltpu.CompilerParams(vmem_limit_bytes=56 * MIB),
     )(pos, codes, buckets, location, candidates)
@@ -264,6 +264,7 @@
         ask[d * per : (d + 1) * per] = (offset // TILE) & (half_tiles - 1)
         ask[rows + d * per : rows + (d + 1) * per] = offset & (TILE - 1)
     ask[2 * rows : 2 * rows + 1] = sizes.astype(I32)
+    loads[1].start()
     copies = [
         pltpu.make_async_copy(ask.at[r], asked.at[pl.ds(r * height, height)], sems.at[r])
         for r in range(2 * rows + 1)
@@ -272,7 +273,6 @@
         copy.start()
     for copy in copies:
         copy.wait()
-    loads[1].start()
     line = lax.broadcasted_iota(I32, (8, width), 0)
 
     for h, table in enumerate((front, back)):
@@ -338,15 +338,17 @@
     )(received, table.reshape(shard_rows // TILE, TILE, width), after)
 
 
-def score_kernel(span, list_ref, replies_ref, residual_hbm, *refs):
+def score_kernel(span, list_hbm, replies_ref, residual_hbm, *refs):
     passages, block, width = residual_hbm.shape
-    *query_refs, out_ref, wide, tile, embedded, residual_ref, sem = refs
-    load = pltpu.make_async_copy(residual_hbm, residual_ref, sem)
+    *query_refs, out_ref, wide, tile, embedded, residual_ref, list_ref, sems = refs
+    listing = pltpu.make_async_copy(list_hbm, list_ref, sems.at[0])
+    listing.start()
+    load = pltpu.make_async_copy(residual_hbm, residual_ref, sems.at[1])
     load.start()
     groups, subs = lax.axis_size("groups"), lax.axis_size("sub")
     own_group, own_sub = lax.axis_index("groups"), lax.axis_index("sub")
     shards = query_refs[0].shape[0]
-    height = list_ref.shape[0] // passages
+    height = list_ref.shape[0] // (passages + 8)
     pair = 2 if shards % 2 == 0 else 1
     ahead = 4 if shards % (4 * pair) == 0 else 1
 
@@ -355,16 +357,22 @@
         at = pl.multiple_of(i * 256, 256)
         wide[pl.ds(at, 256)] = replies_ref[pl.ds(at, 256)].astype(F32)
 
+    listing.wait()
+
     @pl.loop(0, passages)
     def _(p):
-        count = list_ref[p * height] >> COUNT_AT
-
-        @pl.loop(0, (count + UNROLL - 1) // UNROLL)
+        count = list_ref[passages * height + p]
+
+        def move(at, rows):
+            for u in range(rows):
+                place = list_ref[p * height + at + u]
+                tile[pl.ds(p * block + at + u, 1)] = wide[pl.ds(place, 1)]
+
+        move(0, 32)
+
+        @pl.loop(2, (count + UNROLL - 1) // UNROLL)
         def _(i):
-            at = pl.multiple_of(i * UNROLL, UNROLL)
-            for u in range(UNROLL):
-                place = list_ref[p * height + at + u] & ((1 << TOKEN_AT) - 1)
-                tile[pl.ds(p * block + at + u, 1)] = wide[pl.ds(place, 1)]
+            move(pl.multiple_of(i * UNROLL, UNROLL), UNROLL)
 
     load.wait()
     line = lax.broadcasted_iota(I32, (block, width), 0)
@@ -373,7 +381,7 @@
     for p in range(0, passages, 2):
         both = []
         for q in (p, p + 1):
-            count = list_ref[q * height] >> COUNT_AT
+            count = list_ref[passages * height + q]
             counts = jnp.where(here == q, count, counts)
             rows = tile[q * block : (q + 1) * block] + residual_ref[q]
             both.append(jnp.where(line < count, rows, rows[0:1]))
@@ -404,14 +412,15 @@
     return pl.pallas_call(
         functools.partial(score_kernel, span),
         out_shape=jax.ShapeDtypeStruct((devices, passages, span), F32),
-        in_specs=[SMEM, VMEM, HBM] + [VMEM] * len(queries),
+        in_specs=[HBM, VMEM, HBM] + [VMEM] * len(queries),
         out_specs=VMEM,
         scratch_shapes=[
             pltpu.VMEM((replies.shape[0], width), F32),
             pltpu.VMEM((passages * block + UNROLL, width), F32),
             pltpu.VMEM((passages * block, width), BF16),
             pltpu.VMEM((passages, block, width), F32),
-            pltpu.SemaphoreType.DMA,
+            pltpu.SMEM(lists.shape, I32),
+            pltpu.SemaphoreType.DMA((2,)),
         ],
         compiler_params=pltpu.CompilerParams(vmem_limit_bytes=24 * MIB),
     )(lists, replies, residuals, *queries)
@@ -486,7 +495,7 @@
         others = [turned(array, "sub", s) for s in range(1, subs)]
         own = turned(others[-1], "sub", 1) if array is near and others else array
         spread += [own] + others
-    best = score(lists.reshape(token_count), replies.reshape(shards * cap, width), residuals, spread, span)
+    best = score(lists.reshape(lists.size), replies.reshape(shards * cap, width), residuals, spread, span)
     mine = lax.all_to_all(best, ("groups", "blk", "sub"), split_axis=0, concat_axis=0, tiled=True)
     return pick(slots, mine.reshape(parts, shards * subs * passages, span), tokens)
 

time: 64.1 us -> 63.5 us (level)
  Pallas kernels: 19.4 us -> 18.7 us
where the time goes in v5:
time: 63.5 us; the launch traced here: 62.7 us
  Pallas kernels  18.7 us (29%)
  waiting for transfers between devices  16.8 us (26%)
  blocking collectives  13.6 us (21%)
  starting transfers between devices  12.7 us (20%)
  local copies, waits for them, and re-layouts  0.75 us (1%)
    all_to_all x1, blocking collectives, body(): lax.all_to_all(best, ('groups', 'blk', 'sub'), split_axis=0, concat_axis=...  13.6 us
    ppermute x4, waiting for transfers between devices, turned(): lax.ppermute(array, axis, [(i, (i + shift) % size) for i in range(size)])  9.47 us
    all_to_all x1, starting transfers between devices, body(): near = lax.all_to_all(sent, 'blk', split_axis=0, concat_axis=0, tiled=True)  7.29 us
    pallas_call x1, Pallas kernels, fetch(): pl.pallas_call(functools.partial(fetch_kernel, span, cap), out_shape=jax....  6.04 us
    pallas_call x1, Pallas kernels, prepare(): pl.pallas_call(prepare_kernel, out_shape=(jax.ShapeDtypeStruct((passages...  4.85 us
    all_to_all x1, waiting for transfers between devices, body(): near = lax.all_to_all(sent, 'blk', split_axis=0, concat_axis=0, tiled=True)  4.72 us
    pallas_call x1, Pallas kernels, score(): pl.pallas_call(functools.partial(score_kernel, span), out_shape=jax.Shape...  4.35 us
    all_to_all x1, starting transfers between devices, body(): lax.all_to_all(found.reshape(shards, cap, width), 'blk', split_axis=0, co...  3.71 us
  transfers between devices with their start and end apart: 6, of which 5 were waited for; matrix products, arithmetic and copies ran while one was open for 0% of the time, Pallas kernels for 8%

profile of v5, /device:TPU:0, one launch (start us, length us, event | category | flops | bytes accessed | tf_op | source)
XLA Modules:
  0.0 62.7 jit_solution(8024454232710024782)
XLA Ops:
  0.0 2.3 %shard_map.82 = (bf16[8,144,128]{2,1,0:T(8,128)(2,1)}, s32[16,128]{1,0:T(8,128)}) custom-call(s32[16]{0:T(128)} %lengths_hbm.1, s32[16,128]{1,0:T(8,128)} %bitcast.16, bf16[128,128]{1,0:T(8,128)(2,1)} %bitcast.15), custom_call_target="tpu_custom_call" | custom-call | tf_op jit(solution)/shard_map/pallas_call | solution.py:124
  2.3 7.3 %all-to-all-start = ((bf16[8,144,128]{2,1,0:T(8,128)(2,1)}), bf16[8,144,128]{2,1,0:T(8,128)(2,1)S(1)}, u32[]{:S(2)}, u32[]{:S(2)}) async-start(bf16[8,144,128]{2,1,0:T(8,128)(2,1)} %get-tuple-element.13), calls=%async_computation | async-start | bytes 589824 | tf_op jit(solution)/shard_map/all_to_all | solution.py:479
  9.6 4.9 %shard_map.83 = (s32[24,128]{1,0:T(8,128)}, f32[16,72,128]{2,1,0:T(8,128)}, s32[4,128]{1,0:T(4,128)}) custom-call(s32[16,128]{1,0:T(8,128)} %get-tuple-element.10.pos_ref, s32[16,128,128]{2,1,0:T(8,128)} %bitcast.14, f32[4,128]{1,0:T(4,128)} %buckets_ref.1, s32[2,128]{1,0:T(2,128)} %bitcast.17, s32[4,128]{1,0:T(4,128)} %candidates_ref.1), custom_call_target="tpu_custom_call" | custom-call | tf_op jit(solution)/shard_map/pallas_call | solution.py:220
  14.5 0.0 copy-start
  14.5 0.0 copy-start.1
  14.5 0.0 copy-start.2
  14.5 4.7 %all-to-all-done.received_hbm = bf16[8,144,128]{2,1,0:T(8,128)(2,1)S(1)} async-done(((bf16[8,144,128]{2,1,0:T(8,128)(2,1)}), bf16[8,144,128]{2,1,0:T(8,128)(2,1)S(1)}, u32[]{:S(2)}, u32[]{:S(2)}) %all-to-all-start) | async-done | bytes 294944 | tf_op jit(solution)/shard_map/all_to_all | solution.py:479
  19.2 0.0 copy-start.3
  19.2 0.7 %copy-done.3 = bf16[8,144,128]{2,1,0:T(8,128)(2,1)} copy-done((bf16[8,144,128]{2,1,0:T(8,128)(2,1)}, bf16[8,144,128]{2,1,0:T(8,128)(2,1)S(1)}, u32[]{:S(2)}) %copy-start.3) | copy-done | bytes 294936
  20.0 6.0 %shard_map.84 = bf16[2048,128]{1,0:T(8,128)(2,1)} custom-call(bf16[8,144,128]{2,1,0:T(8,128)(2,1)} %copy-done.3, bf16[2048,16,128]{2,1,0:T(8,128)(2,1)} %bitcast.12, s32[4,128]{1,0:T(4,128)} %get-tuple-element.11.after_ref.slots_ref), custom_call_target="tpu_custom_call" | custom-call | tf_op jit(solution)/shard_map/pallas_call | solution.py:320
  26.0 3.7 %all-to-all-start.1 = ((bf16[8,256,128]{2,1,0:T(8,128)(2,1)}), bf16[8,256,128]{2,1,0:T(8,128)(2,1)S(1)}, u32[]{:S(2)}, u32[]{:S(2)}) async-start(bf16[8,256,128]{2,1,0:T(8,128)(2,1)} %bitcast.13), calls=%async_computation.1 | async-start | bytes 1048576 | tf_op jit(solution)/shard_map/all_to_all | solution.py:489
  29.7 0.0 collective-permute-start
  29.7 1.6 %collective-permute-start.2 = (bf16[8,144,128]{2,1,0:T(8,128)(2,1)}, bf16[8,144,128]{2,1,0:T(8,128)(2,1)S(1)}, u32[]{:S(2)}, u32[]{:S(2)}) collective-permute-start(bf16[8,144,128]{2,1,0:T(8,128)(2,1)} %copy-done.3), channel_id=1, source_target_pairs={{0,16},{16,0},{1,17},{17,1},{2,18},{18,2},{3,19},{19,3},{4,20},{20... | collective-permute-start | bytes 884744 | tf_op jit(solution)/shard_map/ppermute | solution.py:456
  31.3 0.2 collective-permute-done.refs_1_
  31.5 0.1 collective-permute-start.1
  31.7 7.7 %collective-permute-done.2.refs_2_ = bf16[8,144,128]{2,1,0:T(8,128)(2,1)S(1)} collective-permute-done((bf16[8,144,128]{2,1,0:T(8,128)(2,1)}, bf16[8,144,128]{2,1,0:T(8,128)(2,1)S(1)}, u32[]{:S(2)}, u32[]{:S(2)}) %collective-permute-start.2) | collective-permute-done | bytes 294944 | tf_op jit(solution)/shard_map/ppermute | solution.py:456
  39.4 0.0 collective-permute-start.3
  39.4 0.0 collective-permute-done.1.refs_0_
  39.4 1.6 %collective-permute-done.3.refs_3_ = bf16[8,144,128]{2,1,0:T(8,128)(2,1)S(1)} collective-permute-done((bf16[8,144,128]{2,1,0:T(8,128)(2,1)S(1)}, bf16[8,144,128]{2,1,0:T(8,128)(2,1)S(1)}, u32[]{:S(2)}, u32[]{:S(2)}) %collective-permute-start.3) | collective-permute-done | bytes 294944 | tf_op jit(solution)/shard_map/ppermute | solution.py:456
  40.9 2.7 %all-to-all-done.1 = bf16[8,256,128]{2,1,0:T(8,128)(2,1)S(1)} async-done(((bf16[8,256,128]{2,1,0:T(8,128)(2,1)}), bf16[8,256,128]{2,1,0:T(8,128)(2,1)S(1)}, u32[]{:S(2)}, u32[]{:S(2)}) %all-to-all-start.1) | async-done | bytes 524320 | tf_op jit(solution)/shard_map/all_to_all | solution.py:489
  43.6 0.0 copy-done
  43.6 0.0 copy-done.1
  43.6 4.4 %shard_map.85 = f32[32,16,128]{2,1,0:T(8,128)S(1)} custom-call(s32[3072]{0:T(1024)S(1)} %bitcast.11, bf16[2048,128]{1,0:T(8,128)(2,1)S(1)} %bitcast.9, f32[16,72,128]{2,1,0:T(8,128)S(1)} %copy-done, bf16[8,144,128]{2,1,0:T(8,128)(2,1)S(1)} %collective-permute-done.1.refs_0_, bf16[8,144,128]{2,1,0:T(8,128)(2,1)S(1)} %collective-permute-done.refs_1_, ...), custom_call_target="tpu_custom_call" | custom-call | tf_op jit(solution)/shard_map/pallas_call | solution.py:412
  48.0 13.6 %all_to_all.15 = f32[32,16,128]{2,1,0:T(8,128)S(1)} all-to-all(f32[32,16,128]{2,1,0:T(8,128)S(1)} %shard_map.85), channel_id=1, replica_groups=mesh['groups'=2,'blk'=8,'sub'=2] {'groups','blk','sub'}, dimensions={0} | all-to-all | bytes 524288 | tf_op jit(solution)/shard_map/all_to_all | solution.py:499
  61.6 0.0 copy-done.2
  61.6 1.1 %shard_map.86 = f32[4,128]{1,0:T(4,128)} custom-call(s32[4,128]{1,0:T(4,128)S(1)} %copy-done.2, f32[2,256,128]{2,1,0:T(8,128)S(1)} %bitcast.10), custom_call_target="tpu_custom_call" | custom-call | tf_op jit(solution)/shard_map/pallas_call | solution.py:447
Async XLA Ops:
  2.3 16.9 %all-to-all-start = ((bf16[8,144,128]{2,1,0:T(8,128)(2,1)}), bf16[8,144,128]{2,1,0:T(8,128)(2,1)S(1)}, u32[]{:S(2)}, u32[]{:S(2)}) async-start(bf16[8,144,128]{2,1,0:T(8,128)(2,1)} %get-tuple-element.13), calls=%async_computation | async-start | bytes 589824 | tf_op jit(solution)/shard_map/all_to_all | solution.py:479
  14.5 29.1 %copy-start = (f32[16,72,128]{2,1,0:T(8,128)S(1)}, f32[16,72,128]{2,1,0:T(8,128)}, u32[]{:S(2)}) copy-start(f32[16,72,128]{2,1,0:T(8,128)} %get-tuple-element.14.residual_hbm) | copy-start | bytes 1769476
  14.5 29.1 %copy-start.1 = (s32[24,128]{1,0:T(8,128)S(1)}, s32[24,128]{1,0:T(8,128)}, u32[]{:S(2)}) copy-start(s32[24,128]{1,0:T(8,128)} %get-tuple-element.12) | copy-start | bytes 36868
  14.5 47.1 %copy-start.2 = (s32[4,128]{1,0:T(4,128)S(1)}, s32[4,128]{1,0:T(4,128)}, u32[]{:S(2)}) copy-start(s32[4,128]{1,0:T(4,128)} %get-tuple-element.11.after_ref.slots_ref) | copy-start | bytes 6148
  19.2 0.7 %copy-start.3 = (bf16[8,144,128]{2,1,0:T(8,128)(2,1)}, bf16[8,144,128]{2,1,0:T(8,128)(2,1)S(1)}, u32[]{:S(2)}) copy-start(bf16[8,144,128]{2,1,0:T(8,128)(2,1)S(1)} %all-to-all-done.received_hbm) | copy-start | bytes 884740
  26.0 17.6 %all-to-all-start.1 = ((bf16[8,256,128]{2,1,0:T(8,128)(2,1)}), bf16[8,256,128]{2,1,0:T(8,128)(2,1)S(1)}, u32[]{:S(2)}, u32[]{:S(2)}) async-start(bf16[8,256,128]{2,1,0:T(8,128)(2,1)} %bitcast.13), calls=%async_computation.1 | async-start | bytes 1048576 | tf_op jit(solution)/shard_map/all_to_all | solution.py:489
  29.7 1.8 %collective-permute-start = (bf16[8,144,128]{2,1,0:T(8,128)(2,1)}, bf16[8,144,128]{2,1,0:T(8,128)(2,1)S(1)}, u32[]{:S(2)}, u32[]{:S(2)}) collective-permute-start(bf16[8,144,128]{2,1,0:T(8,128)(2,1)} %copy-done.3), channel_id=1, source_target_pairs={{0,1},{1,0},{2,3},{3,2},{4,5},{5,4},{6,7},{7,6},{8,9},{9,8},{10,11... | collective-permute-start | bytes 884744 | tf_op jit(solution)/shard_map/ppermute | solution.py:456
  29.7 9.6 %collective-permute-start.2 = (bf16[8,144,128]{2,1,0:T(8,128)(2,1)}, bf16[8,144,128]{2,1,0:T(8,128)(2,1)S(1)}, u32[]{:S(2)}, u32[]{:S(2)}) collective-permute-start(bf16[8,144,128]{2,1,0:T(8,128)(2,1)} %copy-done.3), channel_id=1, source_target_pairs={{0,16},{16,0},{1,17},{17,1},{2,18},{18,2},{3,19},{19,3},{4,20},{20... | collective-permute-start | bytes 884744 | tf_op jit(solution)/shard_map/ppermute | solution.py:456
  31.5 7.8 %collective-permute-start.1 = (bf16[8,144,128]{2,1,0:T(8,128)(2,1)S(1)}, bf16[8,144,128]{2,1,0:T(8,128)(2,1)S(1)}, u32[]{:S(2)}, u32[]{:S(2)}) collective-permute-start(bf16[8,144,128]{2,1,0:T(8,128)(2,1)S(1)} %collective-permute-done.refs_1_), channel_id=1, source_target_pairs={{0,1},{1,0},{2,3},{3,2},{4,5},{5,4},{6,7},{7,6},{8,9},{9,8},{10,11... | collective-permute-start | bytes 884744 | tf_op jit(solution)/shard_map/ppermute | solution.py:456
  39.4 1.6 %collective-permute-start.3 = (bf16[8,144,128]{2,1,0:T(8,128)(2,1)S(1)}, bf16[8,144,128]{2,1,0:T(8,128)(2,1)S(1)}, u32[]{:S(2)}, u32[]{:S(2)}) collective-permute-start(bf16[8,144,128]{2,1,0:T(8,128)(2,1)S(1)} %collective-permute-done.2.refs_2_), channel_id=1, source_target_pairs={{0,1},{1,0},{2,3},{3,2},{4,5},{5,4},{6,7},{7,6},{8,9},{9,8},{10,11... | collective-permute-start | bytes 884744 | tf_op jit(solution)/shard_map/ppermute | solution.py:456

commit v6 on v5

--- a/solution.py
+++ b/solution.py
@@ -237,8 +237,8 @@
 
 
 def fetch_kernel(
-    span, cap, received_hbm, table_hbm, after_ref, out_ref,
-    front, back, message, ask, asked, even, odd, load_sems, sems, sem,
+    span, cap, received_hbm, table_hbm, after_ref, out_hbm,
+    front, back, message, ask, asked, even, odd, out_ref, load_sems, out_sems, sems, sem,
 ):
     shards, _, height = received_hbm.shape
     half_tiles, _, width = front.shape
@@ -275,6 +275,10 @@
         copy.wait()
     line = lax.broadcasted_iota(I32, (8, width), 0)
 
+    def leave(d):
+        own = pl.ds(pl.multiple_of(d * cap, cap), cap)
+        return pltpu.make_async_copy(out_ref.at[own], out_hbm.at[own], out_sems.at[d])
+
     for h, table in enumerate((front, back)):
         loads[h].wait()
 
@@ -309,6 +313,12 @@
                         halves[g] = jnp.where(here, row, halves[g])
                 out_ref[pl.ds(to, TILE)] = jnp.concatenate(halves, axis=0).astype(BF16)
 
+            if h == 1:
+                leave(d).start()
+
+    for d in range(shards):
+        leave(d).wait()
+
 
 def fetch(received, table, after, span, cap):
     shard_rows, width = table.shape
@@ -321,7 +331,7 @@
         functools.partial(fetch_kernel, span, cap),
         out_shape=jax.ShapeDtypeStruct((shards * cap, width), BF16),
         in_specs=[HBM, HBM, HBM],
-        out_specs=VMEM,
+        out_specs=HBM,
         scratch_shapes=[
             pltpu.VMEM(half, table.dtype),
             pltpu.VMEM(half, table.dtype),
@@ -330,7 +340,9 @@
             pltpu.SMEM((ask_rows * height,), I32),
             pltpu.VMEM((8 * TILE, width), F32),
             pltpu.VMEM((8 * TILE, width), F32),
+            pltpu.VMEM((shards * cap, width), BF16),
             pltpu.SemaphoreType.DMA((2,)),
+            pltpu.SemaphoreType.DMA((shards,)),
             pltpu.SemaphoreType.DMA((2 * rows + 1,)),
             pltpu.SemaphoreType.DMA,
         ],
@@ -391,19 +403,26 @@
         group = lax.rem(own_group + groups - step // subs, groups)
         sub = lax.rem(own_sub + subs - step % subs, subs)
 
-        @pl.loop(0, shards // (pair * ahead))
-        def _(i):
-            for h in range(ahead):
-                c = i * ahead + h
-                queries = jnp.concatenate(
-                    [query_ref[c * pair + e, :span] for e in range(pair)], axis=0
-                )
-                scores = dot_nt(embedded[...], queries)
-                best = jnp.max(scores.reshape(passages, block, pair * span), axis=1)
-                best = jnp.where(counts > 0, best, -3e38)
-                for e in range(pair):
-                    device = (group * shards + c * pair + e) * subs + sub
-                    out_ref[device] = best[:, e * span : (e + 1) * span]
+        def columns(c):
+            queries = jnp.concatenate(
+                [query_ref[c * pair + e, :span] for e in range(pair)], axis=0
+            )
+            scores = dot_nt(embedded[...], queries)
+            best = jnp.max(scores.reshape(passages, block, pair * span), axis=1)
+            best = jnp.where(counts > 0, best, -3e38)
+            for e in range(pair):
+                device = (group * shards + c * pair + e) * subs + sub
+                out_ref[device] = best[:, e * span : (e + 1) * span]
+
+        if shards == pair * ahead:
+            for c in range(ahead):
+                columns(c)
+        else:
+
+            @pl.loop(0, shards // (pair * ahead))
+            def _(i):
+                for h in range(ahead):
+                    columns(i * ahead + h)
 
 
 def score(lists, replies, residuals, queries, span):

time: 63.5 us -> 63.3 us (level)
  no operation moved by 1% of the time
where the time goes in v6:
time: 63.3 us; the launch traced here: 62.8 us
  Pallas kernels  18.3 us (29%)
  waiting for transfers between devices  17.3 us (27%)
  blocking collectives  13.7 us (22%)
  starting transfers between devices  12.7 us (20%)
  local copies, waits for them, and re-layouts  0.75 us (1%)
    all_to_all x1, blocking collectives, body(): lax.all_to_all(best, ('groups', 'blk', 'sub'), split_axis=0, concat_axis=...  13.7 us
    ppermute x4, waiting for transfers between devices, turned(): lax.ppermute(array, axis, [(i, (i + shift) % size) for i in range(size)])  9.51 us
    all_to_all x1, starting transfers between devices, body(): near = lax.all_to_all(sent, 'blk', split_axis=0, concat_axis=0, tiled=True)  7.29 us
    pallas_call x1, Pallas kernels, fetch(): pl.pallas_call(functools.partial(fetch_kernel, span, cap), out_shape=jax....  5.71 us
    pallas_call x1, Pallas kernels, prepare(): pl.pallas_call(prepare_kernel, out_shape=(jax.ShapeDtypeStruct((passages...  4.83 us
    all_to_all x1, waiting for transfers between devices, body(): near = lax.all_to_all(sent, 'blk', split_axis=0, concat_axis=0, tiled=True)  4.75 us
    pallas_call x1, Pallas kernels, score(): pl.pallas_call(functools.partial(score_kernel, span), out_shape=jax.Shape...  4.34 us
    all_to_all x1, starting transfers between devices, body(): lax.all_to_all(found.reshape(shards, cap, width), 'blk', split_axis=0, co...  3.76 us
  transfers between devices with their start and end apart: 6, of which 5 were waited for; matrix products, arithmetic and copies ran while one was open for 0% of the time, Pallas kernels for 8%

profile of v6, /device:TPU:0, one launch (start us, length us, event | category | flops | bytes accessed | tf_op | source)
XLA Modules:
  0.0 62.8 jit_solution(5766694243634849276)
XLA Ops:
  0.0 2.3 %shard_map.82 = (bf16[8,144,128]{2,1,0:T(8,128)(2,1)}, s32[16,128]{1,0:T(8,128)}) custom-call(s32[16]{0:T(128)} %lengths_hbm.1, s32[16,128]{1,0:T(8,128)} %bitcast.16, bf16[128,128]{1,0:T(8,128)(2,1)} %bitcast.15), custom_call_target="tpu_custom_call" | custom-call | tf_op jit(solution)/shard_map/pallas_call | solution.py:124
  2.3 7.3 %all-to-all-start = ((bf16[8,144,128]{2,1,0:T(8,128)(2,1)}), bf16[8,144,128]{2,1,0:T(8,128)(2,1)S(1)}, u32[]{:S(2)}, u32[]{:S(2)}) async-start(bf16[8,144,128]{2,1,0:T(8,128)(2,1)} %get-tuple-element.13), calls=%async_computation | async-start | bytes 589824 | tf_op jit(solution)/shard_map/all_to_all | solution.py:498
  9.6 4.8 %shard_map.83 = (s32[24,128]{1,0:T(8,128)}, f32[16,72,128]{2,1,0:T(8,128)}, s32[4,128]{1,0:T(4,128)}) custom-call(s32[16,128]{1,0:T(8,128)} %get-tuple-element.10.pos_ref, s32[16,128,128]{2,1,0:T(8,128)} %bitcast.14, f32[4,128]{1,0:T(4,128)} %buckets_ref.1, s32[2,128]{1,0:T(2,128)} %bitcast.17, s32[4,128]{1,0:T(4,128)} %candidates_ref.1), custom_call_target="tpu_custom_call" | custom-call | tf_op jit(solution)/shard_map/pallas_call | solution.py:220
  14.4 0.0 copy-start
  14.4 0.0 copy-start.1
  14.5 0.0 copy-start.2
  14.5 4.7 %all-to-all-done.received_hbm = bf16[8,144,128]{2,1,0:T(8,128)(2,1)S(1)} async-done(((bf16[8,144,128]{2,1,0:T(8,128)(2,1)}), bf16[8,144,128]{2,1,0:T(8,128)(2,1)S(1)}, u32[]{:S(2)}, u32[]{:S(2)}) %all-to-all-start) | async-done | bytes 294944 | tf_op jit(solution)/shard_map/all_to_all | solution.py:498
  19.2 0.0 copy-start.3
  19.2 0.7 %copy-done.3 = bf16[8,144,128]{2,1,0:T(8,128)(2,1)} copy-done((bf16[8,144,128]{2,1,0:T(8,128)(2,1)}, bf16[8,144,128]{2,1,0:T(8,128)(2,1)S(1)}, u32[]{:S(2)}) %copy-start.3) | copy-done | bytes 294936
  20.0 5.7 %shard_map.84 = bf16[2048,128]{1,0:T(8,128)(2,1)} custom-call(bf16[8,144,128]{2,1,0:T(8,128)(2,1)} %copy-done.3, bf16[2048,16,128]{2,1,0:T(8,128)(2,1)} %bitcast.12, s32[4,128]{1,0:T(4,128)} %get-tuple-element.11.after_ref.slots_ref), custom_call_target="tpu_custom_call" | custom-call | tf_op jit(solution)/shard_map/pallas_call | solution.py:330
  25.7 3.8 %all-to-all-start.1 = ((bf16[8,256,128]{2,1,0:T(8,128)(2,1)}), bf16[8,256,128]{2,1,0:T(8,128)(2,1)S(1)}, u32[]{:S(2)}, u32[]{:S(2)}) async-start(bf16[8,256,128]{2,1,0:T(8,128)(2,1)} %bitcast.13), calls=%async_computation.1 | async-start | bytes 1048576 | tf_op jit(solution)/shard_map/all_to_all | solution.py:508
  29.4 0.0 collective-permute-start
  29.4 1.6 %collective-permute-start.2 = (bf16[8,144,128]{2,1,0:T(8,128)(2,1)}, bf16[8,144,128]{2,1,0:T(8,128)(2,1)S(1)}, u32[]{:S(2)}, u32[]{:S(2)}) collective-permute-start(bf16[8,144,128]{2,1,0:T(8,128)(2,1)} %copy-done.3), channel_id=1, source_target_pairs={{0,16},{16,0},{1,17},{17,1},{2,18},{18,2},{3,19},{19,3},{4,20},{20... | collective-permute-start | bytes 884744 | tf_op jit(solution)/shard_map/ppermute | solution.py:475
  31.0 0.2 collective-permute-done.refs_1_
  31.2 0.1 collective-permute-start.1
  31.4 7.7 %collective-permute-done.2.refs_2_ = bf16[8,144,128]{2,1,0:T(8,128)(2,1)S(1)} collective-permute-done((bf16[8,144,128]{2,1,0:T(8,128)(2,1)}, bf16[8,144,128]{2,1,0:T(8,128)(2,1)S(1)}, u32[]{:S(2)}, u32[]{:S(2)}) %collective-permute-start.2) | collective-permute-done | bytes 294944 | tf_op jit(solution)/shard_map/ppermute | solution.py:475
  39.1 0.0 collective-permute-start.3
  39.1 0.0 collective-permute-done.1.refs_0_
  39.1 1.6 %collective-permute-done.3.refs_3_ = bf16[8,144,128]{2,1,0:T(8,128)(2,1)S(1)} collective-permute-done((bf16[8,144,128]{2,1,0:T(8,128)(2,1)S(1)}, bf16[8,144,128]{2,1,0:T(8,128)(2,1)S(1)}, u32[]{:S(2)}, u32[]{:S(2)}) %collective-permute-start.3) | collective-permute-done | bytes 294944 | tf_op jit(solution)/shard_map/ppermute | solution.py:475
  40.6 3.0 %all-to-all-done.1 = bf16[8,256,128]{2,1,0:T(8,128)(2,1)S(1)} async-done(((bf16[8,256,128]{2,1,0:T(8,128)(2,1)}), bf16[8,256,128]{2,1,0:T(8,128)(2,1)S(1)}, u32[]{:S(2)}, u32[]{:S(2)}) %all-to-all-start.1) | async-done | bytes 524320 | tf_op jit(solution)/shard_map/all_to_all | solution.py:508
  43.7 0.0 copy-done
  43.7 0.0 copy-done.1
  43.7 4.3 %shard_map.85 = f32[32,16,128]{2,1,0:T(8,128)S(1)} custom-call(s32[3072]{0:T(1024)S(1)} %bitcast.11, bf16[2048,128]{1,0:T(8,128)(2,1)S(1)} %bitcast.9, f32[16,72,128]{2,1,0:T(8,128)S(1)} %copy-done, bf16[8,144,128]{2,1,0:T(8,128)(2,1)S(1)} %collective-permute-done.1.refs_0_, bf16[8,144,128]{2,1,0:T(8,128)(2,1)S(1)} %collective-permute-done.refs_1_, ...), custom_call_target="tpu_custom_call" | custom-call | tf_op jit(solution)/shard_map/pallas_call | solution.py:431
  48.0 13.7 %all_to_all.15 = f32[32,16,128]{2,1,0:T(8,128)S(1)} all-to-all(f32[32,16,128]{2,1,0:T(8,128)S(1)} %shard_map.85), channel_id=1, replica_groups=mesh['groups'=2,'blk'=8,'sub'=2] {'groups','blk','sub'}, dimensions={0} | all-to-all | bytes 524288 | tf_op jit(solution)/shard_map/all_to_all | solution.py:518
  61.7 0.0 copy-done.2
  61.7 1.1 %shard_map.86 = f32[4,128]{1,0:T(4,128)} custom-call(s32[4,128]{1,0:T(4,128)S(1)} %copy-done.2, f32[2,256,128]{2,1,0:T(8,128)S(1)} %bitcast.10), custom_call_target="tpu_custom_call" | custom-call | tf_op jit(solution)/shard_map/pallas_call | solution.py:466
Async XLA Ops:
  2.3 16.9 %all-to-all-start = ((bf16[8,144,128]{2,1,0:T(8,128)(2,1)}), bf16[8,144,128]{2,1,0:T(8,128)(2,1)S(1)}, u32[]{:S(2)}, u32[]{:S(2)}) async-start(bf16[8,144,128]{2,1,0:T(8,128)(2,1)} %get-tuple-element.13), calls=%async_computation | async-start | bytes 589824 | tf_op jit(solution)/shard_map/all_to_all | solution.py:498
  14.4 29.2 %copy-start = (f32[16,72,128]{2,1,0:T(8,128)S(1)}, f32[16,72,128]{2,1,0:T(8,128)}, u32[]{:S(2)}) copy-start(f32[16,72,128]{2,1,0:T(8,128)} %get-tuple-element.14.residual_hbm) | copy-start | bytes 1769476
  14.4 29.2 %copy-start.1 = (s32[24,128]{1,0:T(8,128)S(1)}, s32[24,128]{1,0:T(8,128)}, u32[]{:S(2)}) copy-start(s32[24,128]{1,0:T(8,128)} %get-tuple-element.12) | copy-start | bytes 36868
  14.5 47.2 %copy-start.2 = (s32[4,128]{1,0:T(4,128)S(1)}, s32[4,128]{1,0:T(4,128)}, u32[]{:S(2)}) copy-start(s32[4,128]{1,0:T(4,128)} %get-tuple-element.11.after_ref.slots_ref) | copy-start | bytes 6148
  19.2 0.7 %copy-start.3 = (bf16[8,144,128]{2,1,0:T(8,128)(2,1)}, bf16[8,144,128]{2,1,0:T(8,128)(2,1)S(1)}, u32[]{:S(2)}) copy-start(bf16[8,144,128]{2,1,0:T(8,128)(2,1)S(1)} %all-to-all-done.received_hbm) | copy-start | bytes 884740
  25.7 18.0 %all-to-all-start.1 = ((bf16[8,256,128]{2,1,0:T(8,128)(2,1)}), bf16[8,256,128]{2,1,0:T(8,128)(2,1)S(1)}, u32[]{:S(2)}, u32[]{:S(2)}) async-start(bf16[8,256,128]{2,1,0:T(8,128)(2,1)} %bitcast.13), calls=%async_computation.1 | async-start | bytes 1048576 | tf_op jit(solution)/shard_map/all_to_all | solution.py:508
  29.4 1.8 %collective-permute-start = (bf16[8,144,128]{2,1,0:T(8,128)(2,1)}, bf16[8,144,128]{2,1,0:T(8,128)(2,1)S(1)}, u32[]{:S(2)}, u32[]{:S(2)}) collective-permute-start(bf16[8,144,128]{2,1,0:T(8,128)(2,1)} %copy-done.3), channel_id=1, source_target_pairs={{0,1},{1,0},{2,3},{3,2},{4,5},{5,4},{6,7},{7,6},{8,9},{9,8},{10,11... | collective-permute-start | bytes 884744 | tf_op jit(solution)/shard_map/ppermute | solution.py:475
  29.4 9.6 %collective-permute-start.2 = (bf16[8,144,128]{2,1,0:T(8,128)(2,1)}, bf16[8,144,128]{2,1,0:T(8,128)(2,1)S(1)}, u32[]{:S(2)}, u32[]{:S(2)}) collective-permute-start(bf16[8,144,128]{2,1,0:T(8,128)(2,1)} %copy-done.3), channel_id=1, source_target_pairs={{0,16},{16,0},{1,17},{17,1},{2,18},{18,2},{3,19},{19,3},{4,20},{20... | collective-permute-start | bytes 884744 | tf_op jit(solution)/shard_map/ppermute | solution.py:475
  31.2 7.8 %collective-permute-start.1 = (bf16[8,144,128]{2,1,0:T(8,128)(2,1)S(1)}, bf16[8,144,128]{2,1,0:T(8,128)(2,1)S(1)}, u32[]{:S(2)}, u32[]{:S(2)}) collective-permute-start(bf16[8,144,128]{2,1,0:T(8,128)(2,1)S(1)} %collective-permute-done.refs_1_), channel_id=1, source_target_pairs={{0,1},{1,0},{2,3},{3,2},{4,5},{5,4},{6,7},{7,6},{8,9},{9,8},{10,11... | collective-permute-start | bytes 884744 | tf_op jit(solution)/shard_map/ppermute | solution.py:475
  39.1 1.6 %collective-permute-start.3 = (bf16[8,144,128]{2,1,0:T(8,128)(2,1)S(1)}, bf16[8,144,128]{2,1,0:T(8,128)(2,1)S(1)}, u32[]{:S(2)}, u32[]{:S(2)}) collective-permute-start(bf16[8,144,128]{2,1,0:T(8,128)(2,1)S(1)} %collective-permute-done.2.refs_2_), channel_id=1, source_target_pairs={{0,1},{1,0},{2,3},{3,2},{4,5},{5,4},{6,7},{7,6},{8,9},{9,8},{10,11... | collective-permute-start | bytes 884744 | tf_op jit(solution)/shard_map/ppermute | solution.py:475

commit v7 on v6

--- a/solution.py
+++ b/solution.py
@@ -282,7 +282,7 @@
     for h, table in enumerate((front, back)):
         loads[h].wait()
 
-        @pl.loop(0, shards)
+        @pl.loop(0, shards, unroll=4)
         def _(d):
             base = d * (per * height)
             count = asked[2 * rows * height + d]

time: 63.3 us -> 63.2 us (level)
  no operation moved by 1% of the time
where the time goes in v7:
time: 63.2 us; the launch traced here: 62.6 us
  Pallas kernels  18.5 us (29%)
  waiting for transfers between devices  16.8 us (27%)
  blocking collectives  13.6 us (22%)
  starting transfers between devices  12.9 us (20%)
  local copies, waits for them, and re-layouts  0.75 us (1%)
    all_to_all x1, blocking collectives, body(): lax.all_to_all(best, ('groups', 'blk', 'sub'), split_axis=0, concat_axis=...  13.6 us
    ppermute x4, waiting for transfers between devices, turned(): lax.ppermute(array, axis, [(i, (i + shift) % size) for i in range(size)])  9.55 us
    all_to_all x1, starting transfers between devices, body(): near = lax.all_to_all(sent, 'blk', split_axis=0, concat_axis=0, tiled=True)  7.29 us
    pallas_call x1, Pallas kernels, fetch(): pl.pallas_call(functools.partial(fetch_kernel, span, cap), out_shape=jax....  5.68 us
    pallas_call x1, Pallas kernels, prepare(): pl.pallas_call(prepare_kernel, out_shape=(jax.ShapeDtypeStruct((passages...  4.96 us
    all_to_all x1, waiting for transfers between devices, body(): near = lax.all_to_all(sent, 'blk', split_axis=0, concat_axis=0, tiled=True)  4.62 us
    pallas_call x1, Pallas kernels, score(): pl.pallas_call(functools.partial(score_kernel, span), out_shape=jax.Shape...  4.44 us
    all_to_all x1, starting transfers between devices, body(): lax.all_to_all(found.reshape(shards, cap, width), 'blk', split_axis=0, co...  3.91 us
  transfers between devices with their start and end apart: 6, of which 5 were waited for; matrix products, arithmetic and copies ran while one was open for 0% of the time, Pallas kernels for 8%

profile of v7, /device:TPU:0, one launch (start us, length us, event | category | flops | bytes accessed | tf_op | source)
XLA Modules:
  0.0 62.6 jit_solution(12343552631738836468)
XLA Ops:
  0.0 2.3 %shard_map.82 = (bf16[8,144,128]{2,1,0:T(8,128)(2,1)}, s32[16,128]{1,0:T(8,128)}) custom-call(s32[16]{0:T(128)} %lengths_hbm.1, s32[16,128]{1,0:T(8,128)} %bitcast.16, bf16[128,128]{1,0:T(8,128)(2,1)} %bitcast.15), custom_call_target="tpu_custom_call" | custom-call | tf_op jit(solution)/shard_map/pallas_call | solution.py:124
  2.3 7.3 %all-to-all-start = ((bf16[8,144,128]{2,1,0:T(8,128)(2,1)}), bf16[8,144,128]{2,1,0:T(8,128)(2,1)S(1)}, u32[]{:S(2)}, u32[]{:S(2)}) async-start(bf16[8,144,128]{2,1,0:T(8,128)(2,1)} %get-tuple-element.13), calls=%async_computation | async-start | bytes 589824 | tf_op jit(solution)/shard_map/all_to_all | solution.py:498
  9.6 5.0 %shard_map.83 = (s32[24,128]{1,0:T(8,128)}, f32[16,72,128]{2,1,0:T(8,128)}, s32[4,128]{1,0:T(4,128)}) custom-call(s32[16,128]{1,0:T(8,128)} %get-tuple-element.10.pos_ref, s32[16,128,128]{2,1,0:T(8,128)} %bitcast.14, f32[4,128]{1,0:T(4,128)} %buckets_ref.1, s32[2,128]{1,0:T(2,128)} %bitcast.17, s32[4,128]{1,0:T(4,128)} %candidates_ref.1), custom_call_target="tpu_custom_call" | custom-call | tf_op jit(solution)/shard_map/pallas_call | solution.py:220
  14.6 0.0 copy-start
  14.6 0.0 copy-start.1
  14.6 0.0 copy-start.2
  14.6 4.6 %all-to-all-done.received_hbm = bf16[8,144,128]{2,1,0:T(8,128)(2,1)S(1)} async-done(((bf16[8,144,128]{2,1,0:T(8,128)(2,1)}), bf16[8,144,128]{2,1,0:T(8,128)(2,1)S(1)}, u32[]{:S(2)}, u32[]{:S(2)}) %all-to-all-start) | async-done | bytes 294944 | tf_op jit(solution)/shard_map/all_to_all | solution.py:498
  19.2 0.0 copy-start.3
  19.2 0.7 %copy-done.3 = bf16[8,144,128]{2,1,0:T(8,128)(2,1)} copy-done((bf16[8,144,128]{2,1,0:T(8,128)(2,1)}, bf16[8,144,128]{2,1,0:T(8,128)(2,1)S(1)}, u32[]{:S(2)}) %copy-start.3) | copy-done | bytes 294936
  20.0 5.7 %shard_map.84 = bf16[2048,128]{1,0:T(8,128)(2,1)} custom-call(bf16[8,144,128]{2,1,0:T(8,128)(2,1)} %copy-done.3, bf16[2048,16,128]{2,1,0:T(8,128)(2,1)} %bitcast.12, s32[4,128]{1,0:T(4,128)} %get-tuple-element.11.after_ref.slots_ref), custom_call_target="tpu_custom_call" | custom-call | tf_op jit(solution)/shard_map/pallas_call | solution.py:330
  25.6 3.9 %all-to-all-start.1 = ((bf16[8,256,128]{2,1,0:T(8,128)(2,1)}), bf16[8,256,128]{2,1,0:T(8,128)(2,1)S(1)}, u32[]{:S(2)}, u32[]{:S(2)}) async-start(bf16[8,256,128]{2,1,0:T(8,128)(2,1)} %bitcast.13), calls=%async_computation.1 | async-start | bytes 1048576 | tf_op jit(solution)/shard_map/all_to_all | solution.py:508
  29.6 0.0 collective-permute-start
  29.6 1.5 %collective-permute-start.2 = (bf16[8,144,128]{2,1,0:T(8,128)(2,1)}, bf16[8,144,128]{2,1,0:T(8,128)(2,1)S(1)}, u32[]{:S(2)}, u32[]{:S(2)}) collective-permute-start(bf16[8,144,128]{2,1,0:T(8,128)(2,1)} %copy-done.3), channel_id=1, source_target_pairs={{0,16},{16,0},{1,17},{17,1},{2,18},{18,2},{3,19},{19,3},{4,20},{20... | collective-permute-start | bytes 884744 | tf_op jit(solution)/shard_map/ppermute | solution.py:475
  31.1 0.3 collective-permute-done.refs_1_
  31.3 0.1 collective-permute-start.1
  31.5 7.7 %collective-permute-done.2.refs_2_ = bf16[8,144,128]{2,1,0:T(8,128)(2,1)S(1)} collective-permute-done((bf16[8,144,128]{2,1,0:T(8,128)(2,1)}, bf16[8,144,128]{2,1,0:T(8,128)(2,1)S(1)}, u32[]{:S(2)}, u32[]{:S(2)}) %collective-permute-start.2) | collective-permute-done | bytes 294944 | tf_op jit(solution)/shard_map/ppermute | solution.py:475
  39.2 0.0 collective-permute-start.3
  39.2 0.0 collective-permute-done.1.refs_0_
  39.2 1.6 %collective-permute-done.3.refs_3_ = bf16[8,144,128]{2,1,0:T(8,128)(2,1)S(1)} collective-permute-done((bf16[8,144,128]{2,1,0:T(8,128)(2,1)S(1)}, bf16[8,144,128]{2,1,0:T(8,128)(2,1)S(1)}, u32[]{:S(2)}, u32[]{:S(2)}) %collective-permute-start.3) | collective-permute-done | bytes 294944 | tf_op jit(solution)/shard_map/ppermute | solution.py:475
  40.8 2.6 %all-to-all-done.1 = bf16[8,256,128]{2,1,0:T(8,128)(2,1)S(1)} async-done(((bf16[8,256,128]{2,1,0:T(8,128)(2,1)}), bf16[8,256,128]{2,1,0:T(8,128)(2,1)S(1)}, u32[]{:S(2)}, u32[]{:S(2)}) %all-to-all-start.1) | async-done | bytes 524320 | tf_op jit(solution)/shard_map/all_to_all | solution.py:508
  43.4 0.0 copy-done
  43.4 0.0 copy-done.1
  43.4 4.4 %shard_map.85 = f32[32,16,128]{2,1,0:T(8,128)S(1)} custom-call(s32[3072]{0:T(1024)S(1)} %bitcast.11, bf16[2048,128]{1,0:T(8,128)(2,1)S(1)} %bitcast.9, f32[16,72,128]{2,1,0:T(8,128)S(1)} %copy-done, bf16[8,144,128]{2,1,0:T(8,128)(2,1)S(1)} %collective-permute-done.1.refs_0_, bf16[8,144,128]{2,1,0:T(8,128)(2,1)S(1)} %collective-permute-done.refs_1_, ...), custom_call_target="tpu_custom_call" | custom-call | tf_op jit(solution)/shard_map/pallas_call | solution.py:431
  47.8 13.6 %all_to_all.15 = f32[32,16,128]{2,1,0:T(8,128)S(1)} all-to-all(f32[32,16,128]{2,1,0:T(8,128)S(1)} %shard_map.85), channel_id=1, replica_groups=mesh['groups'=2,'blk'=8,'sub'=2] {'groups','blk','sub'}, dimensions={0} | all-to-all | bytes 524288 | tf_op jit(solution)/shard_map/all_to_all | solution.py:518
  61.4 0.0 copy-done.2
  61.4 1.1 %shard_map.86 = f32[4,128]{1,0:T(4,128)} custom-call(s32[4,128]{1,0:T(4,128)S(1)} %copy-done.2, f32[2,256,128]{2,1,0:T(8,128)S(1)} %bitcast.10), custom_call_target="tpu_custom_call" | custom-call | tf_op jit(solution)/shard_map/pallas_call | solution.py:466
Async XLA Ops:
  2.3 16.9 %all-to-all-start = ((bf16[8,144,128]{2,1,0:T(8,128)(2,1)}), bf16[8,144,128]{2,1,0:T(8,128)(2,1)S(1)}, u32[]{:S(2)}, u32[]{:S(2)}) async-start(bf16[8,144,128]{2,1,0:T(8,128)(2,1)} %get-tuple-element.13), calls=%async_computation | async-start | bytes 589824 | tf_op jit(solution)/shard_map/all_to_all | solution.py:498
  14.6 28.8 %copy-start = (f32[16,72,128]{2,1,0:T(8,128)S(1)}, f32[16,72,128]{2,1,0:T(8,128)}, u32[]{:S(2)}) copy-start(f32[16,72,128]{2,1,0:T(8,128)} %get-tuple-element.14.residual_hbm) | copy-start | bytes 1769476
  14.6 28.8 %copy-start.1 = (s32[24,128]{1,0:T(8,128)S(1)}, s32[24,128]{1,0:T(8,128)}, u32[]{:S(2)}) copy-start(s32[24,128]{1,0:T(8,128)} %get-tuple-element.12) | copy-start | bytes 36868
  14.6 46.8 %copy-start.2 = (s32[4,128]{1,0:T(4,128)S(1)}, s32[4,128]{1,0:T(4,128)}, u32[]{:S(2)}) copy-start(s32[4,128]{1,0:T(4,128)} %get-tuple-element.11.after_ref.slots_ref) | copy-start | bytes 6148
  19.2 0.7 %copy-start.3 = (bf16[8,144,128]{2,1,0:T(8,128)(2,1)}, bf16[8,144,128]{2,1,0:T(8,128)(2,1)S(1)}, u32[]{:S(2)}) copy-start(bf16[8,144,128]{2,1,0:T(8,128)(2,1)S(1)} %all-to-all-done.received_hbm) | copy-start | bytes 884740
  25.6 17.7 %all-to-all-start.1 = ((bf16[8,256,128]{2,1,0:T(8,128)(2,1)}), bf16[8,256,128]{2,1,0:T(8,128)(2,1)S(1)}, u32[]{:S(2)}, u32[]{:S(2)}) async-start(bf16[8,256,128]{2,1,0:T(8,128)(2,1)} %bitcast.13), calls=%async_computation.1 | async-start | bytes 1048576 | tf_op jit(solution)/shard_map/all_to_all | solution.py:508
  29.6 1.8 %collective-permute-start = (bf16[8,144,128]{2,1,0:T(8,128)(2,1)}, bf16[8,144,128]{2,1,0:T(8,128)(2,1)S(1)}, u32[]{:S(2)}, u32[]{:S(2)}) collective-permute-start(bf16[8,144,128]{2,1,0:T(8,128)(2,1)} %copy-done.3), channel_id=1, source_target_pairs={{0,1},{1,0},{2,3},{3,2},{4,5},{5,4},{6,7},{7,6},{8,9},{9,8},{10,11... | collective-permute-start | bytes 884744 | tf_op jit(solution)/shard_map/ppermute | solution.py:475
  29.6 9.6 %collective-permute-start.2 = (bf16[8,144,128]{2,1,0:T(8,128)(2,1)}, bf16[8,144,128]{2,1,0:T(8,128)(2,1)S(1)}, u32[]{:S(2)}, u32[]{:S(2)}) collective-permute-start(bf16[8,144,128]{2,1,0:T(8,128)(2,1)} %copy-done.3), channel_id=1, source_target_pairs={{0,16},{16,0},{1,17},{17,1},{2,18},{18,2},{3,19},{19,3},{4,20},{20... | collective-permute-start | bytes 884744 | tf_op jit(solution)/shard_map/ppermute | solution.py:475
  31.3 7.8 %collective-permute-start.1 = (bf16[8,144,128]{2,1,0:T(8,128)(2,1)S(1)}, bf16[8,144,128]{2,1,0:T(8,128)(2,1)S(1)}, u32[]{:S(2)}, u32[]{:S(2)}) collective-permute-start(bf16[8,144,128]{2,1,0:T(8,128)(2,1)S(1)} %collective-permute-done.refs_1_), channel_id=1, source_target_pairs={{0,1},{1,0},{2,3},{3,2},{4,5},{5,4},{6,7},{7,6},{8,9},{9,8},{10,11... | collective-permute-start | bytes 884744 | tf_op jit(solution)/shard_map/ppermute | solution.py:475
  39.2 1.6 %collective-permute-start.3 = (bf16[8,144,128]{2,1,0:T(8,128)(2,1)S(1)}, bf16[8,144,128]{2,1,0:T(8,128)(2,1)S(1)}, u32[]{:S(2)}, u32[]{:S(2)}) collective-permute-start(bf16[8,144,128]{2,1,0:T(8,128)(2,1)S(1)} %collective-permute-done.2.refs_2_), channel_id=1, source_target_pairs={{0,1},{1,0},{2,3},{3,2},{4,5},{5,4},{6,7},{7,6},{8,9},{9,8},{10,11... | collective-permute-start | bytes 884744 | tf_op jit(solution)/shard_map/ppermute | solution.py:475

commit v8 on v7

--- a/solution.py
+++ b/solution.py
@@ -282,7 +282,7 @@
     for h, table in enumerate((front, back)):
         loads[h].wait()
 
-        @pl.loop(0, shards, unroll=4)
+        @pl.loop(0, shards, unroll=8)
         def _(d):
             base = d * (per * height)
             count = asked[2 * rows * height + d]
@@ -371,7 +371,7 @@
 
     listing.wait()
 
-    @pl.loop(0, passages)
+    @pl.loop(0, passages, unroll=4)
     def _(p):
         count = list_ref[passages * height + p]
 

time: 63.2 us -> 62.9 us (level)
  no operation moved by 1% of the time
where the time goes in v8:
time: 62.9 us; the launch traced here: 62.6 us
  Pallas kernels  18.5 us (29%)
  waiting for transfers between devices  16.8 us (27%)
  blocking collectives  13.7 us (22%)
  starting transfers between devices  12.8 us (20%)
  local copies, waits for them, and re-layouts  0.75 us (1%)
    all_to_all x1, blocking collectives, body(): lax.all_to_all(best, ('groups', 'blk', 'sub'), split_axis=0, concat_axis=...  13.7 us
    ppermute x4, waiting for transfers between devices, turned(): lax.ppermute(array, axis, [(i, (i + shift) % size) for i in range(size)])  9.55 us
    all_to_all x1, starting transfers between devices, body(): near = lax.all_to_all(sent, 'blk', split_axis=0, concat_axis=0, tiled=True)  7.29 us
    pallas_call x1, Pallas kernels, fetch(): pl.pallas_call(functools.partial(fetch_kernel, span, cap), out_shape=jax....  5.81 us
    pallas_call x1, Pallas kernels, prepare(): pl.pallas_call(prepare_kernel, out_shape=(jax.ShapeDtypeStruct((passages...  4.9 us
    all_to_all x1, waiting for transfers between devices, body(): near = lax.all_to_all(sent, 'blk', split_axis=0, concat_axis=0, tiled=True)  4.68 us
    pallas_call x1, Pallas kernels, score(): pl.pallas_call(functools.partial(score_kernel, span), out_shape=jax.Shape...  4.33 us
    all_to_all x1, starting transfers between devices, body(): lax.all_to_all(found.reshape(shards, cap, width), 'blk', split_axis=0, co...  3.8 us
  transfers between devices with their start and end apart: 6, of which 5 were waited for; matrix products, arithmetic and copies ran while one was open for 0% of the time, Pallas kernels for 8%

profile of v8, /device:TPU:0, one launch (start us, length us, event | category | flops | bytes accessed | tf_op | source)
XLA Modules:
  0.0 62.6 jit_solution(1332815667163037158)
XLA Ops:
  0.0 2.3 %shard_map.82 = (bf16[8,144,128]{2,1,0:T(8,128)(2,1)}, s32[16,128]{1,0:T(8,128)}) custom-call(s32[16]{0:T(128)} %lengths_hbm.1, s32[16,128]{1,0:T(8,128)} %bitcast.16, bf16[128,128]{1,0:T(8,128)(2,1)} %bitcast.15), custom_call_target="tpu_custom_call" | custom-call | tf_op jit(solution)/shard_map/pallas_call | solution.py:124
  2.3 7.3 %all-to-all-start = ((bf16[8,144,128]{2,1,0:T(8,128)(2,1)}), bf16[8,144,128]{2,1,0:T(8,128)(2,1)S(1)}, u32[]{:S(2)}, u32[]{:S(2)}) async-start(bf16[8,144,128]{2,1,0:T(8,128)(2,1)} %get-tuple-element.13), calls=%async_computation | async-start | bytes 589824 | tf_op jit(solution)/shard_map/all_to_all | solution.py:498
  9.6 4.9 %shard_map.83 = (s32[24,128]{1,0:T(8,128)}, f32[16,72,128]{2,1,0:T(8,128)}, s32[4,128]{1,0:T(4,128)}) custom-call(s32[16,128]{1,0:T(8,128)} %get-tuple-element.10.pos_ref, s32[16,128,128]{2,1,0:T(8,128)} %bitcast.14, f32[4,128]{1,0:T(4,128)} %buckets_ref.1, s32[2,128]{1,0:T(2,128)} %bitcast.17, s32[4,128]{1,0:T(4,128)} %candidates_ref.1), custom_call_target="tpu_custom_call" | custom-call | tf_op jit(solution)/shard_map/pallas_call | solution.py:220
  14.5 0.0 copy-start
  14.5 0.0 copy-start.1
  14.5 0.0 copy-start.2
  14.5 4.7 %all-to-all-done.received_hbm = bf16[8,144,128]{2,1,0:T(8,128)(2,1)S(1)} async-done(((bf16[8,144,128]{2,1,0:T(8,128)(2,1)}), bf16[8,144,128]{2,1,0:T(8,128)(2,1)S(1)}, u32[]{:S(2)}, u32[]{:S(2)}) %all-to-all-start) | async-done | bytes 294944 | tf_op jit(solution)/shard_map/all_to_all | solution.py:498
  19.2 0.0 copy-start.3
  19.2 0.7 %copy-done.3 = bf16[8,144,128]{2,1,0:T(8,128)(2,1)} copy-done((bf16[8,144,128]{2,1,0:T(8,128)(2,1)}, bf16[8,144,128]{2,1,0:T(8,128)(2,1)S(1)}, u32[]{:S(2)}) %copy-start.3) | copy-done | bytes 294936
  20.0 5.8 %shard_map.84 = bf16[2048,128]{1,0:T(8,128)(2,1)} custom-call(bf16[8,144,128]{2,1,0:T(8,128)(2,1)} %copy-done.3, bf16[2048,16,128]{2,1,0:T(8,128)(2,1)} %bitcast.12, s32[4,128]{1,0:T(4,128)} %get-tuple-element.11.after_ref.slots_ref), custom_call_target="tpu_custom_call" | custom-call | tf_op jit(solution)/shard_map/pallas_call | solution.py:330
  25.8 3.8 %all-to-all-start.1 = ((bf16[8,256,128]{2,1,0:T(8,128)(2,1)}), bf16[8,256,128]{2,1,0:T(8,128)(2,1)S(1)}, u32[]{:S(2)}, u32[]{:S(2)}) async-start(bf16[8,256,128]{2,1,0:T(8,128)(2,1)} %bitcast.13), calls=%async_computation.1 | async-start | bytes 1048576 | tf_op jit(solution)/shard_map/all_to_all | solution.py:508
  29.6 0.0 collective-permute-start
  29.6 1.5 %collective-permute-start.2 = (bf16[8,144,128]{2,1,0:T(8,128)(2,1)}, bf16[8,144,128]{2,1,0:T(8,128)(2,1)S(1)}, u32[]{:S(2)}, u32[]{:S(2)}) collective-permute-start(bf16[8,144,128]{2,1,0:T(8,128)(2,1)} %copy-done.3), channel_id=1, source_target_pairs={{0,16},{16,0},{1,17},{17,1},{2,18},{18,2},{3,19},{19,3},{4,20},{20... | collective-permute-start | bytes 884744 | tf_op jit(solution)/shard_map/ppermute | solution.py:475
  31.1 0.3 collective-permute-done.refs_1_
  31.4 0.1 collective-permute-start.1
  31.5 7.7 %collective-permute-done.2.refs_2_ = bf16[8,144,128]{2,1,0:T(8,128)(2,1)S(1)} collective-permute-done((bf16[8,144,128]{2,1,0:T(8,128)(2,1)}, bf16[8,144,128]{2,1,0:T(8,128)(2,1)S(1)}, u32[]{:S(2)}, u32[]{:S(2)}) %collective-permute-start.2) | collective-permute-done | bytes 294944 | tf_op jit(solution)/shard_map/ppermute | solution.py:475
  39.2 0.0 collective-permute-start.3
  39.2 0.0 collective-permute-done.1.refs_0_
  39.2 1.6 %collective-permute-done.3.refs_3_ = bf16[8,144,128]{2,1,0:T(8,128)(2,1)S(1)} collective-permute-done((bf16[8,144,128]{2,1,0:T(8,128)(2,1)S(1)}, bf16[8,144,128]{2,1,0:T(8,128)(2,1)S(1)}, u32[]{:S(2)}, u32[]{:S(2)}) %collective-permute-start.3) | collective-permute-done | bytes 294944 | tf_op jit(solution)/shard_map/ppermute | solution.py:475
  40.8 2.6 %all-to-all-done.1 = bf16[8,256,128]{2,1,0:T(8,128)(2,1)S(1)} async-done(((bf16[8,256,128]{2,1,0:T(8,128)(2,1)}), bf16[8,256,128]{2,1,0:T(8,128)(2,1)S(1)}, u32[]{:S(2)}, u32[]{:S(2)}) %all-to-all-start.1) | async-done | bytes 524320 | tf_op jit(solution)/shard_map/all_to_all | solution.py:508
  43.4 0.0 copy-done
  43.4 0.0 copy-done.1
  43.4 4.3 %shard_map.85 = f32[32,16,128]{2,1,0:T(8,128)S(1)} custom-call(s32[3072]{0:T(1024)S(1)} %bitcast.11, bf16[2048,128]{1,0:T(8,128)(2,1)S(1)} %bitcast.9, f32[16,72,128]{2,1,0:T(8,128)S(1)} %copy-done, bf16[8,144,128]{2,1,0:T(8,128)(2,1)S(1)} %collective-permute-done.1.refs_0_, bf16[8,144,128]{2,1,0:T(8,128)(2,1)S(1)} %collective-permute-done.refs_1_, ...), custom_call_target="tpu_custom_call" | custom-call | tf_op jit(solution)/shard_map/pallas_call | solution.py:431
  47.7 13.7 %all_to_all.15 = f32[32,16,128]{2,1,0:T(8,128)S(1)} all-to-all(f32[32,16,128]{2,1,0:T(8,128)S(1)} %shard_map.85), channel_id=1, replica_groups=mesh['groups'=2,'blk'=8,'sub'=2] {'groups','blk','sub'}, dimensions={0} | all-to-all | bytes 524288 | tf_op jit(solution)/shard_map/all_to_all | solution.py:518
  61.4 0.0 copy-done.2
  61.4 1.1 %shard_map.86 = f32[4,128]{1,0:T(4,128)} custom-call(s32[4,128]{1,0:T(4,128)S(1)} %copy-done.2, f32[2,256,128]{2,1,0:T(8,128)S(1)} %bitcast.10), custom_call_target="tpu_custom_call" | custom-call | tf_op jit(solution)/shard_map/pallas_call | solution.py:466
Async XLA Ops:
  2.3 16.9 %all-to-all-start = ((bf16[8,144,128]{2,1,0:T(8,128)(2,1)}), bf16[8,144,128]{2,1,0:T(8,128)(2,1)S(1)}, u32[]{:S(2)}, u32[]{:S(2)}) async-start(bf16[8,144,128]{2,1,0:T(8,128)(2,1)} %get-tuple-element.13), calls=%async_computation | async-start | bytes 589824 | tf_op jit(solution)/shard_map/all_to_all | solution.py:498
  14.5 28.9 %copy-start = (f32[16,72,128]{2,1,0:T(8,128)S(1)}, f32[16,72,128]{2,1,0:T(8,128)}, u32[]{:S(2)}) copy-start(f32[16,72,128]{2,1,0:T(8,128)} %get-tuple-element.14.residual_hbm) | copy-start | bytes 1769476
  14.5 28.9 %copy-start.1 = (s32[24,128]{1,0:T(8,128)S(1)}, s32[24,128]{1,0:T(8,128)}, u32[]{:S(2)}) copy-start(s32[24,128]{1,0:T(8,128)} %get-tuple-element.12) | copy-start | bytes 36868
  14.5 46.9 %copy-start.2 = (s32[4,128]{1,0:T(4,128)S(1)}, s32[4,128]{1,0:T(4,128)}, u32[]{:S(2)}) copy-start(s32[4,128]{1,0:T(4,128)} %get-tuple-element.11.after_ref.slots_ref) | copy-start | bytes 6148
  19.2 0.7 %copy-start.3 = (bf16[8,144,128]{2,1,0:T(8,128)(2,1)}, bf16[8,144,128]{2,1,0:T(8,128)(2,1)S(1)}, u32[]{:S(2)}) copy-start(bf16[8,144,128]{2,1,0:T(8,128)(2,1)S(1)} %all-to-all-done.received_hbm) | copy-start | bytes 884740
  25.8 17.6 %all-to-all-start.1 = ((bf16[8,256,128]{2,1,0:T(8,128)(2,1)}), bf16[8,256,128]{2,1,0:T(8,128)(2,1)S(1)}, u32[]{:S(2)}, u32[]{:S(2)}) async-start(bf16[8,256,128]{2,1,0:T(8,128)(2,1)} %bitcast.13), calls=%async_computation.1 | async-start | bytes 1048576 | tf_op jit(solution)/shard_map/all_to_all | solution.py:508
  29.6 1.8 %collective-permute-start = (bf16[8,144,128]{2,1,0:T(8,128)(2,1)}, bf16[8,144,128]{2,1,0:T(8,128)(2,1)S(1)}, u32[]{:S(2)}, u32[]{:S(2)}) collective-permute-start(bf16[8,144,128]{2,1,0:T(8,128)(2,1)} %copy-done.3), channel_id=1, source_target_pairs={{0,1},{1,0},{2,3},{3,2},{4,5},{5,4},{6,7},{7,6},{8,9},{9,8},{10,11... | collective-permute-start | bytes 884744 | tf_op jit(solution)/shard_map/ppermute | solution.py:475
  29.6 9.6 %collective-permute-start.2 = (bf16[8,144,128]{2,1,0:T(8,128)(2,1)}, bf16[8,144,128]{2,1,0:T(8,128)(2,1)S(1)}, u32[]{:S(2)}, u32[]{:S(2)}) collective-permute-start(bf16[8,144,128]{2,1,0:T(8,128)(2,1)} %copy-done.3), channel_id=1, source_target_pairs={{0,16},{16,0},{1,17},{17,1},{2,18},{18,2},{3,19},{19,3},{4,20},{20... | collective-permute-start | bytes 884744 | tf_op jit(solution)/shard_map/ppermute | solution.py:475
  31.4 7.8 %collective-permute-start.1 = (bf16[8,144,128]{2,1,0:T(8,128)(2,1)S(1)}, bf16[8,144,128]{2,1,0:T(8,128)(2,1)S(1)}, u32[]{:S(2)}, u32[]{:S(2)}) collective-permute-start(bf16[8,144,128]{2,1,0:T(8,128)(2,1)S(1)} %collective-permute-done.refs_1_), channel_id=1, source_target_pairs={{0,1},{1,0},{2,3},{3,2},{4,5},{5,4},{6,7},{7,6},{8,9},{9,8},{10,11... | collective-permute-start | bytes 884744 | tf_op jit(solution)/shard_map/ppermute | solution.py:475
  39.2 1.6 %collective-permute-start.3 = (bf16[8,144,128]{2,1,0:T(8,128)(2,1)S(1)}, bf16[8,144,128]{2,1,0:T(8,128)(2,1)S(1)}, u32[]{:S(2)}, u32[]{:S(2)}) collective-permute-start(bf16[8,144,128]{2,1,0:T(8,128)(2,1)S(1)} %collective-permute-done.2.refs_2_), channel_id=1, source_target_pairs={{0,1},{1,0},{2,3},{3,2},{4,5},{5,4},{6,7},{7,6},{8,9},{9,8},{10,11... | collective-permute-start | bytes 884744 | tf_op jit(solution)/shard_map/ppermute | solution.py:475
